TPU v7x, 256 devices: a whole 4x4x8 slice. The times are simulated.
256 devices in a mesh: row: 8 (over y, x_hi), col: 32 (over x_lo, z, core).
Axes of the slice: x: 4 (x_hi: 2, x_lo: 2; x = x_hi * 2 + x_lo), y: 4, z: 8, core: 2. Of those that a mesh axis runs over, the one named last changes fastest.
Arguments:
- tokens: bfloat16 [512, 12288], P('col', 'row'), may hold values from -6 to 6
- up_weight: bfloat16 [12288, 24576], P('row', 'col'), may hold values from -0.0546875 to 0.0546875
- up_bias: bfloat16 [24576], P('col'), may hold values from -4 to 4
- down_weight: bfloat16 [24576, 12288], P('col', 'row'), may hold values from -0.0390625 to 0.0390625
- cotangent: bfloat16 [512, 12288], P('col', 'row'), may hold values from -6 to 6
Outputs:
- grad_tokens: bfloat16 [512, 12288], P('col', 'row')
- grad_up: bfloat16 [12288, 24576], P('row', 'col')
- grad_down: bfloat16 [24576, 12288], P('col', 'row')
All inputs are finite; a program needn't handle non-finite values.
Results may differ from a plain program's by a relative error of at most 0.0049.
Values may be sent and summed in bfloat16 or wider, within the bound.
No kernel may reach another device: no remote copies, remote signals or barrier semaphores. Data moves between devices by JAX's collectives and lax.ppermute only.
A program may use at most 64 MiB of HBM per device.

v0:
```python
import math

import jax
import jax.numpy as jnp
from jax import lax
from jax.sharding import PartitionSpec as P


def gelu_value(hidden):
    return hidden * 0.5 * (1.0 + lax.erf(hidden / math.sqrt(2.0)))


def gelu_slope(hidden):
    cumulative = 0.5 * (1.0 + lax.erf(hidden / math.sqrt(2.0)))
    density = jnp.exp(-0.5 * hidden * hidden) / math.sqrt(2.0 * math.pi)
    return cumulative + hidden * density


def pointwise(hidden_sum, act_grad, up_bias):
    hidden = hidden_sum + up_bias.astype(jnp.float32)[None, :]
    activated = gelu_value(hidden).astype(jnp.bfloat16)
    hidden_grad = (act_grad * gelu_slope(hidden)).astype(jnp.bfloat16)
    return (activated, hidden_grad)


def on_device(tokens, up_weight, up_bias, down_weight, cotangent):
    all_rows, all_cots = (
        lax.all_gather(tokens, "col", axis=0, tiled=True),
        lax.all_gather(cotangent, "col", axis=0, tiled=True),
    )
    hidden_part = jnp.dot(all_rows, up_weight, preferred_element_type=jnp.float32)
    act_part = lax.dot_general(
        all_cots, down_weight, (((1,), (1,)), ((), ())), preferred_element_type=jnp.float32
    )
    hidden_sum, act_grad = lax.psum((hidden_part, act_part), "row")
    activated, hidden_grad = pointwise(hidden_sum, act_grad, up_bias)
    norm_factor = 1.0 / math.sqrt(all_rows.shape[0])
    grad_up = (
        lax.dot_general(
            all_rows, hidden_grad, (((0,), (0,)), ((), ())), preferred_element_type=jnp.float32
        )
        * norm_factor
    )
    grad_down = (
        lax.dot_general(
            activated, all_cots, (((0,), (0,)), ((), ())), preferred_element_type=jnp.float32
        )
        * norm_factor
    )
    grad_tokens = lax.psum_scatter(
        lax.dot_general(
            hidden_grad, up_weight, (((1,), (1,)), ((), ())), preferred_element_type=jnp.float32
        ),
        "col",
        scatter_dimension=0,
        tiled=True,
    )
    return (
        grad_tokens.astype(jnp.bfloat16),
        grad_up.astype(jnp.bfloat16),
        grad_down.astype(jnp.bfloat16),
    )


def solution(mesh):
    placed = (P("col", "row"), P("row", "col"), P("col"), P("col", "row"), P("col", "row"))
    return jax.shard_map(
        on_device,
        mesh=mesh,
        in_specs=placed,
        out_specs=(P("col", "row"), P("row", "col"), P("col", "row")),
        check_vma=False,
    )
```

profile of v0, /device:TPU:8, one launch (start us, length us, event | category | flops | bytes accessed | tf_op | source)
XLA Modules:
  0.0 431.0 jit_solution(8830324274815115759)
XLA Ops:
  7.2 0.0 copy-start
  7.2 0.0 all-gather.3.cloned.1.call-start
  7.2 0.7 all-gather.3.cloned.1.call-update
  7.9 0.0 all-gather.5.cloned.1.call-start
  8.0 0.7 all-gather.5.cloned.1.call-update
  8.7 0.0 all-reduce.3.cloned.1.call-start
  8.7 68.4 %all-gather.3.cloned.1.call-done = bf16[512,1536]{1,0:T(8,128)(2,1)} async-done(((bf16[16,1536]{1,0:T(8,128)(2,1)}), bf16[512,1536]{1,0:T(8,128)(2,1)}) %all-gather.3.cloned.1.call-update) | async-done | bytes 1572880 | tf_op jit(solution)/shard_map/all_gather | solution.py:29
  77.1 4.7 %fusion.10 = f32[512,768]{1,0:T(8,128)} fusion(bf16[512,1536]{1,0:T(8,128)(2,1)} %all-gather.3.cloned.1.call-done, bf16[768,1536]{1,0:T(8,128)(2,1)} %param.8), kind=kOutput, calls=%fused_computation.15 | convolution fusion | flops 1207959552 | bytes 5505024 | tf_op jit(solution)/shard_map/dot_general | solution.py:32
  81.8 61.1 %all-gather.5.cloned.1.call-done = bf16[512,1536]{1,0:T(8,128)(2,1)} async-done(((bf16[16,1536]{1,0:T(8,128)(2,1)}), bf16[512,1536]{1,0:T(8,128)(2,1)}) %all-gather.5.cloned.1.call-update) | async-done | bytes 1572880 | tf_op jit(solution)/shard_map/all_gather | solution.py:28
  142.9 0.0 copy-done
  142.9 3.9 fusion.11
  146.9 0.0 copy-start.1
  146.9 0.0 all-reduce.3.cloned.1.call-update
  146.9 0.0 reduce-scatter.2.cloned.1.call-start
  147.0 0.6 copy-done.1
  147.6 149.4 %all-reduce.3.cloned.1.call-done = (f32[512,768]{1,0:T(8,128)}, f32[512,768]{1,0:T(8,128)}) async-done(((f32[512,768]{1,0:T(8,128)}, f32[512,768]{1,0:T(8,128)}), (f32[512,768]{1,0:T(8,128)}, f32[512,768]{1,0:T(8,128)})) %all-reduce.3.cloned.1.call-update) | async-done | bytes 3145744 | tf_op jit(solution)/shard_map/psum | solution.py:35
  297.0 2.6 fusion.6
  299.6 3.1 fusion.12
  302.6 0.0 reduce-scatter.2.cloned.1.call-update
  302.6 4.2 fusion
  306.9 4.3 copy.8
  311.1 4.7 %multiply_convert_fusion = bf16[768,1536]{1,0:T(8,128)(2,1)} fusion(bf16[512,1536]{1,0:T(8,128)(2,1)} %all-gather.3.cloned.1.call-done, f32[512,768]{1,0:T(8,128)} %get-tuple-element.7, f32[768]{0:T(1024)S(1)} %convert_element_type.21), kind=kOutput, calls=%fused_computation | convolution fusion | flops 1212678144 | bytes 5508096 | tf_op jit(solution)/shard_map/dot_general | solution.py:45
  315.9 107.0 %reduce-scatter.2.cloned.1.call-done = f32[16,1536]{1,0:T(8,128)} async-done(((f32[512,1536]{1,0:T(8,128)}), f32[16,1536]{1,0:T(8,128)}) %reduce-scatter.2.cloned.1.call-update) | async-done | bytes 98320 | tf_op jit(solution)/shard_map/reduce_scatter | solution.py:50
  422.9 1.5 convert_element_type.23
  (1 shorter events, 0.0 us)
Async XLA Ops:
  7.2 135.8 %copy-start = (bf16[1536,768]{1,0:T(8,128)(2,1)S(1)}, bf16[1536,768]{1,0:T(8,128)(2,1)}, u32[]{:S(2)}) copy-start(bf16[1536,768]{1,0:T(8,128)(2,1)} %param.6) | copy-start | bytes 7077892
  7.2 69.9 %all-gather.3.cloned.1.call-start = ((), (), s32[]{:S(2)}) async-start(), calls=%async_computation.1 | async-start | bytes 1622016 | tf_op jit(solution)/shard_map/all_gather | solution.py:29
  7.9 135.0 %all-gather.5.cloned.1.call-start = ((), (), s32[]{:S(2)}) async-start(), calls=%async_computation.2 | async-start | bytes 1622016 | tf_op jit(solution)/shard_map/all_gather | solution.py:28
  8.7 288.3 %all-reduce.3.cloned.1.call-start = ((), (), s32[]{:S(2)}) async-start(), calls=%async_computation.4 | async-start | bytes 6291456 | tf_op jit(solution)/shard_map/psum | solution.py:35
  146.9 0.7 copy-start.1
  146.9 276.0 %reduce-scatter.2.cloned.1.call-start = ((), (), s32[]{:S(2)}) async-start(), calls=%async_computation.3 | async-start | bytes 3244032 | tf_op jit(solution)/shard_map/reduce_scatter | solution.py:50
Sparse Core Ops, SparseCore 0:
  9.9 67.1 all-gather.2
  79.0 63.9 all-gather.4
  147.0 149.9 all-reduce.2
  302.8 120.1 reduce-scatter.1
where the time goes:
time: 431 us
  waiting for transfers between devices  387 us (90%)
  matrix products  20.7 us (5%)
  between operations  13.8 us (3%)
  local copies, waits for them, and re-layouts  4.88 us (1%)
    psum x1, waiting for transfers between devices, on_device(): hidden_sum, act_grad = lax.psum((hidden_part, act_part), 'row')  149 us
    reduce_scatter x1, waiting for transfers between devices, on_device(): lax.psum_scatter(lax.dot_general(hidden_grad, up_weight, (((1,), (1,)), (...  107 us
    all_gather x1, waiting for transfers between devices, on_device(): lax.all_gather(cotangent, 'col', axis=0, tiled=True)  68.4 us
    all_gather x1, waiting for transfers between devices, on_device(): lax.all_gather(tokens, 'col', axis=0, tiled=True)  61.1 us
  transfers between devices with their start and end apart: 4, of which 4 were waited for; matrix products, arithmetic and copies ran while one was open for 4% of the time, Pallas kernels for 0%

commit v1 on v0

v1 whole, which is shorter than its diff:
```python
import math

import jax
import jax.numpy as jnp
from jax import lax
from jax.sharding import Mesh, PartitionSpec as P

ROW = ("y", "x_hi")
COL = ("x_lo", "z", "core")
BF16 = jnp.bfloat16
F32 = jnp.float32


def gelu_value(hidden):
    return hidden * 0.5 * (1.0 + lax.erf(hidden / math.sqrt(2.0)))


def gelu_slope(hidden):
    cumulative = 0.5 * (1.0 + lax.erf(hidden / math.sqrt(2.0)))
    density = jnp.exp(-0.5 * hidden * hidden) / math.sqrt(2.0 * math.pi)
    return cumulative + hidden * density


def pointwise(hidden_sum, act_grad, up_bias):
    hidden = hidden_sum + up_bias.astype(F32)[None, :]
    activated = gelu_value(hidden).astype(BF16)
    hidden_grad = (act_grad * gelu_slope(hidden)).astype(BF16)
    return (activated, hidden_grad)


def on_device(tokens, up_weight, up_bias, down_weight, cotangent):
    width, units = up_weight.shape
    packed = jnp.concatenate([tokens, cotangent], axis=1)
    gathered = lax.all_gather(packed, COL, axis=0, tiled=True)
    all_rows, all_cots = gathered[:, :width], gathered[:, width:]
    count = all_rows.shape[0]
    hidden_part = jnp.dot(all_rows, up_weight, preferred_element_type=F32).astype(BF16)
    act_part = lax.dot_general(
        all_cots, down_weight, (((1,), (1,)), ((), ())), preferred_element_type=F32
    ).astype(BF16)
    parts = jnp.concatenate([hidden_part, act_part], axis=1)
    parts = lax.all_to_all(parts, ROW, 0, 0, tiled=True)
    sums = parts.reshape(8, count // 8, 2 * units).astype(F32).sum(axis=0)
    activated, hidden_grad = pointwise(sums[:, :units], sums[:, units:], up_bias)
    both = jnp.concatenate([activated, hidden_grad], axis=1)
    both = lax.all_to_all(jnp.tile(both, (8, 1)), ROW, 0, 0, tiled=True)
    activated, hidden_grad = both[:, :units], both[:, units:]
    norm_factor = 1.0 / math.sqrt(count)
    token_part = lax.dot_general(
        hidden_grad, up_weight, (((1,), (1,)), ((), ())), preferred_element_type=F32
    ).astype(BF16)
    token_part = lax.all_to_all(token_part, COL, 0, 0, tiled=True)
    grad_tokens = token_part.reshape(32, count // 32, width).astype(F32).sum(axis=0)
    grad_up = (
        lax.dot_general(
            all_rows, hidden_grad, (((0,), (0,)), ((), ())), preferred_element_type=F32
        )
        * norm_factor
    )
    grad_down = (
        lax.dot_general(
            activated, all_cots, (((0,), (0,)), ((), ())), preferred_element_type=F32
        )
        * norm_factor
    )
    return (grad_tokens.astype(BF16), grad_up.astype(BF16), grad_down.astype(BF16))


def solution(mesh):
    fine = Mesh(mesh.devices.reshape(4, 2, 2, 8, 2), ROW + COL)
    placed = (P(COL, ROW), P(ROW, COL), P(COL), P(COL, ROW), P(COL, ROW))
    return jax.shard_map(
        on_device,
        mesh=fine,
        in_specs=placed,
        out_specs=(P(COL, ROW), P(ROW, COL), P(COL, ROW)),
        check_vma=False,
    )
```

time: 431 us -> 202 us (0.47)
  waiting for transfers between devices: 387 us -> 123 us
  blocking collectives: 0 us -> 26 us
  starting transfers between devices: 0.16 us -> 13.3 us
  matrix products: 20.7 us -> 15.1 us
  local copies, waits for them, and re-layouts: 4.88 us -> 0.15 us
    psum x1 -> x0, waiting for transfers between devices: 149 us -> none  [on_device(): hidden_sum, act_grad = lax.psum((hidden_part, act_part), 'row')]
    reduce_scatter x1 -> x0, waiting for transfers between devices: 107 us -> none  [on_device(): lax.psum_scatter(lax.dot_general(hidden_grad, up_weight, (((1,), (1,)), (...]
    all_gather x2 -> x1, waiting for transfers between devices: 130 us -> 70.6 us  [on_device(): gathered = lax.all_gather(packed, COL, axis=0, tiled=True)]
    all_to_all x0 -> x2, waiting for transfers between devices: none -> 52.9 us  [the longest x1 31.7 us: on_device(): token_part = lax.all_to_all(token_part, COL, 0, 0, tiled=True)]
    all_to_all x0 -> x1, blocking collectives: none -> 26 us  [on_device(): both = lax.all_to_all(jnp.tile(both, (8, 1)), ROW, 0, 0, tiled=True)]
    all_to_all x0 -> x2, starting transfers between devices: none -> 13.3 us  [the longest x1 7.07 us: on_device(): parts = lax.all_to_all(parts, ROW, 0, 0, tiled=True)]
    unnamed x5 -> x12, local copies, waits for them, and re-layouts: 4.88 us -> 0.03 us
  transfers between devices with their start and end apart: 4 -> 3, of which waited for: 4 -> 3; matrix products, arithmetic and copies ran while one was open for 4% -> 4% of each run, Pallas kernels for 0% -> 0%
where the time goes in v1:
time: 202 us; the launch traced here: 199 us
  waiting for transfers between devices  123 us (61%)
  blocking collectives  26 us (13%)
  matrix products  15.1 us (7%)
  between operations  14.1 us (7%)
  starting transfers between devices  13.3 us (7%)
  other arithmetic  6.94 us (3%)
    all_gather x1, waiting for transfers between devices, on_device(): gathered = lax.all_gather(packed, COL, axis=0, tiled=True)  70.6 us
    all_to_all x1, waiting for transfers between devices, on_device(): token_part = lax.all_to_all(token_part, COL, 0, 0, tiled=True)  31.7 us
    all_to_all x1, blocking collectives, on_device(): both = lax.all_to_all(jnp.tile(both, (8, 1)), ROW, 0, 0, tiled=True)  26 us
    all_to_all x1, waiting for transfers between devices, on_device(): parts = lax.all_to_all(parts, ROW, 0, 0, tiled=True)  21.1 us
    all_to_all x1, starting transfers between devices, on_device(): parts = lax.all_to_all(parts, ROW, 0, 0, tiled=True)  7.07 us
    all_to_all x1, starting transfers between devices, on_device(): token_part = lax.all_to_all(token_part, COL, 0, 0, tiled=True)  6.19 us
    dot_general x1, matrix products, on_device(): lax.dot_general(activated, all_cots, (((0,), (0,)), ((), ())), preferred_...  4.62 us
  transfers between devices with their start and end apart: 3, of which 3 were waited for; matrix products, arithmetic and copies ran while one was open for 4% of the time, Pallas kernels for 0%

profile of v1, /device:TPU:8, one launch (start us, length us, event | category | flops | bytes accessed | tf_op | source)
XLA Modules:
  0.0 199.1 jit_solution(5463455599354585840)
XLA Ops:
  7.2 0.0 copy-start
  7.2 0.0 all-gather.2.cloned.1.call-start
  7.2 1.6 pad_maximum_fusion.2
  8.8 0.0 all-gather.2.cloned.1.call-update
  8.9 70.6 %all-gather.2.cloned.1.call-done = bf16[512,3072]{1,0:T(8,128)(2,1)} async-done(((bf16[16,3072]{1,0:T(8,128)(2,1)}), bf16[512,3072]{1,0:T(8,128)(2,1)}) %all-gather.2.cloned.1.call-update) | async-done | bytes 3145744 | tf_op jit(solution)/shard_map/all_gather | solution.py:34
  79.5 0.0 copy-start.4
  79.5 3.7 %convolution_convert_fusion.1 = bf16[512,768]{1,0:T(8,128)(2,1)S(1)} fusion(bf16[768,1536]{1,0:T(8,128)(2,1)} %param.8, bf16[512,3072]{1,0:T(8,128)(2,1)} %all-gather.2.cloned.1.call-done), kind=kOutput, calls=%fused_computation.5 | convolution fusion | flops 1208352768 | bytes 4718592 | tf_op jit(solution)/shard_map/dot_general | solution.py:38
  83.2 0.0 copy-done
  83.2 0.0 copy-done.4
  83.2 1.4 convolution_convert_fusion.2
  84.6 1.3 pad_maximum_fusion
  85.9 0.0 copy-start.3
  85.9 7.1 %all-to-all-start = ((bf16[8,64,1536]{2,1,0:T(8,128)(2,1)}), bf16[8,64,1536]{2,1,0:T(8,128)(2,1)}, u32[]{:S(2)}, u32[]{:S(2)}) async-start(bf16[8,64,1536]{2,1,0:T(8,128)(2,1)} %bitcast.6), calls=%async_computation | async-start | bytes 3145728 | tf_op jit(solution)/shard_map/all_to_all | solution.py:42
  93.0 0.0 copy-done.3
  93.0 21.1 %all-to-all-done = bf16[8,64,1536]{2,1,0:T(8,128)(2,1)} async-done(((bf16[8,64,1536]{2,1,0:T(8,128)(2,1)}), bf16[8,64,1536]{2,1,0:T(8,128)(2,1)}, u32[]{:S(2)}, u32[]{:S(2)}) %all-to-all-start) | async-done | bytes 1572896 | tf_op jit(solution)/shard_map/all_to_all | solution.py:42
  114.1 1.7 convert_reduce_fusion
  115.8 0.1 multiply_convert_fusion.2
  115.9 0.1 tile.2
  116.0 26.0 %all_to_all.27 = bf16[8,64,1536]{2,1,0:T(8,128)(2,1)S(1)} all-to-all(bf16[8,64,1536]{2,1,0:T(8,128)(2,1)S(1)} %tile.2), channel_id=1, replica_groups=mesh['y'=4,'x_hi'=2,'x_lo'=2,'z'=8,'core'=2] {'y','x_hi'}, dimensions={0} | all-to-all | bytes 3145728 | tf_op jit(solution)/shard_map/all_to_all | solution.py:46
  142.0 0.0 copy-start.1
  142.0 2.6 %convolution_convert_fusion = bf16[512,1536]{1,0:T(8,128)(2,1)} fusion(bf16[1536,768]{1,0:T(8,128)(2,1)S(1)} %copy-done, bf16[512,1536]{1,0:T(8,128)(2,1)S(1)} %bitcast.7), kind=kOutput, calls=%fused_computation.3 | convolution fusion | flops 1208745984 | bytes 4718592 | tf_op jit(solution)/shard_map/dot_general | solution.py:49
  144.6 0.0 copy-done.1
  144.6 6.2 %all-to-all-start.2 = ((bf16[32,16,1536]{2,1,0:T(8,128)(2,1)}), bf16[32,16,1536]{2,1,0:T(8,128)(2,1)}, u32[]{:S(2)}, u32[]{:S(2)}) async-start(bf16[32,16,1536]{2,1,0:T(8,128)(2,1)} %bitcast.10), calls=%async_computation.2 | async-start | bytes 3145728 | tf_op jit(solution)/shard_map/all_to_all | solution.py:52
  150.8 0.0 copy-start.2
  150.8 0.0 copy-start.5
  150.8 4.6 %multiply_convert_fusion = bf16[768,1536]{1,0:T(8,128)(2,1)} fusion(bf16[512,3072]{1,0:T(8,128)(2,1)} %all-gather.2.cloned.1.call-done, bf16[512,1536]{1,0:T(8,128)(2,1)} %bitcast.8), kind=kOutput, calls=%fused_computation | convolution fusion | flops 1210318848 | bytes 4718592 | tf_op jit(solution)/shard_map/dot_general | solution.py:61
  155.4 0.0 copy-done.2
  155.4 0.0 copy-done.5
  155.4 2.8 %multiply_convert_fusion.1 = bf16[1536,768]{1,0:T(8,128)(2,1)} fusion(bf16[512,3072]{1,0:T(8,128)(2,1)S(1)} %copy-done.5, bf16[512,1536]{1,0:T(8,128)(2,1)S(1)} %bitcast.9), kind=kOutput, calls=%fused_computation.1 | convolution fusion | flops 1210318848 | bytes 4718592 | tf_op jit(solution)/shard_map/dot_general | solution.py:55
  158.3 31.7 %all-to-all-done.2 = bf16[32,16,1536]{2,1,0:T(8,128)(2,1)} async-done(((bf16[32,16,1536]{2,1,0:T(8,128)(2,1)}), bf16[32,16,1536]{2,1,0:T(8,128)(2,1)}, u32[]{:S(2)}, u32[]{:S(2)}) %all-to-all-start.2) | async-done | bytes 1572896 | tf_op jit(solution)/shard_map/all_to_all | solution.py:52
  190.0 2.3 %reduce_sum.22 = bf16[16,1536]{1,0:T(8,128)(2,1)} reduce(bf16[32,16,1536]{2,1,0:T(8,128)(2,1)} %all-to-all-done.2, bf16[]{:T(256)} %constant.17.clone.1), dimensions={0}, to_apply=%region_1.0 | reduce | flops 761856 | bytes 1622018 | tf_op jit(solution)/shard_map/reduce_sum | solution.py:53
  (2 shorter events, 0.0 us)
Async XLA Ops:
  7.2 76.0 %copy-start = (bf16[1536,768]{1,0:T(8,128)(2,1)S(1)}, bf16[1536,768]{1,0:T(8,128)(2,1)}, u32[]{:S(2)}) copy-start(bf16[1536,768]{1,0:T(8,128)(2,1)} %param.6) | copy-start | bytes 7077892
  7.2 72.3 %all-gather.2.cloned.1.call-start = ((), (), s32[]{:S(2)}) async-start(), calls=%async_computation.3 | async-start | bytes 3244032 | tf_op jit(solution)/shard_map/all_gather | solution.py:34
  79.5 3.7 %copy-start.4 = (bf16[512,3072]{1,0:T(8,128)(2,1)S(1)}, bf16[512,3072]{1,0:T(8,128)(2,1)}, u32[]{:S(2)}) copy-start(bf16[512,3072]{1,0:T(8,128)(2,1)} %all-gather.2.cloned.1.call-done) | copy-start | bytes 9437188
  85.9 7.1 %copy-start.3 = (bf16[768]{0:T(1024)(128)(2,1)S(1)}, bf16[768]{0:T(1024)(128)(2,1)}, u32[]{:S(2)}) copy-start(bf16[768]{0:T(1024)(128)(2,1)} %param.7) | copy-start | bytes 4612
  85.9 28.2 %all-to-all-start = ((bf16[8,64,1536]{2,1,0:T(8,128)(2,1)}), bf16[8,64,1536]{2,1,0:T(8,128)(2,1)}, u32[]{:S(2)}, u32[]{:S(2)}) async-start(bf16[8,64,1536]{2,1,0:T(8,128)(2,1)} %bitcast.6), calls=%async_computation | async-start | bytes 3145728 | tf_op jit(solution)/shard_map/all_to_all | solution.py:42
  142.0 2.6 %copy-start.1 = (bf16[8,64,1536]{2,1,0:T(8,128)(2,1)}, bf16[8,64,1536]{2,1,0:T(8,128)(2,1)S(1)}, u32[]{:S(2)}) copy-start(bf16[8,64,1536]{2,1,0:T(8,128)(2,1)S(1)} %all_to_all.27) | copy-start | bytes 4718596
  144.6 45.4 %all-to-all-start.2 = ((bf16[32,16,1536]{2,1,0:T(8,128)(2,1)}), bf16[32,16,1536]{2,1,0:T(8,128)(2,1)}, u32[]{:S(2)}, u32[]{:S(2)}) async-start(bf16[32,16,1536]{2,1,0:T(8,128)(2,1)} %bitcast.10), calls=%async_computation.2 | async-start | bytes 3145728 | tf_op jit(solution)/shard_map/all_to_all | solution.py:52
  150.8 4.6 %copy-start.2 = (bf16[8,64,1536]{2,1,0:T(8,128)(2,1)S(1)}, bf16[8,64,1536]{2,1,0:T(8,128)(2,1)}, u32[]{:S(2)}) copy-start(bf16[8,64,1536]{2,1,0:T(8,128)(2,1)} %copy-done.1) | copy-start | bytes 4718596
  150.8 4.6 %copy-start.5 = (bf16[512,3072]{1,0:T(8,128)(2,1)S(1)}, bf16[512,3072]{1,0:T(8,128)(2,1)}, u32[]{:S(2)}) copy-start(bf16[512,3072]{1,0:T(8,128)(2,1)} %all-gather.2.cloned.1.call-done) | copy-start | bytes 9437188
Sparse Core Ops, SparseCore 0:
  10.4 69.0 all-gather.1

commit v2 on v1

v2 whole, which is shorter than its diff:
```python
import functools
import math

import jax
import jax.numpy as jnp
from jax import lax
from jax.experimental import pallas as pl
from jax.experimental.pallas import tpu as pltpu
from jax.sharding import Mesh, PartitionSpec as P

ROW = ("y", "x_hi")
COL = ("x_lo", "z", "core")
BF16 = jnp.bfloat16
F32 = jnp.float32
ZN = 8
RN = 8
EARLY = (0, -1, 1, -2, 2)
LATE = (-3, 3, 4)
BLOCKS = tuple((side, k) for group in (EARLY, LATE) for side in (0, 1) for k in group)
WHOLE = pl.BlockSpec(memory_space=pltpu.VMEM)


def light():
    return pl.CostEstimate(flops=1, bytes_accessed=1, transcendentals=0)


def params(steps):
    return pltpu.CompilerParams(
        dimension_semantics=("arbitrary",) * steps, vmem_limit_bytes=24 * 2**20
    )


def gelu_value(hidden):
    return hidden * 0.5 * (1.0 + lax.erf(hidden / math.sqrt(2.0)))


def gelu_slope(hidden):
    cumulative = 0.5 * (1.0 + lax.erf(hidden / math.sqrt(2.0)))
    density = jnp.exp(-0.5 * hidden * hidden) / math.sqrt(2.0 * math.pi)
    return cumulative + hidden * density


def shift_z(x, k):
    return lax.ppermute(x, "z", [(i, (i + k) % ZN) for i in range(ZN)])


def swap(x, axis):
    return lax.ppermute(x, axis, [(0, 1), (1, 0)])


def dot(a, b):
    return jnp.dot(a, b, preferred_element_type=F32)


def dot_t(a, b):
    return lax.dot_general(a, b, (((1,), (1,)), ((), ())), preferred_element_type=F32)


def dot_rows(a, b):
    return lax.dot_general(a, b, (((0,), (0,)), ((), ())), preferred_element_type=F32)


def project_kernel(pieces, width, units, tile, *refs):
    given, (up, down, out, rows) = refs[:pieces], refs[pieces:]

    @pl.when(pl.program_id(0) == 0)
    def _():
        base = 0
        for piece in given:
            rows[base : base + piece.shape[0], :] = piece[...]
            base += piece.shape[0]

    at = pl.multiple_of(pl.program_id(0) * tile, tile)
    later = pl.multiple_of(units + pl.program_id(0) * tile, tile)
    out[:, pl.ds(at, tile)] = dot(rows[:, :width], up[...]).astype(BF16)
    out[:, pl.ds(later, tile)] = dot_t(rows[:, width:], down[...]).astype(BF16)


def project(pieces, up, down):
    width, units = up.shape
    tile = units // 3
    count = sum(piece.shape[0] for piece in pieces)
    return pl.pallas_call(
        functools.partial(project_kernel, len(pieces), width, units, tile),
        grid=(3,),
        out_shape=jax.ShapeDtypeStruct((count, 2 * units), BF16),
        in_specs=[pl.BlockSpec(piece.shape, lambda j: (0, 0)) for piece in pieces]
        + [
            pl.BlockSpec((width, tile), lambda j: (0, j)),
            pl.BlockSpec((tile, width), lambda j: (j, 0)),
        ],
        out_specs=pl.BlockSpec((count, 2 * units), lambda j: (0, 0)),
        scratch_shapes=[pltpu.VMEM((count, 2 * width), BF16)],
        compiler_params=params(1),
        cost_estimate=light(),
        name="project",
    )(*pieces, up, down)


def pointwise_kernel(units, parts, bias, out):
    count = parts.shape[0] // RN
    sums = parts[:count, :].astype(F32)
    for r in range(1, RN):
        sums += parts[r * count : (r + 1) * count, :].astype(F32)
    hidden = sums[:, :units] + bias[...].astype(F32)
    activated = gelu_value(hidden).astype(BF16)
    hidden_grad = (sums[:, units:] * gelu_slope(hidden)).astype(BF16)
    for r in range(RN):
        out[r * count : (r + 1) * count, :units] = activated
        out[r * count : (r + 1) * count, units:] = hidden_grad


def pointwise(parts, bias):
    units = bias.shape[0]
    return pl.pallas_call(
        functools.partial(pointwise_kernel, units),
        out_shape=jax.ShapeDtypeStruct(parts.shape, BF16),
        in_specs=[WHOLE] * 2,
        out_specs=WHOLE,
        compiler_params=params(0),
        cost_estimate=light(),
        name="pointwise",
    )(parts, bias.reshape(1, units))


def place(where, grads, rows, share, core):
    z, x = where[0], where[1]
    for i, (side, k) in enumerate(BLOCKS):
        owner = lax.rem(z + k + ZN, ZN) + ZN * (1 - x if side else x)
        at = pl.multiple_of(owner * share, share)
        base = (core * len(BLOCKS) + i) * share
        rows[pl.ds(at, share), :] = grads[base : base + share, :]


def others_kernel(share, where, grads, up, out, rows):
    @pl.when(pl.program_id(0) == 0)
    def _():
        place(where, grads, rows, share, 1)

    out[...] = dot_t(rows[...], up[...]).astype(BF16)


def mine_kernel(share, where, grads, up, given, out, rows):
    @pl.when(pl.program_id(0) == 0)
    def _():
        place(where, grads, rows, share, 0)

    out[...] = (dot_t(rows[...], up[...]) + given[...].astype(F32)).astype(BF16)


def back(where, both, up, given, share):
    width, units = up.shape
    count = both.shape[0] // 2
    tile = width // 3
    block = pl.BlockSpec((count, tile), lambda j: (0, j))
    more = [] if given is None else [given]
    return pl.pallas_call(
        functools.partial(others_kernel if given is None else mine_kernel, share),
        grid=(3,),
        out_shape=jax.ShapeDtypeStruct((count, width), BF16),
        in_specs=[
            pl.BlockSpec(memory_space=pltpu.SMEM),
            pl.BlockSpec((2 * count, units), lambda j: (0, 1)),
            pl.BlockSpec((tile, units), lambda j: (j, 0)),
        ]
        + [block] * len(more),
        out_specs=block,
        scratch_shapes=[pltpu.VMEM((count, units), BF16)],
        compiler_params=params(1),
        cost_estimate=light(),
        name="back",
    )(where, both, up, *more)


def collect_kernel(parts, out):
    count = out.shape[0]
    sums = parts[:count, :].astype(F32)
    for r in range(1, parts.shape[0] // count):
        sums += parts[r * count : (r + 1) * count, :].astype(F32)
    out[...] = sums.astype(BF16)


def collect(parts, share):
    return pl.pallas_call(
        collect_kernel,
        out_shape=jax.ShapeDtypeStruct((share, parts.shape[1]), BF16),
        in_specs=[WHOLE],
        out_specs=WHOLE,
        compiler_params=params(0),
        cost_estimate=light(),
        name="collect",
    )(parts)


def on_device(tokens, up_weight, up_bias, down_weight, cotangent):
    width, units = up_weight.shape
    share = tokens.shape[0]
    where = jnp.stack([lax.axis_index("z"), lax.axis_index("x_lo")]).astype(jnp.int32)

    held = {0: jnp.concatenate([tokens, cotangent], axis=1)}
    across = {0: swap(held[0], "x_lo")}
    for k in range(1, ZN // 2):
        held[-k] = shift_z(held[1 - k], 1)
        held[k] = shift_z(held[k - 1], -1)
        pair = swap(jnp.concatenate([held[-k], held[k]], axis=0), "x_lo")
        across[-k], across[k] = pair[:share], pair[share:]
    held[ZN // 2] = shift_z(held[ZN // 2 - 1], -1)
    across[ZN // 2] = swap(held[ZN // 2], "x_lo")

    mine = [
        jnp.concatenate([held[k] for k in group] + [across[k] for k in group], axis=0)
        for group in (EARLY, LATE)
    ]
    pieces = mine + [swap(piece, "core") for piece in mine]

    parts = project(pieces, up_weight, down_weight)
    parts = lax.all_to_all(parts, ROW, 0, 0, tiled=True)
    both = pointwise(parts, up_bias)
    both = lax.all_to_all(both, ROW, 0, 0, tiled=True)

    other = swap(back(where, both, up_weight, None, share), "core")
    near = back(where, both, up_weight, other, share)
    near = lax.all_to_all(near, ("x_lo", "z"), 0, 0, tiled=True)
    grad_tokens = collect(near, share)

    all_rows = jnp.concatenate(pieces, axis=0)
    norm_factor = 1.0 / math.sqrt(all_rows.shape[0])
    grad_up = dot_rows(all_rows[:, :width], both[:, units:]) * norm_factor
    grad_down = dot_rows(both[:, :units], all_rows[:, width:]) * norm_factor
    return (grad_tokens, grad_up.astype(BF16), grad_down.astype(BF16))


def solution(mesh):
    fine = Mesh(mesh.devices.reshape(4, 2, 2, 8, 2), ROW + COL)
    placed = (P(COL, ROW), P(ROW, COL), P(COL), P(COL, ROW), P(COL, ROW))
    return jax.shard_map(
        on_device,
        mesh=fine,
        in_specs=placed,
        out_specs=(P(COL, ROW), P(ROW, COL), P(COL, ROW)),
        check_vma=False,
    )
```

time: 202 us -> 142 us (0.70)
  waiting for transfers between devices: 123 us -> 64.7 us
  blocking collectives: 26 us -> 0 us
  starting transfers between devices: 13.3 us -> 38.7 us
  local copies, waits for them, and re-layouts: 0.15 us -> 16.1 us
  between operations: 14.1 us -> 0.78 us
  Pallas kernels: 0 us -> 10.9 us
  other arithmetic: 6.94 us -> 0.12 us
  matrix products: 15.1 us -> 8.91 us
    all_gather x1 -> x0, waiting for transfers between devices: 70.6 us -> none  [on_device(): gathered = lax.all_gather(packed, COL, axis=0, tiled=True)]
    all_to_all x1 -> x0, blocking collectives: 26 us -> none  [on_device(): both = lax.all_to_all(jnp.tile(both, (8, 1)), ROW, 0, 0, tiled=True)]
    ppermute x0 -> x15, starting transfers between devices: none -> 19.7 us  [the longest x7 13 us: shift_z(): return lax.ppermute(x, 'z', [(i, (i + k) % ZN) for i in range(ZN)])]
    unnamed x12 -> x31, local copies, waits for them, and re-layouts: 0.03 us -> 15.2 us
    ppermute x0 -> x15, waiting for transfers between devices: none -> 13.4 us  [the longest x7 7.04 us: shift_z(): return lax.ppermute(x, 'z', [(i, (i + k) % ZN) for i in range(ZN)])]
    pallas_call x0 -> x5, Pallas kernels: none -> 10.9 us  [the longest x2 5.1 us: back(): pl.pallas_call(functools.partial(others_kernel if given is None else mine...]
    dot_general x5 -> x2, matrix products: 15.1 us -> 8.91 us  [dot_rows(): lax.dot_general(a, b, (((0,), (0,)), ((), ())), preferred_element_type=F32)]
    all_to_all x1 -> x2, starting transfers between devices: 6.19 us -> 11.8 us  [the longest x1 6.66 us: on_device(): both = lax.all_to_all(both, ROW, 0, 0, tiled=True)]
  transfers between devices with their start and end apart: 3 -> 18, of which waited for: 3 -> 11; matrix products, arithmetic and copies ran while one was open for 4% -> 13% of each run, Pallas kernels for 0% -> 0%
where the time goes in v2:
time: 142 us; the launch traced here: 140 us
  waiting for transfers between devices  64.7 us (46%)
  starting transfers between devices  38.7 us (27%)
  local copies, waits for them, and re-layouts  16.1 us (11%)
  Pallas kernels  10.9 us (8%)
  matrix products  8.91 us (6%)
    all_to_all x1, waiting for transfers between devices, on_device(): parts = lax.all_to_all(parts, ROW, 0, 0, tiled=True)  20.8 us
    all_to_all x1, waiting for transfers between devices, on_device(): both = lax.all_to_all(both, ROW, 0, 0, tiled=True)  19.5 us
    unnamed x31, local copies, waits for them, and re-layouts  15.2 us
    ppermute x7, starting transfers between devices, shift_z(): return lax.ppermute(x, 'z', [(i, (i + k) % ZN) for i in range(ZN)])  13 us
    all_to_all x1, waiting for transfers between devices, on_device(): near = lax.all_to_all(near, ('x_lo', 'z'), 0, 0, tiled=True)  10.9 us
    dot_general x2, matrix products, dot_rows(): lax.dot_general(a, b, (((0,), (0,)), ((), ())), preferred_element_type=F32)  8.91 us
    all_to_all x1, starting transfers between devices, on_device(): parts = lax.all_to_all(parts, ROW, 0, 0, tiled=True)  7.19 us
    ppermute x7, waiting for transfers between devices, shift_z(): return lax.ppermute(x, 'z', [(i, (i + k) % ZN) for i in range(ZN)])  7.04 us
  transfers between devices with their start and end apart: 18, of which 11 were waited for; matrix products, arithmetic and copies ran while one was open for 13% of the time, Pallas kernels for 0%

profile of v2, /device:TPU:8, one launch (start us, length us, event | category | flops | bytes accessed | tf_op | source)
XLA Modules:
  0.0 140.2 jit_solution(10049296813040801602)
XLA Ops:
  0.7 1.6 %constant_dynamic-update-slice_fusion.31 = (bf16[512,3072]{1,0:T(8,128)(2,1)}, bf16[160,3072]{1,0:T(8,128)(2,1)S(1)}, bf16[16,3072]{1,0:T(8,128)(2,1)S(1)}) fusion(bf16[16,1536]{1,0:T(8,128)(2,1)} %param.5), kind=kLoop, calls=%fused_computation.40 | loop fusion | bytes 196608
  2.2 1.4 %constant_dynamic-update-slice_fusion.30 = (bf16[512,3072]{1,0:T(8,128)(2,1)}, bf16[160,3072]{1,0:T(8,128)(2,1)S(1)}, bf16[16,3072]{1,0:T(8,128)(2,1)S(1)}) fusion(bf16[512,3072]{1,0:T(8,128)(2,1)} %get-tuple-element.30, bf16[16,1536]{1,0:T(8,128)(2,1)} %param.9, bf16[160,3072]{1,0:T(8,128)(2,1)S(1)} %get-tuple-element.31, ...), kind=kLoop, calls=%fused_computation.39 | loop fusion | bytes 196608
  3.6 1.9 %collective-permute-start = (bf16[16,3072]{1,0:T(8,128)(2,1)S(1)}, bf16[16,3072]{1,0:T(8,128)(2,1)S(1)}, u32[]{:S(2)}, u32[]{:S(2)}) collective-permute-start(bf16[16,3072]{1,0:T(8,128)(2,1)S(1)} %get-tuple-element.29), channel_id=1, source_target_pairs={{0,2},{2,4},{4,6},{6,8},{8,10},{10,12},{12,14},{14,0},{1,3},{3,5},... | collective-permute-start | bytes 294920 | tf_op jit(solution)/shard_map/ppermute | solution.py:44
  5.6 3.9 %collective-permute-start.1 = (bf16[16,3072]{1,0:T(8,128)(2,1)S(1)}, bf16[16,3072]{1,0:T(8,128)(2,1)S(1)}, u32[]{:S(2)}, u32[]{:S(2)}) collective-permute-start(bf16[16,3072]{1,0:T(8,128)(2,1)S(1)} %get-tuple-element.29), channel_id=1, source_target_pairs={{0,14},{2,0},{4,2},{6,4},{8,6},{10,8},{12,10},{14,12},{1,15},{3,1}... | collective-permute-start | bytes 294920 | tf_op jit(solution)/shard_map/ppermute | solution.py:44
  9.5 1.5 %collective-permute-start.4 = (bf16[16,3072]{1,0:T(8,128)(2,1)S(1)}, bf16[16,3072]{1,0:T(8,128)(2,1)S(1)}, u32[]{:S(2)}, u32[]{:S(2)}) collective-permute-start(bf16[16,3072]{1,0:T(8,128)(2,1)S(1)} %get-tuple-element.29), channel_id=1, source_target_pairs={{0,16},{16,0},{1,17},{17,1},{2,18},{18,2},{3,19},{19,3},{4,20},{20... | collective-permute-start | bytes 294920 | tf_op jit(solution)/shard_map/ppermute | solution.py:48
  11.0 1.3 collective-permute-done
  12.3 1.6 %collective-permute-start.5 = (bf16[32,3072]{1,0:T(8,128)(2,1)S(1)}, bf16[32,3072]{1,0:T(8,128)(2,1)S(1)}, u32[]{:S(2)}, u32[]{:S(2)}) collective-permute-start(bf16[32,3072]{1,0:T(8,128)(2,1)S(1)} %pad_maximum_fusion), channel_id=1, source_target_pairs={{0,16},{16,0},{1,17},{17,1},{2,18},{18,2},{3,19},{19,3},{4,20},{20... | collective-permute-start | bytes 589832 | tf_op jit(solution)/shard_map/ppermute | solution.py:48
  13.9 3.2 %collective-permute-start.3 = (bf16[16,3072]{1,0:T(8,128)(2,1)S(1)}, bf16[16,3072]{1,0:T(8,128)(2,1)S(1)}, u32[]{:S(2)}, u32[]{:S(2)}) collective-permute-start(bf16[16,3072]{1,0:T(8,128)(2,1)S(1)} %collective-permute-done.1), channel_id=1, source_target_pairs={{0,14},{2,0},{4,2},{6,4},{8,6},{10,8},{12,10},{14,12},{1,15},{3,1}... | collective-permute-start | bytes 294920 | tf_op jit(solution)/shard_map/ppermute | solution.py:44
  18.4 1.3 collective-permute-done.2
  20.4 2.8 %collective-permute-start.7 = (bf16[16,3072]{1,0:T(8,128)(2,1)S(1)}, bf16[16,3072]{1,0:T(8,128)(2,1)S(1)}, u32[]{:S(2)}, u32[]{:S(2)}) collective-permute-start(bf16[16,3072]{1,0:T(8,128)(2,1)S(1)} %collective-permute-done.2), channel_id=1, source_target_pairs={{0,2},{2,4},{4,6},{6,8},{8,10},{10,12},{12,14},{14,0},{1,3},{3,5},... | collective-permute-start | bytes 294920 | tf_op jit(solution)/shard_map/ppermute | solution.py:44
  26.2 2.0 %collective-permute-done.8 = bf16[16,3072]{1,0:T(8,128)(2,1)S(1)} collective-permute-done((bf16[16,3072]{1,0:T(8,128)(2,1)S(1)}, bf16[16,3072]{1,0:T(8,128)(2,1)S(1)}, u32[]{:S(2)}, u32[]{:S(2)}) %collective-permute-start.8) | collective-permute-done | bytes 98336 | tf_op jit(solution)/shard_map/ppermute | solution.py:44
  28.2 2.1 %collective-permute-start.10 = (bf16[32,3072]{1,0:T(8,128)(2,1)S(1)}, bf16[32,3072]{1,0:T(8,128)(2,1)S(1)}, u32[]{:S(2)}, u32[]{:S(2)}) collective-permute-start(bf16[32,3072]{1,0:T(8,128)(2,1)S(1)} %pad_maximum_fusion.2), channel_id=1, source_target_pairs={{0,16},{16,0},{1,17},{17,1},{2,18},{18,2},{3,19},{19,3},{4,20},{20... | collective-permute-start | bytes 589832 | tf_op jit(solution)/shard_map/ppermute | solution.py:48
  33.1 1.8 %collective-permute-done.9 = bf16[16,3072]{1,0:T(8,128)(2,1)S(1)} collective-permute-done((bf16[16,3072]{1,0:T(8,128)(2,1)S(1)}, bf16[16,3072]{1,0:T(8,128)(2,1)S(1)}, u32[]{:S(2)}, u32[]{:S(2)}) %collective-permute-start.9) | collective-permute-done | bytes 98336 | tf_op jit(solution)/shard_map/ppermute | solution.py:44
  37.5 2.1 %collective-permute-done.11 = bf16[16,3072]{1,0:T(8,128)(2,1)S(1)} collective-permute-done((bf16[16,3072]{1,0:T(8,128)(2,1)S(1)}, bf16[16,3072]{1,0:T(8,128)(2,1)S(1)}, u32[]{:S(2)}, u32[]{:S(2)}) %collective-permute-start.11) | collective-permute-done | bytes 98336 | tf_op jit(solution)/shard_map/ppermute | solution.py:48
  40.2 2.0 %collective-permute-done.13.refs_3_ = bf16[96,3072]{1,0:T(8,128)(2,1)S(1)} collective-permute-done((bf16[96,3072]{1,0:T(8,128)(2,1)S(1)}, bf16[96,3072]{1,0:T(8,128)(2,1)S(1)}, u32[]{:S(2)}, u32[]{:S(2)}) %collective-permute-start.13) | collective-permute-done | bytes 589856 | tf_op jit(solution)/shard_map/ppermute | solution.py:48
  42.2 3.4 %project.1 = bf16[512,1536]{1,0:T(8,128)(2,1)S(1)} custom-call(bf16[160,3072]{1,0:T(8,128)(2,1)S(1)} %get-tuple-element.6.refs_0_, bf16[96,3072]{1,0:T(8,128)(2,1)S(1)} %get-tuple-element.10.refs_1_, bf16[160,3072]{1,0:T(8,128)(2,1)S(1)} %collective-permute-done.12.refs_2_, bf16[96,3072]{1,0:T(8,128)(2,1)S(1)} %collective-permute-done.13.refs_3_, ...), custom_call_target="tpu_custom_call" | custom-call | flops 1 | bytes 1 | tf_op jit(solution)/shard_map/project/pallas_call | solution.py:83
  45.6 1.1 copy-done.2
  46.8 7.2 %all-to-all-start = ((bf16[8,64,1536]{2,1,0:T(8,128)(2,1)}), bf16[8,64,1536]{2,1,0:T(8,128)(2,1)}, u32[]{:S(2)}, u32[]{:S(2)}) async-start(bf16[8,64,1536]{2,1,0:T(8,128)(2,1)} %bitcast.9), calls=%async_computation | async-start | bytes 3145728 | tf_op jit(solution)/shard_map/all_to_all | solution.py:217
  54.0 20.8 %all-to-all-done = bf16[8,64,1536]{2,1,0:T(8,128)(2,1)} async-done(((bf16[8,64,1536]{2,1,0:T(8,128)(2,1)}), bf16[8,64,1536]{2,1,0:T(8,128)(2,1)}, u32[]{:S(2)}, u32[]{:S(2)}) %all-to-all-start) | async-done | bytes 1572896 | tf_op jit(solution)/shard_map/all_to_all | solution.py:217
  74.8 1.7 %pointwise.1 = bf16[512,1536]{1,0:T(8,128)(2,1)S(1)} custom-call(bf16[512,1536]{1,0:T(8,128)(2,1)} %bitcast.3.parts, bf16[1,768]{1,0:T(2,128)(2,1)S(1)} %reshape.15.bias), custom_call_target="tpu_custom_call" | custom-call | flops 1 | bytes 1 | tf_op jit(solution)/shard_map/pointwise/pallas_call | solution.py:115
  76.5 1.1 copy-done.1
  77.6 6.7 %all-to-all-start.1 = ((bf16[8,64,1536]{2,1,0:T(8,128)(2,1)}), bf16[8,64,1536]{2,1,0:T(8,128)(2,1)}, u32[]{:S(2)}, u32[]{:S(2)}) async-start(bf16[8,64,1536]{2,1,0:T(8,128)(2,1)} %bitcast.8), calls=%async_computation.1 | async-start | bytes 3145728 | tf_op jit(solution)/shard_map/all_to_all | solution.py:219
  84.4 19.5 %all-to-all-done.1 = bf16[8,64,1536]{2,1,0:T(8,128)(2,1)} async-done(((bf16[8,64,1536]{2,1,0:T(8,128)(2,1)}), bf16[8,64,1536]{2,1,0:T(8,128)(2,1)}, u32[]{:S(2)}, u32[]{:S(2)}) %all-to-all-start.1) | async-done | bytes 1572896 | tf_op jit(solution)/shard_map/all_to_all | solution.py:219
  103.9 2.5 %back.2 = bf16[256,1536]{1,0:T(8,128)(2,1)S(1)} custom-call(s32[2]{0:T(128)S(1)} %pad_add_fusion.where, bf16[512,1536]{1,0:T(8,128)(2,1)} %bitcast.5.grads, bf16[1536,768]{1,0:T(8,128)(2,1)S(1)} %copy-done), custom_call_target="tpu_custom_call" | custom-call | flops 1 | bytes 1 | tf_op jit(solution)/shard_map/back/pallas_call | solution.py:157
  106.7 2.3 %collective-permute-done.14.given = bf16[256,1536]{1,0:T(8,128)(2,1)S(1)} collective-permute-done((bf16[256,1536]{1,0:T(8,128)(2,1)S(1)}, bf16[256,1536]{1,0:T(8,128)(2,1)S(1)}, u32[]{:S(2)}, u32[]{:S(2)}) %collective-permute-start.14) | collective-permute-done | bytes 786464 | tf_op jit(solution)/shard_map/ppermute | solution.py:48
  109.0 2.6 %back.3 = bf16[256,1536]{1,0:T(8,128)(2,1)S(1)} custom-call(s32[2]{0:T(128)S(1)} %pad_add_fusion.where, bf16[512,1536]{1,0:T(8,128)(2,1)} %bitcast.5.grads, bf16[1536,768]{1,0:T(8,128)(2,1)S(1)} %copy-done, bf16[256,1536]{1,0:T(8,128)(2,1)S(1)} %collective-permute-done.14.given), custom_call_target="tpu_custom_call" | custom-call | flops 1 | bytes 1 | tf_op jit(solution)/shard_map/back/pallas_call | solution.py:157
  111.6 0.9 copy-done.3
  112.5 5.2 %all-to-all-start.2 = ((bf16[16,16,1536]{2,1,0:T(8,128)(2,1)}), bf16[16,16,1536]{2,1,0:T(8,128)(2,1)S(1)}, u32[]{:S(2)}, u32[]{:S(2)}) async-start(bf16[16,16,1536]{2,1,0:T(8,128)(2,1)} %bitcast.11), calls=%async_computation.2 | async-start | bytes 1572864 | tf_op jit(solution)/shard_map/all_to_all | solution.py:223
  117.7 1.0 constant_dynamic-update-slice_fusion.17
  119.6 4.5 %multiply_convert_fusion = bf16[768,1536]{1,0:T(8,128)(2,1)} fusion(bf16[512,3072]{1,0:T(8,128)(2,1)} %constant_dynamic-update-slice_fusion.16, bf16[512,1536]{1,0:T(8,128)(2,1)} %bitcast.5.grads), kind=kOutput, calls=%fused_computation | convolution fusion | flops 1210318848 | bytes 4718592 | tf_op jit(solution)/shard_map/dot_general | solution.py:60
  124.1 4.4 %multiply_convert_fusion.1 = bf16[1536,768]{1,0:T(8,128)(2,1)} fusion(bf16[512,3072]{1,0:T(8,128)(2,1)} %constant_dynamic-update-slice_fusion.16, bf16[512,1536]{1,0:T(8,128)(2,1)} %bitcast.5.grads), kind=kOutput, calls=%fused_computation.1 | convolution fusion | flops 1210318848 | bytes 4718592 | tf_op jit(solution)/shard_map/dot_general | solution.py:60
  128.5 10.9 %all-to-all-done.2 = bf16[16,16,1536]{2,1,0:T(8,128)(2,1)S(1)} async-done(((bf16[16,16,1536]{2,1,0:T(8,128)(2,1)}), bf16[16,16,1536]{2,1,0:T(8,128)(2,1)S(1)}, u32[]{:S(2)}, u32[]{:S(2)}) %all-to-all-start.2) | async-done | bytes 786464 | tf_op jit(solution)/shard_map/all_to_all | solution.py:223
  (48 shorter events, 12.9 us)
Async XLA Ops:
  0.6 41.6 %copy-start = (bf16[1536,768]{1,0:T(8,128)(2,1)S(1)}, bf16[1536,768]{1,0:T(8,128)(2,1)}, u32[]{:S(2)}) copy-start(bf16[1536,768]{1,0:T(8,128)(2,1)} %up.3) | copy-start | bytes 7077892
  0.6 41.6 %copy-start.6 = (bf16[768,1536]{1,0:T(8,128)(2,1)S(1)}, bf16[768,1536]{1,0:T(8,128)(2,1)}, u32[]{:S(2)}) copy-start(bf16[768,1536]{1,0:T(8,128)(2,1)} %refs_5_.1) | copy-start | bytes 7077892
  3.6 8.6 %collective-permute-start = (bf16[16,3072]{1,0:T(8,128)(2,1)S(1)}, bf16[16,3072]{1,0:T(8,128)(2,1)S(1)}, u32[]{:S(2)}, u32[]{:S(2)}) collective-permute-start(bf16[16,3072]{1,0:T(8,128)(2,1)S(1)} %get-tuple-element.29), channel_id=1, source_target_pairs={{0,2},{2,4},{4,6},{6,8},{8,10},{10,12},{12,14},{14,0},{1,3},{3,5},... | collective-permute-start | bytes 294920 | tf_op jit(solution)/shard_map/ppermute | solution.py:44
  5.6 6.7 %collective-permute-start.1 = (bf16[16,3072]{1,0:T(8,128)(2,1)S(1)}, bf16[16,3072]{1,0:T(8,128)(2,1)S(1)}, u32[]{:S(2)}, u32[]{:S(2)}) collective-permute-start(bf16[16,3072]{1,0:T(8,128)(2,1)S(1)} %get-tuple-element.29), channel_id=1, source_target_pairs={{0,14},{2,0},{4,2},{6,4},{8,6},{10,8},{12,10},{14,12},{1,15},{3,1}... | collective-permute-start | bytes 294920 | tf_op jit(solution)/shard_map/ppermute | solution.py:44
  9.5 15.4 %collective-permute-start.4 = (bf16[16,3072]{1,0:T(8,128)(2,1)S(1)}, bf16[16,3072]{1,0:T(8,128)(2,1)S(1)}, u32[]{:S(2)}, u32[]{:S(2)}) collective-permute-start(bf16[16,3072]{1,0:T(8,128)(2,1)S(1)} %get-tuple-element.29), channel_id=1, source_target_pairs={{0,16},{16,0},{1,17},{17,1},{2,18},{18,2},{3,19},{19,3},{4,20},{20... | collective-permute-start | bytes 294920 | tf_op jit(solution)/shard_map/ppermute | solution.py:48
  12.3 18.7 %collective-permute-start.5 = (bf16[32,3072]{1,0:T(8,128)(2,1)S(1)}, bf16[32,3072]{1,0:T(8,128)(2,1)S(1)}, u32[]{:S(2)}, u32[]{:S(2)}) collective-permute-start(bf16[32,3072]{1,0:T(8,128)(2,1)S(1)} %pad_maximum_fusion), channel_id=1, source_target_pairs={{0,16},{16,0},{1,17},{17,1},{2,18},{18,2},{3,19},{19,3},{4,20},{20... | collective-permute-start | bytes 589832 | tf_op jit(solution)/shard_map/ppermute | solution.py:48
  13.9 5.8 %collective-permute-start.2 = (bf16[16,3072]{1,0:T(8,128)(2,1)S(1)}, bf16[16,3072]{1,0:T(8,128)(2,1)S(1)}, u32[]{:S(2)}, u32[]{:S(2)}) collective-permute-start(bf16[16,3072]{1,0:T(8,128)(2,1)S(1)} %collective-permute-done), channel_id=1, source_target_pairs={{0,2},{2,4},{4,6},{6,8},{8,10},{10,12},{12,14},{14,0},{1,3},{3,5},... | collective-permute-start | bytes 294920 | tf_op jit(solution)/shard_map/ppermute | solution.py:44
  13.9 5.8 %collective-permute-start.3 = (bf16[16,3072]{1,0:T(8,128)(2,1)S(1)}, bf16[16,3072]{1,0:T(8,128)(2,1)S(1)}, u32[]{:S(2)}, u32[]{:S(2)}) collective-permute-start(bf16[16,3072]{1,0:T(8,128)(2,1)S(1)} %collective-permute-done.1), channel_id=1, source_target_pairs={{0,14},{2,0},{4,2},{6,4},{8,6},{10,8},{12,10},{14,12},{1,15},{3,1}... | collective-permute-start | bytes 294920 | tf_op jit(solution)/shard_map/ppermute | solution.py:44
  19.7 12.0 %collective-permute-start.6 = (bf16[32,3072]{1,0:T(8,128)(2,1)S(1)}, bf16[32,3072]{1,0:T(8,128)(2,1)S(1)}, u32[]{:S(2)}, u32[]{:S(2)}) collective-permute-start(bf16[32,3072]{1,0:T(8,128)(2,1)S(1)} %pad_maximum_fusion.1), channel_id=1, source_target_pairs={{0,16},{16,0},{1,17},{17,1},{2,18},{18,2},{3,19},{19,3},{4,20},{20... | collective-permute-start | bytes 589832 | tf_op jit(solution)/shard_map/ppermute | solution.py:48
  20.4 5.8 %collective-permute-start.7 = (bf16[16,3072]{1,0:T(8,128)(2,1)S(1)}, bf16[16,3072]{1,0:T(8,128)(2,1)S(1)}, u32[]{:S(2)}, u32[]{:S(2)}) collective-permute-start(bf16[16,3072]{1,0:T(8,128)(2,1)S(1)} %collective-permute-done.2), channel_id=1, source_target_pairs={{0,2},{2,4},{4,6},{6,8},{8,10},{10,12},{12,14},{14,0},{1,3},{3,5},... | collective-permute-start | bytes 294920 | tf_op jit(solution)/shard_map/ppermute | solution.py:44
  23.2 5.0 %collective-permute-start.8 = (bf16[16,3072]{1,0:T(8,128)(2,1)S(1)}, bf16[16,3072]{1,0:T(8,128)(2,1)S(1)}, u32[]{:S(2)}, u32[]{:S(2)}) collective-permute-start(bf16[16,3072]{1,0:T(8,128)(2,1)S(1)} %collective-permute-done.3), channel_id=1, source_target_pairs={{0,14},{2,0},{4,2},{6,4},{8,6},{10,8},{12,10},{14,12},{1,15},{3,1}... | collective-permute-start | bytes 294920 | tf_op jit(solution)/shard_map/ppermute | solution.py:44
  28.2 8.6 %collective-permute-start.10 = (bf16[32,3072]{1,0:T(8,128)(2,1)S(1)}, bf16[32,3072]{1,0:T(8,128)(2,1)S(1)}, u32[]{:S(2)}, u32[]{:S(2)}) collective-permute-start(bf16[32,3072]{1,0:T(8,128)(2,1)S(1)} %pad_maximum_fusion.2), channel_id=1, source_target_pairs={{0,16},{16,0},{1,17},{17,1},{2,18},{18,2},{3,19},{19,3},{4,20},{20... | collective-permute-start | bytes 589832 | tf_op jit(solution)/shard_map/ppermute | solution.py:48
  30.3 4.6 %collective-permute-start.9 = (bf16[16,3072]{1,0:T(8,128)(2,1)S(1)}, bf16[16,3072]{1,0:T(8,128)(2,1)S(1)}, u32[]{:S(2)}, u32[]{:S(2)}) collective-permute-start(bf16[16,3072]{1,0:T(8,128)(2,1)S(1)} %collective-permute-done.8), channel_id=1, source_target_pairs={{0,14},{2,0},{4,2},{6,4},{8,6},{10,8},{12,10},{14,12},{1,15},{3,1}... | collective-permute-start | bytes 294920 | tf_op jit(solution)/shard_map/ppermute | solution.py:44
  32.4 9.8 %collective-permute-start.12 = (bf16[160,3072]{1,0:T(8,128)(2,1)S(1)}, bf16[160,3072]{1,0:T(8,128)(2,1)S(1)}, u32[]{:S(2)}, u32[]{:S(2)}) collective-permute-start(bf16[160,3072]{1,0:T(8,128)(2,1)S(1)} %get-tuple-element.6.refs_0_), channel_id=1, source_target_pairs={{0,1},{1,0},{2,3},{3,2},{4,5},{5,4},{6,7},{7,6},{8,9},{9,8},{10,11... | collective-permute-start | bytes 2949128 | tf_op jit(solution)/shard_map/ppermute | solution.py:48
  34.9 4.6 %collective-permute-start.11 = (bf16[16,3072]{1,0:T(8,128)(2,1)S(1)}, bf16[16,3072]{1,0:T(8,128)(2,1)S(1)}, u32[]{:S(2)}, u32[]{:S(2)}) collective-permute-start(bf16[16,3072]{1,0:T(8,128)(2,1)S(1)} %collective-permute-done.9), channel_id=1, source_target_pairs={{0,16},{16,0},{1,17},{17,1},{2,18},{18,2},{3,19},{19,3},{4,20},{20... | collective-permute-start | bytes 294920 | tf_op jit(solution)/shard_map/ppermute | solution.py:48
  40.2 2.0 %collective-permute-start.13 = (bf16[96,3072]{1,0:T(8,128)(2,1)S(1)}, bf16[96,3072]{1,0:T(8,128)(2,1)S(1)}, u32[]{:S(2)}, u32[]{:S(2)}) collective-permute-start(bf16[96,3072]{1,0:T(8,128)(2,1)S(1)} %get-tuple-element.10.refs_1_), channel_id=1, source_target_pairs={{0,1},{1,0},{2,3},{3,2},{4,5},{5,4},{6,7},{7,6},{8,9},{9,8},{10,11... | collective-permute-start | bytes 1769480 | tf_op jit(solution)/shard_map/ppermute | solution.py:48
  42.2 3.4 %copy-start.4 = (bf16[96,3072]{1,0:T(8,128)(2,1)}, bf16[96,3072]{1,0:T(8,128)(2,1)S(1)}, u32[]{:S(2)}) copy-start(bf16[96,3072]{1,0:T(8,128)(2,1)S(1)} %collective-permute-done.13.refs_3_) | copy-start | bytes 1769476
  45.6 1.1 copy-start.2
  46.8 7.2 %copy-start.7 = (bf16[768]{0:T(1024)(128)(2,1)S(1)}, bf16[768]{0:T(1024)(128)(2,1)}, u32[]{:S(2)}) copy-start(bf16[768]{0:T(1024)(128)(2,1)} %param.7) | copy-start | bytes 4612
  46.8 28.0 %all-to-all-start = ((bf16[8,64,1536]{2,1,0:T(8,128)(2,1)}), bf16[8,64,1536]{2,1,0:T(8,128)(2,1)}, u32[]{:S(2)}, u32[]{:S(2)}) async-start(bf16[8,64,1536]{2,1,0:T(8,128)(2,1)} %bitcast.9), calls=%async_computation | async-start | bytes 3145728 | tf_op jit(solution)/shard_map/all_to_all | solution.py:217
  76.5 1.1 copy-start.1
  77.6 26.3 %all-to-all-start.1 = ((bf16[8,64,1536]{2,1,0:T(8,128)(2,1)}), bf16[8,64,1536]{2,1,0:T(8,128)(2,1)}, u32[]{:S(2)}, u32[]{:S(2)}) async-start(bf16[8,64,1536]{2,1,0:T(8,128)(2,1)} %bitcast.8), calls=%async_computation.1 | async-start | bytes 3145728 | tf_op jit(solution)/shard_map/all_to_all | solution.py:219
  106.4 2.6 %collective-permute-start.14 = (bf16[256,1536]{1,0:T(8,128)(2,1)S(1)}, bf16[256,1536]{1,0:T(8,128)(2,1)S(1)}, u32[]{:S(2)}, u32[]{:S(2)}) collective-permute-start(bf16[256,1536]{1,0:T(8,128)(2,1)S(1)} %back.2), channel_id=1, source_target_pairs={{0,1},{1,0},{2,3},{3,2},{4,5},{5,4},{6,7},{7,6},{8,9},{9,8},{10,11... | collective-permute-start | bytes 2359304 | tf_op jit(solution)/shard_map/ppermute | solution.py:48
  111.6 0.9 copy-start.3
  112.5 6.2 %copy-start.5 = (bf16[96,3072]{1,0:T(8,128)(2,1)S(1)}, bf16[96,3072]{1,0:T(8,128)(2,1)}, u32[]{:S(2)}) copy-start(bf16[96,3072]{1,0:T(8,128)(2,1)} %copy-done.4) | copy-start | bytes 1769476
  112.5 26.9 %all-to-all-start.2 = ((bf16[16,16,1536]{2,1,0:T(8,128)(2,1)}), bf16[16,16,1536]{2,1,0:T(8,128)(2,1)S(1)}, u32[]{:S(2)}, u32[]{:S(2)}) async-start(bf16[16,16,1536]{2,1,0:T(8,128)(2,1)} %bitcast.11), calls=%async_computation.2 | async-start | bytes 1572864 | tf_op jit(solution)/shard_map/all_to_all | solution.py:223

commit v3 on v2

v3 whole, which is shorter than its diff:
```python
import functools
import math

import jax
import jax.numpy as jnp
from jax import lax
from jax.experimental import pallas as pl
from jax.experimental.pallas import tpu as pltpu
from jax.sharding import Mesh, PartitionSpec as P

ROW = ("y", "x_hi")
COL = ("x_lo", "z", "core")
BF16 = jnp.bfloat16
F32 = jnp.float32
ZN = 8
RN = 8
BLOCKS = tuple((side, k) for k in (0, -1, -2, -3, 1, 2, 3, 4) for side in (0, 1))
WHOLE = pl.BlockSpec(memory_space=pltpu.VMEM)
UNREAD = pl.BlockSpec(memory_space=pl.ANY)


def light():
    return pl.CostEstimate(flops=1, bytes_accessed=1, transcendentals=0)


def params(steps):
    return pltpu.CompilerParams(
        dimension_semantics=("arbitrary",) * steps, vmem_limit_bytes=56 * 2**20
    )


def gelu_value(hidden):
    return hidden * 0.5 * (1.0 + lax.erf(hidden / math.sqrt(2.0)))


def gelu_slope(hidden):
    cumulative = 0.5 * (1.0 + lax.erf(hidden / math.sqrt(2.0)))
    density = jnp.exp(-0.5 * hidden * hidden) / math.sqrt(2.0 * math.pi)
    return cumulative + hidden * density


def shift_z(x, k):
    return lax.ppermute(x, "z", [(i, (i + k) % ZN) for i in range(ZN)])


def swap(x, axis):
    return lax.ppermute(x, axis, [(0, 1), (1, 0)])


def dot(a, b):
    return jnp.dot(a, b, preferred_element_type=F32)


def dot_t(a, b):
    return lax.dot_general(a, b, (((1,), (1,)), ((), ())), preferred_element_type=F32)


def dot_rows(a, b):
    return lax.dot_general(a, b, (((0,), (0,)), ((), ())), preferred_element_type=F32)


def pack_kernel(tokens, cotangent, out):
    width = tokens.shape[1]
    out[:, :width] = tokens[...]
    out[:, width:] = cotangent[...]


def pack(tokens, cotangent):
    return pl.pallas_call(
        pack_kernel,
        out_shape=jax.ShapeDtypeStruct((tokens.shape[0], 2 * tokens.shape[1]), BF16),
        in_specs=[WHOLE] * 2,
        out_specs=WHOLE,
        compiler_params=params(0),
        cost_estimate=light(),
        name="pack",
    )(tokens, cotangent)


def project_kernel(pieces, width, *refs):
    given, (up, up_two, down, down_two, out, kept, rows, sem) = refs[:pieces], refs[pieces:]
    j = pl.program_id(0)
    keep = pltpu.make_async_copy(rows, kept, sem)

    @pl.when(j == 0)
    def _():
        base = 0
        for piece in given:
            rows[base : base + piece.shape[0], :] = piece[...]
            base += piece.shape[0]
        keep.start()

    for step, weight in ((0, up), (1, up_two)):

        @pl.when(j // 2 == step)
        def _():
            out[...] = dot(rows[:, :width], weight[...]).astype(BF16)

    for step, weight in ((2, down), (3, down_two)):

        @pl.when(j // 2 == step)
        def _():
            out[...] = dot_t(rows[:, width:], weight[...]).astype(BF16)

    @pl.when(j == 7)
    def _():
        keep.wait()


def project(pieces, up, up_two, down, down_two):
    width, units = up.shape
    tile = units // 2
    count = sum(piece.shape[0] for piece in pieces)

    def columns(first):
        return pl.BlockSpec((width, tile), lambda j: (0, jnp.clip(j - first, 0, 1)))

    def lines(first):
        return pl.BlockSpec((tile, width), lambda j: (jnp.clip(j - first, 0, 1), 0))

    return pl.pallas_call(
        functools.partial(project_kernel, len(pieces), width),
        grid=(8,),
        out_shape=[
            jax.ShapeDtypeStruct((count, 4 * units), BF16),
            jax.ShapeDtypeStruct((count, 2 * width), BF16),
        ],
        in_specs=[pl.BlockSpec(piece.shape, lambda j: (0, 0)) for piece in pieces]
        + [columns(0), columns(2), lines(4), lines(6)],
        out_specs=[pl.BlockSpec((count, tile), lambda j: (0, j)), UNREAD],
        scratch_shapes=[pltpu.VMEM((count, 2 * width), BF16), pltpu.SemaphoreType.DMA],
        compiler_params=params(1),
        cost_estimate=light(),
        name="project",
    )(*pieces, up, up_two, down, down_two)


def pointwise_kernel(parts, bias, bias_two, out):
    count = parts.shape[0] // RN
    units = parts.shape[1] // 4
    for k, offset in enumerate((bias, bias_two)):
        hidden = offset[...].astype(F32) + jnp.zeros((count, units), F32)
        act_grad = jnp.zeros((count, units), F32)
        for r in range(RN):
            some = parts[r * count : (r + 1) * count, :]
            hidden += some[:, k * units : (k + 1) * units].astype(F32)
            act_grad += some[:, (2 + k) * units : (3 + k) * units].astype(F32)
        activated = gelu_value(hidden).astype(BF16)
        hidden_grad = (act_grad * gelu_slope(hidden)).astype(BF16)
        at = (3 - k) * units
        for r in range(RN):
            out[r * count : (r + 1) * count, k * units : (k + 1) * units] = hidden_grad
            out[r * count : (r + 1) * count, at : at + units] = activated


def pointwise(parts, bias, bias_two):
    return pl.pallas_call(
        pointwise_kernel,
        out_shape=jax.ShapeDtypeStruct(parts.shape, BF16),
        in_specs=[WHOLE] * 3,
        out_specs=WHOLE,
        compiler_params=params(0),
        cost_estimate=light(),
        name="pointwise",
    )(parts, bias.reshape(1, -1), bias_two.reshape(1, -1))


def back_kernel(share, where, grads, up, up_two, out, rows):
    units = up.shape[1]

    @pl.when(pl.program_id(0) == 0)
    def _():
        z, x = where[0], where[1]
        for i, (side, k) in enumerate(BLOCKS):
            owner = lax.rem(z + k + ZN, ZN) + ZN * (1 - x if side else x)
            at = pl.multiple_of(owner * share, share)
            rows[pl.ds(at, share), :] = grads[i * share : (i + 1) * share, :]

    part = dot_t(rows[:, :units], up[...]) + dot_t(rows[:, units:], up_two[...])
    out[...] = part.astype(BF16)


def back(where, both, up, up_two, share):
    width, units = up.shape
    count = both.shape[0]
    tile = width // 3
    return pl.pallas_call(
        functools.partial(back_kernel, share),
        grid=(3,),
        out_shape=jax.ShapeDtypeStruct((count, width), BF16),
        in_specs=[
            pl.BlockSpec(memory_space=pltpu.SMEM),
            pl.BlockSpec((count, 2 * units), lambda j: (0, 0)),
            pl.BlockSpec((tile, units), lambda j: (j, 0)),
            pl.BlockSpec((tile, units), lambda j: (j, 0)),
        ],
        out_specs=pl.BlockSpec((count, tile), lambda j: (0, j)),
        scratch_shapes=[pltpu.VMEM((count, 2 * units), BF16)],
        compiler_params=params(1),
        cost_estimate=light(),
        name="back",
    )(where, both, up, up_two)


def collect_kernel(parts, out):
    count = out.shape[0]
    sums = parts[:count, :].astype(F32)
    for r in range(1, parts.shape[0] // count):
        sums += parts[r * count : (r + 1) * count, :].astype(F32)
    out[...] = sums.astype(BF16)


def collect(parts, share):
    return pl.pallas_call(
        collect_kernel,
        out_shape=jax.ShapeDtypeStruct((share, parts.shape[1]), BF16),
        in_specs=[WHOLE],
        out_specs=WHOLE,
        compiler_params=params(0),
        cost_estimate=light(),
        name="collect",
    )(parts)


def outer_kernel(factor, left, left_two, right, right_two, out):
    sums = dot_rows(left[...], right[...]) + dot_rows(left_two[...], right_two[...])
    out[...] = (sums * factor).astype(BF16)


def outer(factor, tiles, left, left_two, right, right_two):
    count = left[0].shape[0]
    size = left[2] // tiles

    def tiled(given):
        array, first, columns = given
        return pl.BlockSpec((count, size), lambda j: (0, first * tiles + j))

    def full(given):
        array, first, columns = given
        return pl.BlockSpec((count, columns), lambda j: (0, first))

    return pl.pallas_call(
        functools.partial(outer_kernel, factor),
        grid=(tiles,),
        out_shape=jax.ShapeDtypeStruct((left[2], right[2]), BF16),
        in_specs=[tiled(left), tiled(left_two), full(right), full(right_two)],
        out_specs=pl.BlockSpec((size, right[2]), lambda j: (j, 0)),
        compiler_params=params(1),
        cost_estimate=light(),
        name="outer",
    )(left[0], left_two[0], right[0], right_two[0])


def on_device(tokens, up_weight, up_bias, down_weight, cotangent):
    width, units = up_weight.shape
    share = tokens.shape[0]
    where = jnp.stack([lax.axis_index("z"), lax.axis_index("x_lo")]).astype(jnp.int32)

    held = pack(tokens, cotangent)
    across = swap(held, "x_lo")
    pieces = [held, across]
    forward = jnp.concatenate([held, across], axis=0)
    backward = held
    fore, aft = [], []
    for k in range(1, ZN // 2 + 1):
        backward = shift_z(backward, -1)
        if k < ZN // 2:
            forward = shift_z(forward, 1)
            fore.append(forward)
        aft += [backward, swap(backward, "x_lo")]
    pieces += fore + aft

    up_two, down_two, bias_two = (swap(w, "core") for w in (up_weight, down_weight, up_bias))
    parts, rows = project(pieces, up_weight, up_two, down_weight, down_two)
    parts = lax.all_to_all(parts, ROW, 0, 0, tiled=True)
    both = pointwise(parts, up_bias, bias_two)
    both = lax.all_to_all(both, ROW, 0, 0, tiled=True)

    near = back(where, both, up_weight, up_two, share)
    near = lax.all_to_all(near, ("x_lo", "z"), 0, 0, tiled=True)
    grad_tokens = collect(near, share)

    rows_two = swap(rows, "core")
    both_two = swap(both[:, units : 3 * units], "core")
    factor = 1.0 / math.sqrt(2 * rows.shape[0])
    grad_up = outer(
        factor, 3, (rows, 0, width), (rows_two, 0, width), (both, 0, units), (both_two, 0, units)
    )
    grad_down = outer(
        factor, 3, (both, 3, units), (both_two, 1, units), (rows, 1, width), (rows_two, 1, width)
    )
    return (grad_tokens, grad_up, grad_down)


def solution(mesh):
    fine = Mesh(mesh.devices.reshape(4, 2, 2, 8, 2), ROW + COL)
    placed = (P(COL, ROW), P(ROW, COL), P(COL), P(COL, ROW), P(COL, ROW))
    return jax.shard_map(
        on_device,
        mesh=fine,
        in_specs=placed,
        out_specs=(P(COL, ROW), P(ROW, COL), P(COL, ROW)),
        check_vma=False,
    )
```

time: 142 us -> 133 us (0.937)
  waiting for transfers between devices: 64.7 us -> 42.2 us
  Pallas kernels: 10.9 us -> 31.7 us
  matrix products: 8.91 us -> 0 us
  starting transfers between devices: 38.7 us -> 46.1 us
  local copies, waits for them, and re-layouts: 16.1 us -> 9.25 us
  other arithmetic: 0.12 us -> 1.55 us
    pallas_call x4 -> x6, Pallas kernels: 10.2 us -> 29.9 us  [the longest x1 10.8 us: project(): pl.pallas_call(functools.partial(project_kernel, len(pieces), width), gri...]
    all_to_all x1, waiting for transfers between devices: 10.9 us -> 1.53 us  [on_device(): near = lax.all_to_all(near, ('x_lo', 'z'), 0, 0, tiled=True)]
    dot_general x2 -> x0, matrix products: 8.91 us -> none  [dot_rows(): lax.dot_general(a, b, (((0,), (0,)), ((), ())), preferred_element_type=F32)]
    unnamed x31 -> x40, local copies, waits for them, and re-layouts: 15.2 us -> 6.89 us
    all_to_all x1, waiting for transfers between devices: 20.8 us -> 12.5 us  [on_device(): parts = lax.all_to_all(parts, ROW, 0, 0, tiled=True)]
    all_to_all x1, waiting for transfers between devices: 19.5 us -> 13.8 us  [on_device(): both = lax.all_to_all(both, ROW, 0, 0, tiled=True)]
    ppermute x7, starting transfers between devices: 13 us -> 16.8 us  [shift_z(): return lax.ppermute(x, 'z', [(i, (i + k) % ZN) for i in range(ZN)])]
    ppermute x8 -> x10, waiting for transfers between devices: 6.36 us -> 9.48 us  [swap(): return lax.ppermute(x, axis, [(0, 1), (1, 0)])]
  transfers between devices with their start and end apart: 18 -> 20, of which waited for: 11 -> 13; matrix products, arithmetic and copies ran while one was open for 13% -> 3% of each run, Pallas kernels for 0% -> 12%
where the time goes in v3:
time: 133 us; the launch traced here: 132 us
  starting transfers between devices  46.1 us (35%)
  waiting for transfers between devices  42.2 us (32%)
  Pallas kernels  31.7 us (24%)
  local copies, waits for them, and re-layouts  9.25 us (7%)
  other arithmetic  1.55 us (1%)
    ppermute x7, starting transfers between devices, shift_z(): return lax.ppermute(x, 'z', [(i, (i + k) % ZN) for i in range(ZN)])  16.8 us
    all_to_all x1, waiting for transfers between devices, on_device(): both = lax.all_to_all(both, ROW, 0, 0, tiled=True)  13.8 us
    all_to_all x1, waiting for transfers between devices, on_device(): parts = lax.all_to_all(parts, ROW, 0, 0, tiled=True)  12.5 us
    pallas_call x1, Pallas kernels, project(): pl.pallas_call(functools.partial(project_kernel, len(pieces), width), gri...  10.8 us
    pallas_call x2, Pallas kernels, outer(): pl.pallas_call(functools.partial(outer_kernel, factor), grid=(tiles,), ou...  9.57 us
    ppermute x10, waiting for transfers between devices, swap(): return lax.ppermute(x, axis, [(0, 1), (1, 0)])  9.48 us
    ppermute x10, starting transfers between devices, swap(): return lax.ppermute(x, axis, [(0, 1), (1, 0)])  8.32 us
    all_to_all x1, starting transfers between devices, on_device(): parts = lax.all_to_all(parts, ROW, 0, 0, tiled=True)  7.38 us
  transfers between devices with their start and end apart: 20, of which 13 were waited for; matrix products, arithmetic and copies ran while one was open for 3% of the time, Pallas kernels for 12%

profile of v3, /device:TPU:8, one launch (start us, length us, event | category | flops | bytes accessed | tf_op | source)
XLA Modules:
  0.0 131.7 jit_solution(5108272687984768791)
XLA Ops:
  1.2 1.5 %pack.1.refs_0_ = bf16[16,3072]{1,0:T(8,128)(2,1)} custom-call(bf16[16,1536]{1,0:T(8,128)(2,1)} %tokens.1, bf16[16,1536]{1,0:T(8,128)(2,1)} %cotangent.1), custom_call_target="tpu_custom_call" | custom-call | flops 1 | bytes 1 | tf_op jit(solution)/shard_map/pack/pallas_call | solution.py:69
  2.7 1.5 %collective-permute-start = (bf16[16,3072]{1,0:T(8,128)(2,1)}, bf16[16,3072]{1,0:T(8,128)(2,1)S(1)}, u32[]{:S(2)}, u32[]{:S(2)}) collective-permute-start(bf16[16,3072]{1,0:T(8,128)(2,1)} %pack.1.refs_0_), channel_id=1, source_target_pairs={{0,16},{16,0},{1,17},{17,1},{2,18},{18,2},{3,19},{19,3},{4,20},{20... | collective-permute-start | bytes 294920 | tf_op jit(solution)/shard_map/ppermute | solution.py:47
  4.2 3.5 %collective-permute-done.refs_1_ = bf16[16,3072]{1,0:T(8,128)(2,1)S(1)} collective-permute-done((bf16[16,3072]{1,0:T(8,128)(2,1)}, bf16[16,3072]{1,0:T(8,128)(2,1)S(1)}, u32[]{:S(2)}, u32[]{:S(2)}) %collective-permute-start) | collective-permute-done | bytes 98336 | tf_op jit(solution)/shard_map/ppermute | solution.py:47
  8.6 2.0 %collective-permute-start.1 = (bf16[32,3072]{1,0:T(8,128)(2,1)S(1)}, bf16[32,3072]{1,0:T(8,128)(2,1)S(1)}, u32[]{:S(2)}, u32[]{:S(2)}) collective-permute-start(bf16[32,3072]{1,0:T(8,128)(2,1)S(1)} %pad_maximum_fusion), channel_id=1, source_target_pairs={{0,2},{2,4},{4,6},{6,8},{8,10},{10,12},{12,14},{14,0},{1,3},{3,5},... | collective-permute-start | bytes 589832 | tf_op jit(solution)/shard_map/ppermute | solution.py:43
  10.6 4.0 %collective-permute-start.4 = (bf16[16,3072]{1,0:T(8,128)(2,1)}, bf16[16,3072]{1,0:T(8,128)(2,1)S(1)}, u32[]{:S(2)}, u32[]{:S(2)}) collective-permute-start(bf16[16,3072]{1,0:T(8,128)(2,1)} %pack.1.refs_0_), channel_id=1, source_target_pairs={{0,14},{2,0},{4,2},{6,4},{8,6},{10,8},{12,10},{14,12},{1,15},{3,1}... | collective-permute-start | bytes 294920 | tf_op jit(solution)/shard_map/ppermute | solution.py:43
  14.7 2.5 %collective-permute-done.4.refs_5_ = bf16[16,3072]{1,0:T(8,128)(2,1)S(1)} collective-permute-done((bf16[16,3072]{1,0:T(8,128)(2,1)}, bf16[16,3072]{1,0:T(8,128)(2,1)S(1)}, u32[]{:S(2)}, u32[]{:S(2)}) %collective-permute-start.4) | collective-permute-done | bytes 98336 | tf_op jit(solution)/shard_map/ppermute | solution.py:43
  17.2 3.5 %collective-permute-start.6 = (bf16[16,3072]{1,0:T(8,128)(2,1)S(1)}, bf16[16,3072]{1,0:T(8,128)(2,1)S(1)}, u32[]{:S(2)}, u32[]{:S(2)}) collective-permute-start(bf16[16,3072]{1,0:T(8,128)(2,1)S(1)} %collective-permute-done.4.refs_5_), channel_id=1, source_target_pairs={{0,14},{2,0},{4,2},{6,4},{8,6},{10,8},{12,10},{14,12},{1,15},{3,1}... | collective-permute-start | bytes 294920 | tf_op jit(solution)/shard_map/ppermute | solution.py:43
  20.7 1.6 %collective-permute-start.5 = (bf16[16,3072]{1,0:T(8,128)(2,1)S(1)}, bf16[16,3072]{1,0:T(8,128)(2,1)S(1)}, u32[]{:S(2)}, u32[]{:S(2)}) collective-permute-start(bf16[16,3072]{1,0:T(8,128)(2,1)S(1)} %collective-permute-done.4.refs_5_), channel_id=1, source_target_pairs={{0,16},{16,0},{1,17},{17,1},{2,18},{18,2},{3,19},{19,3},{4,20},{20... | collective-permute-start | bytes 294920 | tf_op jit(solution)/shard_map/ppermute | solution.py:47
  22.9 3.6 %collective-permute-start.8 = (bf16[16,3072]{1,0:T(8,128)(2,1)S(1)}, bf16[16,3072]{1,0:T(8,128)(2,1)S(1)}, u32[]{:S(2)}, u32[]{:S(2)}) collective-permute-start(bf16[16,3072]{1,0:T(8,128)(2,1)S(1)} %collective-permute-done.6.refs_7_), channel_id=1, source_target_pairs={{0,14},{2,0},{4,2},{6,4},{8,6},{10,8},{12,10},{14,12},{1,15},{3,1}... | collective-permute-start | bytes 294920 | tf_op jit(solution)/shard_map/ppermute | solution.py:43
  26.5 1.5 %collective-permute-start.7 = (bf16[16,3072]{1,0:T(8,128)(2,1)S(1)}, bf16[16,3072]{1,0:T(8,128)(2,1)S(1)}, u32[]{:S(2)}, u32[]{:S(2)}) collective-permute-start(bf16[16,3072]{1,0:T(8,128)(2,1)S(1)} %collective-permute-done.6.refs_7_), channel_id=1, source_target_pairs={{0,16},{16,0},{1,17},{17,1},{2,18},{18,2},{3,19},{19,3},{4,20},{20... | collective-permute-start | bytes 294920 | tf_op jit(solution)/shard_map/ppermute | solution.py:47
  28.0 1.1 collective-permute-done.8.refs_9_
  29.1 3.7 %collective-permute-start.10 = (bf16[16,3072]{1,0:T(8,128)(2,1)S(1)}, bf16[16,3072]{1,0:T(8,128)(2,1)S(1)}, u32[]{:S(2)}, u32[]{:S(2)}) collective-permute-start(bf16[16,3072]{1,0:T(8,128)(2,1)S(1)} %collective-permute-done.8.refs_9_), channel_id=1, source_target_pairs={{0,14},{2,0},{4,2},{6,4},{8,6},{10,8},{12,10},{14,12},{1,15},{3,1}... | collective-permute-start | bytes 294920 | tf_op jit(solution)/shard_map/ppermute | solution.py:43
  32.8 1.6 %collective-permute-start.9 = (bf16[16,3072]{1,0:T(8,128)(2,1)S(1)}, bf16[16,3072]{1,0:T(8,128)(2,1)S(1)}, u32[]{:S(2)}, u32[]{:S(2)}) collective-permute-start(bf16[16,3072]{1,0:T(8,128)(2,1)S(1)} %collective-permute-done.8.refs_9_), channel_id=1, source_target_pairs={{0,16},{16,0},{1,17},{17,1},{2,18},{18,2},{3,19},{19,3},{4,20},{20... | collective-permute-start | bytes 294920 | tf_op jit(solution)/shard_map/ppermute | solution.py:47
  35.0 1.5 %collective-permute-start.11 = (bf16[16,3072]{1,0:T(8,128)(2,1)S(1)}, bf16[16,3072]{1,0:T(8,128)(2,1)S(1)}, u32[]{:S(2)}, u32[]{:S(2)}) collective-permute-start(bf16[16,3072]{1,0:T(8,128)(2,1)S(1)} %collective-permute-done.10.refs_11_), channel_id=1, source_target_pairs={{0,16},{16,0},{1,17},{17,1},{2,18},{18,2},{3,19},{19,3},{4,20},{20... | collective-permute-start | bytes 294920 | tf_op jit(solution)/shard_map/ppermute | solution.py:47
  37.5 2.1 %collective-permute-done.11.refs_12_ = bf16[16,3072]{1,0:T(8,128)(2,1)S(1)} collective-permute-done((bf16[16,3072]{1,0:T(8,128)(2,1)S(1)}, bf16[16,3072]{1,0:T(8,128)(2,1)S(1)}, u32[]{:S(2)}, u32[]{:S(2)}) %collective-permute-start.11) | collective-permute-done | bytes 98336 | tf_op jit(solution)/shard_map/ppermute | solution.py:47
  41.2 1.4 %copy-done.1 = bf16[1536,768]{1,0:T(8,128)(2,1)} copy-done((bf16[1536,768]{1,0:T(8,128)(2,1)}, bf16[1536,768]{1,0:T(8,128)(2,1)S(1)}, u32[]{:S(2)}) %copy-start.1) | copy-done | bytes 2359320
  42.6 10.8 %project.1 = (bf16[256,3072]{1,0:T(8,128)(2,1)}, bf16[256,3072]{1,0:T(8,128)(2,1)}) custom-call(bf16[16,3072]{1,0:T(8,128)(2,1)} %pack.1.refs_0_, bf16[16,3072]{1,0:T(8,128)(2,1)} %copy-done.7, bf16[32,3072]{1,0:T(8,128)(2,1)} %copy-done.8, bf16[32,3072]{1,0:T(8,128)(2,1)} %copy-done.9, bf16[32,3072]{1,0:T(8,128)(2,1)} %copy-done.10, ...), custom_call_target="tpu_custom_call" | custom-call | flops 1 | bytes 1 | tf_op jit(solution)/shard_map/project/pallas_call | solution.py:121
  53.4 7.4 %all-to-all-start = ((bf16[8,32,3072]{2,1,0:T(8,128)(2,1)}), bf16[8,32,3072]{2,1,0:T(8,128)(2,1)S(1)}, u32[]{:S(2)}, u32[]{:S(2)}) async-start(bf16[8,32,3072]{2,1,0:T(8,128)(2,1)} %bitcast.16), calls=%async_computation | async-start | bytes 3145728 | tf_op jit(solution)/shard_map/all_to_all | solution.py:275
  62.5 12.5 %all-to-all-done = bf16[8,32,3072]{2,1,0:T(8,128)(2,1)S(1)} async-done(((bf16[8,32,3072]{2,1,0:T(8,128)(2,1)}), bf16[8,32,3072]{2,1,0:T(8,128)(2,1)S(1)}, u32[]{:S(2)}, u32[]{:S(2)}) %all-to-all-start) | async-done | bytes 1572896 | tf_op jit(solution)/shard_map/all_to_all | solution.py:275
  75.0 1.1 copy-done.2
  76.2 2.9 %pointwise.1 = bf16[256,3072]{1,0:T(8,128)(2,1)} custom-call(bf16[256,3072]{1,0:T(8,128)(2,1)} %bitcast.13, bf16[1,768]{1,0:T(2,128)(2,1)} %reshape.18.bias, bf16[1,768]{1,0:T(2,128)(2,1)} %reshape.19.bias_two), custom_call_target="tpu_custom_call" | custom-call | flops 1 | bytes 1 | tf_op jit(solution)/shard_map/pointwise/pallas_call | solution.py:157
  79.1 6.3 %all-to-all-start.1 = ((bf16[8,32,3072]{2,1,0:T(8,128)(2,1)}), bf16[8,32,3072]{2,1,0:T(8,128)(2,1)S(1)}, u32[]{:S(2)}, u32[]{:S(2)}) async-start(bf16[8,32,3072]{2,1,0:T(8,128)(2,1)} %bitcast.12), calls=%async_computation.1 | async-start | bytes 3145728 | tf_op jit(solution)/shard_map/all_to_all | solution.py:277
  86.0 13.8 %all-to-all-done.1 = bf16[8,32,3072]{2,1,0:T(8,128)(2,1)S(1)} async-done(((bf16[8,32,3072]{2,1,0:T(8,128)(2,1)}), bf16[8,32,3072]{2,1,0:T(8,128)(2,1)S(1)}, u32[]{:S(2)}, u32[]{:S(2)}) %all-to-all-start.1) | async-done | bytes 1572896 | tf_op jit(solution)/shard_map/all_to_all | solution.py:277
  99.8 1.1 copy-done
  100.9 5.1 %back.1 = bf16[256,1536]{1,0:T(8,128)(2,1)} custom-call(s32[2]{0:T(128)} %pad_add_fusion.where, bf16[256,3072]{1,0:T(8,128)(2,1)} %bitcast.8, bf16[1536,768]{1,0:T(8,128)(2,1)} %up.1, bf16[1536,768]{1,0:T(8,128)(2,1)} %copy-done.1), custom_call_target="tpu_custom_call" | custom-call | flops 1 | bytes 1 | tf_op jit(solution)/shard_map/back/pallas_call | solution.py:187
  106.1 7.3 %all-to-all-start.2 = ((bf16[16,16,1536]{2,1,0:T(8,128)(2,1)}), bf16[16,16,1536]{2,1,0:T(8,128)(2,1)S(1)}, u32[]{:S(2)}, u32[]{:S(2)}) async-start(bf16[16,16,1536]{2,1,0:T(8,128)(2,1)} %bitcast.14), calls=%async_computation.2 | async-start | bytes 1572864 | tf_op jit(solution)/shard_map/all_to_all | solution.py:280
  113.4 1.2 slice.4
  114.7 2.3 %collective-permute-done.16.right_two.left_two = bf16[256,1536]{1,0:T(8,128)(2,1)S(1)} collective-permute-done((bf16[256,1536]{1,0:T(8,128)(2,1)S(1)}, bf16[256,1536]{1,0:T(8,128)(2,1)S(1)}, u32[]{:S(2)}, u32[]{:S(2)}) %collective-permute-start.16) | collective-permute-done | bytes 786464 | tf_op jit(solution)/shard_map/ppermute | solution.py:47
  117.8 4.9 %outer.3 = bf16[768,1536]{1,0:T(8,128)(2,1)} custom-call(bf16[256,3072]{1,0:T(8,128)(2,1)} %bitcast.10, bf16[256,1536]{1,0:T(8,128)(2,1)} %copy-done.5, bf16[256,3072]{1,0:T(8,128)(2,1)} %get-tuple-element.6.left.right, bf16[256,3072]{1,0:T(8,128)(2,1)} %collective-permute-done.15.left_two.right_two), custom_call_target="tpu_custom_call" | custom-call | flops 1 | bytes 1 | tf_op jit(solution)/shard_map/outer/pallas_call | solution.py:242
  122.7 4.7 %outer.2 = bf16[1536,768]{1,0:T(8,128)(2,1)} custom-call(bf16[256,3072]{1,0:T(8,128)(2,1)} %get-tuple-element.6.left.right, bf16[256,3072]{1,0:T(8,128)(2,1)} %collective-permute-done.15.left_two.right_two, bf16[256,3072]{1,0:T(8,128)(2,1)} %bitcast.11, bf16[256,1536]{1,0:T(8,128)(2,1)} %copy-done.5), custom_call_target="tpu_custom_call" | custom-call | flops 1 | bytes 1 | tf_op jit(solution)/shard_map/outer/pallas_call | solution.py:242
  127.4 1.5 %all-to-all-done.2 = bf16[16,16,1536]{2,1,0:T(8,128)(2,1)S(1)} async-done(((bf16[16,16,1536]{2,1,0:T(8,128)(2,1)}), bf16[16,16,1536]{2,1,0:T(8,128)(2,1)S(1)}, u32[]{:S(2)}, u32[]{:S(2)}) %all-to-all-start.2) | async-done | bytes 786464 | tf_op jit(solution)/shard_map/all_to_all | solution.py:280
  129.8 1.9 %collect.1 = bf16[16,1536]{1,0:T(8,128)(2,1)} custom-call(bf16[256,1536]{1,0:T(8,128)(2,1)} %bitcast.15), custom_call_target="tpu_custom_call" | custom-call | flops 1 | bytes 1 | tf_op jit(solution)/shard_map/collect/pallas_call | solution.py:214
  (60 shorter events, 9.5 us)
Async XLA Ops:
  0.6 39.1 %collective-permute-start.13 = (bf16[768,1536]{1,0:T(8,128)(2,1)}, bf16[768,1536]{1,0:T(8,128)(2,1)S(1)}, u32[]{:S(2)}, u32[]{:S(2)}) collective-permute-start(bf16[768,1536]{1,0:T(8,128)(2,1)} %refs_15_.1), channel_id=1, source_target_pairs={{0,1},{1,0},{2,3},{3,2},{4,5},{5,4},{6,7},{7,6},{8,9},{9,8},{10,11... | collective-permute-start | bytes 7077896 | tf_op jit(solution)/shard_map/ppermute | solution.py:47
  0.7 39.0 %collective-permute-start.12 = (bf16[1536,768]{1,0:T(8,128)(2,1)}, bf16[1536,768]{1,0:T(8,128)(2,1)S(1)}, u32[]{:S(2)}, u32[]{:S(2)}) collective-permute-start(bf16[1536,768]{1,0:T(8,128)(2,1)} %up.1), channel_id=1, source_target_pairs={{0,1},{1,0},{2,3},{3,2},{4,5},{5,4},{6,7},{7,6},{8,9},{9,8},{10,11... | collective-permute-start | bytes 7077896 | tf_op jit(solution)/shard_map/ppermute | solution.py:47
  2.7 5.0 %collective-permute-start = (bf16[16,3072]{1,0:T(8,128)(2,1)}, bf16[16,3072]{1,0:T(8,128)(2,1)S(1)}, u32[]{:S(2)}, u32[]{:S(2)}) collective-permute-start(bf16[16,3072]{1,0:T(8,128)(2,1)} %pack.1.refs_0_), channel_id=1, source_target_pairs={{0,16},{16,0},{1,17},{17,1},{2,18},{18,2},{3,19},{19,3},{4,20},{20... | collective-permute-start | bytes 294920 | tf_op jit(solution)/shard_map/ppermute | solution.py:47
  7.7 32.0 %copy-start.7 = (bf16[16,3072]{1,0:T(8,128)(2,1)}, bf16[16,3072]{1,0:T(8,128)(2,1)S(1)}, u32[]{:S(2)}) copy-start(bf16[16,3072]{1,0:T(8,128)(2,1)S(1)} %collective-permute-done.refs_1_) | copy-start | bytes 294916
  8.6 12.1 %collective-permute-start.1 = (bf16[32,3072]{1,0:T(8,128)(2,1)S(1)}, bf16[32,3072]{1,0:T(8,128)(2,1)S(1)}, u32[]{:S(2)}, u32[]{:S(2)}) collective-permute-start(bf16[32,3072]{1,0:T(8,128)(2,1)S(1)} %pad_maximum_fusion), channel_id=1, source_target_pairs={{0,2},{2,4},{4,6},{6,8},{8,10},{10,12},{12,14},{14,0},{1,3},{3,5},... | collective-permute-start | bytes 589832 | tf_op jit(solution)/shard_map/ppermute | solution.py:43
  10.6 6.6 %collective-permute-start.4 = (bf16[16,3072]{1,0:T(8,128)(2,1)}, bf16[16,3072]{1,0:T(8,128)(2,1)S(1)}, u32[]{:S(2)}, u32[]{:S(2)}) collective-permute-start(bf16[16,3072]{1,0:T(8,128)(2,1)} %pack.1.refs_0_), channel_id=1, source_target_pairs={{0,14},{2,0},{4,2},{6,4},{8,6},{10,8},{12,10},{14,12},{1,15},{3,1}... | collective-permute-start | bytes 294920 | tf_op jit(solution)/shard_map/ppermute | solution.py:43
  17.2 22.5 %copy-start.11 = (bf16[16,3072]{1,0:T(8,128)(2,1)}, bf16[16,3072]{1,0:T(8,128)(2,1)S(1)}, u32[]{:S(2)}) copy-start(bf16[16,3072]{1,0:T(8,128)(2,1)S(1)} %collective-permute-done.4.refs_5_) | copy-start | bytes 294916
  17.2 5.7 %collective-permute-start.6 = (bf16[16,3072]{1,0:T(8,128)(2,1)S(1)}, bf16[16,3072]{1,0:T(8,128)(2,1)S(1)}, u32[]{:S(2)}, u32[]{:S(2)}) collective-permute-start(bf16[16,3072]{1,0:T(8,128)(2,1)S(1)} %collective-permute-done.4.refs_5_), channel_id=1, source_target_pairs={{0,14},{2,0},{4,2},{6,4},{8,6},{10,8},{12,10},{14,12},{1,15},{3,1}... | collective-permute-start | bytes 294920 | tf_op jit(solution)/shard_map/ppermute | solution.py:43
  20.7 19.0 %copy-start.8 = (bf16[32,3072]{1,0:T(8,128)(2,1)}, bf16[32,3072]{1,0:T(8,128)(2,1)S(1)}, u32[]{:S(2)}) copy-start(bf16[32,3072]{1,0:T(8,128)(2,1)S(1)} %collective-permute-done.1.refs_2_) | copy-start | bytes 589828
  20.7 12.1 %collective-permute-start.2 = (bf16[32,3072]{1,0:T(8,128)(2,1)S(1)}, bf16[32,3072]{1,0:T(8,128)(2,1)S(1)}, u32[]{:S(2)}, u32[]{:S(2)}) collective-permute-start(bf16[32,3072]{1,0:T(8,128)(2,1)S(1)} %collective-permute-done.1.refs_2_), channel_id=1, source_target_pairs={{0,2},{2,4},{4,6},{6,8},{8,10},{10,12},{12,14},{14,0},{1,3},{3,5},... | collective-permute-start | bytes 589832 | tf_op jit(solution)/shard_map/ppermute | solution.py:43
  20.7 5.8 %collective-permute-start.5 = (bf16[16,3072]{1,0:T(8,128)(2,1)S(1)}, bf16[16,3072]{1,0:T(8,128)(2,1)S(1)}, u32[]{:S(2)}, u32[]{:S(2)}) collective-permute-start(bf16[16,3072]{1,0:T(8,128)(2,1)S(1)} %collective-permute-done.4.refs_5_), channel_id=1, source_target_pairs={{0,16},{16,0},{1,17},{17,1},{2,18},{18,2},{3,19},{19,3},{4,20},{20... | collective-permute-start | bytes 294920 | tf_op jit(solution)/shard_map/ppermute | solution.py:47
  22.9 16.8 %copy-start.12 = (bf16[16,3072]{1,0:T(8,128)(2,1)}, bf16[16,3072]{1,0:T(8,128)(2,1)S(1)}, u32[]{:S(2)}) copy-start(bf16[16,3072]{1,0:T(8,128)(2,1)S(1)} %collective-permute-done.6.refs_7_) | copy-start | bytes 294916
  22.9 6.2 %collective-permute-start.8 = (bf16[16,3072]{1,0:T(8,128)(2,1)S(1)}, bf16[16,3072]{1,0:T(8,128)(2,1)S(1)}, u32[]{:S(2)}, u32[]{:S(2)}) collective-permute-start(bf16[16,3072]{1,0:T(8,128)(2,1)S(1)} %collective-permute-done.6.refs_7_), channel_id=1, source_target_pairs={{0,14},{2,0},{4,2},{6,4},{8,6},{10,8},{12,10},{14,12},{1,15},{3,1}... | collective-permute-start | bytes 294920 | tf_op jit(solution)/shard_map/ppermute | solution.py:43
  26.5 13.2 %copy-start.13 = (bf16[16,3072]{1,0:T(8,128)(2,1)}, bf16[16,3072]{1,0:T(8,128)(2,1)S(1)}, u32[]{:S(2)}) copy-start(bf16[16,3072]{1,0:T(8,128)(2,1)S(1)} %collective-permute-done.5.refs_6_) | copy-start | bytes 294916
  26.5 6.3 %collective-permute-start.7 = (bf16[16,3072]{1,0:T(8,128)(2,1)S(1)}, bf16[16,3072]{1,0:T(8,128)(2,1)S(1)}, u32[]{:S(2)}, u32[]{:S(2)}) collective-permute-start(bf16[16,3072]{1,0:T(8,128)(2,1)S(1)} %collective-permute-done.6.refs_7_), channel_id=1, source_target_pairs={{0,16},{16,0},{1,17},{17,1},{2,18},{18,2},{3,19},{19,3},{4,20},{20... | collective-permute-start | bytes 294920 | tf_op jit(solution)/shard_map/ppermute | solution.py:47
  29.1 10.6 %copy-start.14 = (bf16[16,3072]{1,0:T(8,128)(2,1)}, bf16[16,3072]{1,0:T(8,128)(2,1)S(1)}, u32[]{:S(2)}) copy-start(bf16[16,3072]{1,0:T(8,128)(2,1)S(1)} %collective-permute-done.8.refs_9_) | copy-start | bytes 294916
  29.1 5.9 %collective-permute-start.10 = (bf16[16,3072]{1,0:T(8,128)(2,1)S(1)}, bf16[16,3072]{1,0:T(8,128)(2,1)S(1)}, u32[]{:S(2)}, u32[]{:S(2)}) collective-permute-start(bf16[16,3072]{1,0:T(8,128)(2,1)S(1)} %collective-permute-done.8.refs_9_), channel_id=1, source_target_pairs={{0,14},{2,0},{4,2},{6,4},{8,6},{10,8},{12,10},{14,12},{1,15},{3,1}... | collective-permute-start | bytes 294920 | tf_op jit(solution)/shard_map/ppermute | solution.py:43
  32.8 7.0 %copy-start.9 = (bf16[32,3072]{1,0:T(8,128)(2,1)}, bf16[32,3072]{1,0:T(8,128)(2,1)S(1)}, u32[]{:S(2)}) copy-start(bf16[32,3072]{1,0:T(8,128)(2,1)S(1)} %collective-permute-done.2.refs_3_) | copy-start | bytes 589828
  32.8 6.9 %collective-permute-start.3 = (bf16[32,3072]{1,0:T(8,128)(2,1)S(1)}, bf16[32,3072]{1,0:T(8,128)(2,1)S(1)}, u32[]{:S(2)}, u32[]{:S(2)}) collective-permute-start(bf16[32,3072]{1,0:T(8,128)(2,1)S(1)} %collective-permute-done.2.refs_3_), channel_id=1, source_target_pairs={{0,2},{2,4},{4,6},{6,8},{8,10},{10,12},{12,14},{14,0},{1,3},{3,5},... | collective-permute-start | bytes 589832 | tf_op jit(solution)/shard_map/ppermute | solution.py:43
  32.8 7.0 %copy-start.15 = (bf16[16,3072]{1,0:T(8,128)(2,1)}, bf16[16,3072]{1,0:T(8,128)(2,1)S(1)}, u32[]{:S(2)}) copy-start(bf16[16,3072]{1,0:T(8,128)(2,1)S(1)} %collective-permute-done.7.refs_8_) | copy-start | bytes 294916
  32.8 4.7 %collective-permute-start.9 = (bf16[16,3072]{1,0:T(8,128)(2,1)S(1)}, bf16[16,3072]{1,0:T(8,128)(2,1)S(1)}, u32[]{:S(2)}, u32[]{:S(2)}) collective-permute-start(bf16[16,3072]{1,0:T(8,128)(2,1)S(1)} %collective-permute-done.8.refs_9_), channel_id=1, source_target_pairs={{0,16},{16,0},{1,17},{17,1},{2,18},{18,2},{3,19},{19,3},{4,20},{20... | collective-permute-start | bytes 294920 | tf_op jit(solution)/shard_map/ppermute | solution.py:47
  35.0 4.8 %copy-start.16 = (bf16[16,3072]{1,0:T(8,128)(2,1)}, bf16[16,3072]{1,0:T(8,128)(2,1)S(1)}, u32[]{:S(2)}) copy-start(bf16[16,3072]{1,0:T(8,128)(2,1)S(1)} %collective-permute-done.10.refs_11_) | copy-start | bytes 294916
  35.0 4.6 %collective-permute-start.11 = (bf16[16,3072]{1,0:T(8,128)(2,1)S(1)}, bf16[16,3072]{1,0:T(8,128)(2,1)S(1)}, u32[]{:S(2)}, u32[]{:S(2)}) collective-permute-start(bf16[16,3072]{1,0:T(8,128)(2,1)S(1)} %collective-permute-done.10.refs_11_), channel_id=1, source_target_pairs={{0,16},{16,0},{1,17},{17,1},{2,18},{18,2},{3,19},{19,3},{4,20},{20... | collective-permute-start | bytes 294920 | tf_op jit(solution)/shard_map/ppermute | solution.py:47
  37.5 2.3 %copy-start.17 = (bf16[16,3072]{1,0:T(8,128)(2,1)}, bf16[16,3072]{1,0:T(8,128)(2,1)S(1)}, u32[]{:S(2)}) copy-start(bf16[16,3072]{1,0:T(8,128)(2,1)S(1)} %collective-permute-done.9.refs_10_) | copy-start | bytes 294916
  53.4 7.4 %copy-start.19 = (bf16[768]{0:T(1024)(128)(2,1)S(1)}, bf16[768]{0:T(1024)(128)(2,1)}, u32[]{:S(2)}) copy-start(bf16[768]{0:T(1024)(128)(2,1)} %param.7) | copy-start | bytes 4612
  53.4 21.7 %all-to-all-start = ((bf16[8,32,3072]{2,1,0:T(8,128)(2,1)}), bf16[8,32,3072]{2,1,0:T(8,128)(2,1)S(1)}, u32[]{:S(2)}, u32[]{:S(2)}) async-start(bf16[8,32,3072]{2,1,0:T(8,128)(2,1)} %bitcast.16), calls=%async_computation | async-start | bytes 3145728 | tf_op jit(solution)/shard_map/all_to_all | solution.py:275
  60.8 1.2 collective-permute-start.14
  79.1 6.3 %copy-start.3 = (bf16[256,3072]{1,0:T(8,128)(2,1)S(1)}, bf16[256,3072]{1,0:T(8,128)(2,1)}, u32[]{:S(2)}) copy-start(bf16[256,3072]{1,0:T(8,128)(2,1)} %get-tuple-element.6.left.right) | copy-start | bytes 4718596
  79.1 20.7 %all-to-all-start.1 = ((bf16[8,32,3072]{2,1,0:T(8,128)(2,1)}), bf16[8,32,3072]{2,1,0:T(8,128)(2,1)S(1)}, u32[]{:S(2)}, u32[]{:S(2)}) async-start(bf16[8,32,3072]{2,1,0:T(8,128)(2,1)} %bitcast.12), calls=%async_computation.1 | async-start | bytes 3145728 | tf_op jit(solution)/shard_map/all_to_all | solution.py:277
  85.4 29.3 %collective-permute-start.15 = (bf16[256,3072]{1,0:T(8,128)(2,1)S(1)}, bf16[256,3072]{1,0:T(8,128)(2,1)}, u32[]{:S(2)}, u32[]{:S(2)}) collective-permute-start(bf16[256,3072]{1,0:T(8,128)(2,1)S(1)} %copy-done.3), channel_id=1, source_target_pairs={{0,1},{1,0},{2,3},{3,2},{4,5},{5,4},{6,7},{7,6},{8,9},{9,8},{10,11... | collective-permute-start | bytes 4718600 | tf_op jit(solution)/shard_map/ppermute | solution.py:47
  106.1 22.8 %all-to-all-start.2 = ((bf16[16,16,1536]{2,1,0:T(8,128)(2,1)}), bf16[16,16,1536]{2,1,0:T(8,128)(2,1)S(1)}, u32[]{:S(2)}, u32[]{:S(2)}) async-start(bf16[16,16,1536]{2,1,0:T(8,128)(2,1)} %bitcast.14), calls=%async_computation.2 | async-start | bytes 1572864 | tf_op jit(solution)/shard_map/all_to_all | solution.py:280
  114.5 2.4 %collective-permute-start.16 = (bf16[256,1536]{1,0:T(8,128)(2,1)S(1)}, bf16[256,1536]{1,0:T(8,128)(2,1)S(1)}, u32[]{:S(2)}, u32[]{:S(2)}) collective-permute-start(bf16[256,1536]{1,0:T(8,128)(2,1)S(1)} %slice.4), channel_id=1, source_target_pairs={{0,1},{1,0},{2,3},{3,2},{4,5},{5,4},{6,7},{7,6},{8,9},{9,8},{10,11... | collective-permute-start | bytes 2359304 | tf_op jit(solution)/shard_map/ppermute | solution.py:47
  (8 other events, 8.2 us)

commit v4 on v3

--- a/solution.py
+++ b/solution.py
@@ -16,16 +16,21 @@
 RN = 8
 BLOCKS = tuple((side, k) for k in (0, -1, -2, -3, 1, 2, 3, 4) for side in (0, 1))
 WHOLE = pl.BlockSpec(memory_space=pltpu.VMEM)
-UNREAD = pl.BlockSpec(memory_space=pl.ANY)
+REMAIN = pl.BlockSpec(memory_space=pl.ANY)
+FAR = pl.BlockSpec(memory_space=pltpu.HBM)
 
 
 def light():
     return pl.CostEstimate(flops=1, bytes_accessed=1, transcendentals=0)
 
 
+def heavy():
+    return pl.CostEstimate(flops=2 * 10**10, bytes_accessed=2 * 10**6, transcendentals=0)
+
+
 def params(steps):
     return pltpu.CompilerParams(
-        dimension_semantics=("arbitrary",) * steps, vmem_limit_bytes=56 * 2**20
+        dimension_semantics=("arbitrary",) * steps, vmem_limit_bytes=20 * 2**20
     )
 
 
@@ -72,70 +77,63 @@
         in_specs=[WHOLE] * 2,
         out_specs=WHOLE,
         compiler_params=params(0),
-        cost_estimate=light(),
+        cost_estimate=heavy(),
         name="pack",
     )(tokens, cotangent)
 
 
-def project_kernel(pieces, width, *refs):
-    given, (up, up_two, down, down_two, out, kept, rows, sem) = refs[:pieces], refs[pieces:]
-    j = pl.program_id(0)
-    keep = pltpu.make_async_copy(rows, kept, sem)
-
-    @pl.when(j == 0)
-    def _():
-        base = 0
-        for piece in given:
-            rows[base : base + piece.shape[0], :] = piece[...]
-            base += piece.shape[0]
-        keep.start()
-
-    for step, weight in ((0, up), (1, up_two)):
-
-        @pl.when(j // 2 == step)
-        def _():
-            out[...] = dot(rows[:, :width], weight[...]).astype(BF16)
-
-    for step, weight in ((2, down), (3, down_two)):
-
-        @pl.when(j // 2 == step)
-        def _():
-            out[...] = dot_t(rows[:, width:], weight[...]).astype(BF16)
-
-    @pl.when(j == 7)
-    def _():
-        keep.wait()
+def project_kernel(pieces, width, units, *refs):
+    given, weights = refs[:pieces], refs[pieces : pieces + 4]
+    out, kept, rows, made, sems = refs[pieces + 4 :]
+    loads, base = [], 0
+    for piece in given:
+        at = rows.at[base : base + piece.shape[0], :]
+        loads.append(pltpu.make_async_copy(piece, at, sems.at[len(loads)]))
+        base += piece.shape[0]
+    for copy in loads:
+        copy.start()
+    for copy in loads:
+        copy.wait()
+    sends = [pltpu.make_async_copy(rows, kept, sems.at[pieces])]
+    sends[0].start()
+    for k, weight in enumerate(weights):
+        at = slice(k * units, (k + 1) * units)
+        if k < 2:
+            product = dot(rows[:, :width], weight[...])
+        else:
+            product = dot_t(rows[:, width:], weight[...])
+        made[:, at] = product.astype(BF16)
+        sends.append(
+            pltpu.make_async_copy(made.at[:, at], out.at[:, at], sems.at[pieces + 1 + k])
+        )
+        sends[-1].start()
+    for copy in sends:
+        copy.wait()
 
 
 def project(pieces, up, up_two, down, down_two):
     width, units = up.shape
-    tile = units // 2
     count = sum(piece.shape[0] for piece in pieces)
-
-    def columns(first):
-        return pl.BlockSpec((width, tile), lambda j: (0, jnp.clip(j - first, 0, 1)))
-
-    def lines(first):
-        return pl.BlockSpec((tile, width), lambda j: (jnp.clip(j - first, 0, 1), 0))
-
-    return pl.pallas_call(
-        functools.partial(project_kernel, len(pieces), width),
-        grid=(8,),
+    return pl.pallas_call(
+        functools.partial(project_kernel, len(pieces), width, units),
         out_shape=[
-            jax.ShapeDtypeStruct((count, 4 * units), BF16),
+            pltpu.HBM((count, 4 * units), BF16),
             jax.ShapeDtypeStruct((count, 2 * width), BF16),
         ],
-        in_specs=[pl.BlockSpec(piece.shape, lambda j: (0, 0)) for piece in pieces]
-        + [columns(0), columns(2), lines(4), lines(6)],
-        out_specs=[pl.BlockSpec((count, tile), lambda j: (0, j)), UNREAD],
-        scratch_shapes=[pltpu.VMEM((count, 2 * width), BF16), pltpu.SemaphoreType.DMA],
-        compiler_params=params(1),
+        in_specs=[REMAIN] * len(pieces) + [WHOLE] * 4,
+        out_specs=[FAR, REMAIN],
+        scratch_shapes=[
+            pltpu.VMEM((count, 2 * width), BF16),
+            pltpu.VMEM((count, 4 * units), BF16),
+            pltpu.SemaphoreType.DMA((len(pieces) + 5,)),
+        ],
+        compiler_params=params(0),
         cost_estimate=light(),
         name="project",
     )(*pieces, up, up_two, down, down_two)
 
 
-def pointwise_kernel(parts, bias, bias_two, out):
+def pointwise_kernel(parts, bias, bias_two, out, made, sems):
     count = parts.shape[0] // RN
     units = parts.shape[1] // 4
     for k, offset in enumerate((bias, bias_two)):
@@ -148,65 +146,92 @@
         activated = gelu_value(hidden).astype(BF16)
         hidden_grad = (act_grad * gelu_slope(hidden)).astype(BF16)
         at = (3 - k) * units
-        for r in range(RN):
-            out[r * count : (r + 1) * count, k * units : (k + 1) * units] = hidden_grad
-            out[r * count : (r + 1) * count, at : at + units] = activated
+        made[:, k * units : (k + 1) * units] = hidden_grad
+        made[:, at : at + units] = activated
+    sends = [
+        pltpu.make_async_copy(made, out.at[r * count : (r + 1) * count, :], sems.at[r])
+        for r in range(RN)
+    ]
+    for send in sends:
+        send.start()
+    for send in sends:
+        send.wait()
 
 
 def pointwise(parts, bias, bias_two):
     return pl.pallas_call(
         pointwise_kernel,
-        out_shape=jax.ShapeDtypeStruct(parts.shape, BF16),
+        out_shape=pltpu.HBM(parts.shape, BF16),
         in_specs=[WHOLE] * 3,
-        out_specs=WHOLE,
-        compiler_params=params(0),
-        cost_estimate=light(),
+        out_specs=FAR,
+        scratch_shapes=[
+            pltpu.VMEM((parts.shape[0] // RN, parts.shape[1]), BF16),
+            pltpu.SemaphoreType.DMA((RN,)),
+        ],
+        compiler_params=params(0),
+        cost_estimate=heavy(),
         name="pointwise",
     )(parts, bias.reshape(1, -1), bias_two.reshape(1, -1))
 
 
-def back_kernel(share, where, grads, up, up_two, out, rows):
-    units = up.shape[1]
-
-    @pl.when(pl.program_id(0) == 0)
-    def _():
-        z, x = where[0], where[1]
-        for i, (side, k) in enumerate(BLOCKS):
-            owner = lax.rem(z + k + ZN, ZN) + ZN * (1 - x if side else x)
-            at = pl.multiple_of(owner * share, share)
-            rows[pl.ds(at, share), :] = grads[i * share : (i + 1) * share, :]
-
-    part = dot_t(rows[:, :units], up[...]) + dot_t(rows[:, units:], up_two[...])
-    out[...] = part.astype(BF16)
+def back_kernel(share, where, grads, up, up_two, out, rows, made, sems):
+    width, units = up.shape
+    tile = width // 3
+    z, x = where[0], where[1]
+    loads, sends = [], []
+    for i, (side, k) in enumerate(BLOCKS):
+        owner = lax.rem(z + k + ZN, ZN) + ZN * (1 - x if side else x)
+        at = pl.multiple_of(owner * share, share)
+        source = grads.at[i * share : (i + 1) * share, : 2 * units]
+        loads.append(pltpu.make_async_copy(source, rows.at[pl.ds(at, share), :], sems.at[i]))
+    for copy in loads:
+        copy.start()
+    for copy in loads:
+        copy.wait()
+    for t in range(3):
+        part = slice(t * tile, (t + 1) * tile)
+        product = dot_t(rows[:, :units], up[part, :]) + dot_t(rows[:, units:], up_two[part, :])
+        made[:, part] = product.astype(BF16)
+        sends.append(
+            pltpu.make_async_copy(made.at[:, part], out.at[:, part], sems.at[len(BLOCKS) + t])
+        )
+        sends[-1].start()
+    for copy in sends:
+        copy.wait()
 
 
 def back(where, both, up, up_two, share):
     width, units = up.shape
     count = both.shape[0]
-    tile = width // 3
     return pl.pallas_call(
         functools.partial(back_kernel, share),
-        grid=(3,),
-        out_shape=jax.ShapeDtypeStruct((count, width), BF16),
-        in_specs=[
-            pl.BlockSpec(memory_space=pltpu.SMEM),
-            pl.BlockSpec((count, 2 * units), lambda j: (0, 0)),
-            pl.BlockSpec((tile, units), lambda j: (j, 0)),
-            pl.BlockSpec((tile, units), lambda j: (j, 0)),
+        out_shape=pltpu.HBM((count, width), BF16),
+        in_specs=[pl.BlockSpec(memory_space=pltpu.SMEM), REMAIN, WHOLE, WHOLE],
+        out_specs=FAR,
+        scratch_shapes=[
+            pltpu.VMEM((count, 2 * units), BF16),
+            pltpu.VMEM((count, width), BF16),
+            pltpu.SemaphoreType.DMA((len(BLOCKS) + 3,)),
         ],
-        out_specs=pl.BlockSpec((count, tile), lambda j: (0, j)),
-        scratch_shapes=[pltpu.VMEM((count, 2 * units), BF16)],
-        compiler_params=params(1),
+        compiler_params=params(0),
         cost_estimate=light(),
         name="back",
     )(where, both, up, up_two)
 
 
-def collect_kernel(parts, out):
+def collect_kernel(parts, out, held, sems):
     count = out.shape[0]
-    sums = parts[:count, :].astype(F32)
-    for r in range(1, parts.shape[0] // count):
-        sums += parts[r * count : (r + 1) * count, :].astype(F32)
+    loads = []
+    for r in range(4):
+        at = slice(r * held.shape[0] // 4, (r + 1) * held.shape[0] // 4)
+        loads.append(pltpu.make_async_copy(parts.at[at, :], held.at[at, :], sems.at[r]))
+    for copy in loads:
+        copy.start()
+    sums = jnp.zeros(out.shape, F32)
+    for r in range(held.shape[0] // count):
+        if r * count % (held.shape[0] // 4) == 0:
+            loads[r * count // (held.shape[0] // 4)].wait()
+        sums += held[r * count : (r + 1) * count, :].astype(F32)
     out[...] = sums.astype(BF16)
 
 
@@ -214,8 +239,9 @@
     return pl.pallas_call(
         collect_kernel,
         out_shape=jax.ShapeDtypeStruct((share, parts.shape[1]), BF16),
-        in_specs=[WHOLE],
+        in_specs=[REMAIN],
         out_specs=WHOLE,
+        scratch_shapes=[pltpu.VMEM(parts.shape, BF16), pltpu.SemaphoreType.DMA((4,))],
         compiler_params=params(0),
         cost_estimate=light(),
         name="collect",

time: 133 us -> 121 us (0.910)
  Pallas kernels: 31.7 us -> 21.1 us
  waiting for transfers between devices: 42.2 us -> 47.4 us
  local copies, waits for them, and re-layouts: 9.25 us -> 5.31 us
  other arithmetic: 1.55 us -> 0.09 us
    pallas_call x3, Pallas kernels: 18.8 us -> 10.8 us  [the longest x1 5.82 us: project(): pl.pallas_call(functools.partial(project_kernel, len(pieces), width, unit...]
    all_to_all x1, waiting for transfers between devices: 1.53 us -> 4.83 us  [on_device(): near = lax.all_to_all(near, ('x_lo', 'z'), 0, 0, tiled=True)]
    unnamed x40 -> x16, local copies, waits for them, and re-layouts: 6.89 us -> 5.25 us
    pallas_call x1, Pallas kernels: 1.46 us -> 0.01 us  [pack(): pl.pallas_call(pack_kernel, out_shape=jax.ShapeDtypeStruct((tokens.shape[...]
  transfers between devices with their start and end apart: 20 -> 20, of which waited for: 13 -> 13; matrix products, arithmetic and copies ran while one was open for 3% -> 0% of each run, Pallas kernels for 12% -> 10%
where the time goes in v4:
time: 121 us
  waiting for transfers between devices  47.4 us (39%)
  starting transfers between devices  45.8 us (38%)
  Pallas kernels  21.1 us (17%)
  local copies, waits for them, and re-layouts  5.31 us (4%)
    ppermute x7, starting transfers between devices, shift_z(): return lax.ppermute(x, 'z', [(i, (i + k) % ZN) for i in range(ZN)])  16.9 us
    all_to_all x1, waiting for transfers between devices, on_device(): both = lax.all_to_all(both, ROW, 0, 0, tiled=True)  14.7 us
    all_to_all x1, waiting for transfers between devices, on_device(): parts = lax.all_to_all(parts, ROW, 0, 0, tiled=True)  13.4 us
    ppermute x10, waiting for transfers between devices, swap(): return lax.ppermute(x, axis, [(0, 1), (1, 0)])  9.97 us
    pallas_call x2, Pallas kernels, outer(): pl.pallas_call(functools.partial(outer_kernel, factor), grid=(tiles,), ou...  8.41 us
    ppermute x10, starting transfers between devices, swap(): return lax.ppermute(x, axis, [(0, 1), (1, 0)])  8.31 us
    all_to_all x1, starting transfers between devices, on_device(): parts = lax.all_to_all(parts, ROW, 0, 0, tiled=True)  7.39 us
    all_to_all x1, starting transfers between devices, on_device(): near = lax.all_to_all(near, ('x_lo', 'z'), 0, 0, tiled=True)  7.02 us
  transfers between devices with their start and end apart: 20, of which 13 were waited for; matrix products, arithmetic and copies ran while one was open for 0% of the time, Pallas kernels for 10%

profile of v4, /device:TPU:8, one launch (start us, length us, event | category | flops | bytes accessed | tf_op | source)
XLA Modules:
  0.0 120.7 jit_solution(12919233982116966854)
XLA Ops:
  1.3 1.1 copy-done.5
  3.2 1.6 %collective-permute-start = (bf16[16,3072]{1,0:T(8,128)(2,1)S(1)}, bf16[16,3072]{1,0:T(8,128)(2,1)S(1)}, u32[]{:S(2)}, u32[]{:S(2)}) collective-permute-start(bf16[16,3072]{1,0:T(8,128)(2,1)S(1)} %pack.1.refs_0_), channel_id=1, source_target_pairs={{0,16},{16,0},{1,17},{17,1},{2,18},{18,2},{3,19},{19,3},{4,20},{20... | collective-permute-start | bytes 294920 | tf_op jit(solution)/shard_map/ppermute | solution.py:52
  4.7 3.4 %collective-permute-done.refs_1_ = bf16[16,3072]{1,0:T(8,128)(2,1)S(1)} collective-permute-done((bf16[16,3072]{1,0:T(8,128)(2,1)S(1)}, bf16[16,3072]{1,0:T(8,128)(2,1)S(1)}, u32[]{:S(2)}, u32[]{:S(2)}) %collective-permute-start) | collective-permute-done | bytes 98336 | tf_op jit(solution)/shard_map/ppermute | solution.py:52
  8.2 2.0 %collective-permute-start.1 = (bf16[32,3072]{1,0:T(8,128)(2,1)S(1)}, bf16[32,3072]{1,0:T(8,128)(2,1)S(1)}, u32[]{:S(2)}, u32[]{:S(2)}) collective-permute-start(bf16[32,3072]{1,0:T(8,128)(2,1)S(1)} %pad_maximum_fusion), channel_id=1, source_target_pairs={{0,2},{2,4},{4,6},{6,8},{8,10},{10,12},{12,14},{14,0},{1,3},{3,5},... | collective-permute-start | bytes 589832 | tf_op jit(solution)/shard_map/ppermute | solution.py:48
  10.2 4.0 %collective-permute-start.4 = (bf16[16,3072]{1,0:T(8,128)(2,1)S(1)}, bf16[16,3072]{1,0:T(8,128)(2,1)S(1)}, u32[]{:S(2)}, u32[]{:S(2)}) collective-permute-start(bf16[16,3072]{1,0:T(8,128)(2,1)S(1)} %pack.1.refs_0_), channel_id=1, source_target_pairs={{0,14},{2,0},{4,2},{6,4},{8,6},{10,8},{12,10},{14,12},{1,15},{3,1}... | collective-permute-start | bytes 294920 | tf_op jit(solution)/shard_map/ppermute | solution.py:48
  14.2 2.2 %collective-permute-done.4.refs_5_ = bf16[16,3072]{1,0:T(8,128)(2,1)S(1)} collective-permute-done((bf16[16,3072]{1,0:T(8,128)(2,1)S(1)}, bf16[16,3072]{1,0:T(8,128)(2,1)S(1)}, u32[]{:S(2)}, u32[]{:S(2)}) %collective-permute-start.4) | collective-permute-done | bytes 98336 | tf_op jit(solution)/shard_map/ppermute | solution.py:48
  16.4 3.6 %collective-permute-start.6 = (bf16[16,3072]{1,0:T(8,128)(2,1)S(1)}, bf16[16,3072]{1,0:T(8,128)(2,1)S(1)}, u32[]{:S(2)}, u32[]{:S(2)}) collective-permute-start(bf16[16,3072]{1,0:T(8,128)(2,1)S(1)} %collective-permute-done.4.refs_5_), channel_id=1, source_target_pairs={{0,14},{2,0},{4,2},{6,4},{8,6},{10,8},{12,10},{14,12},{1,15},{3,1}... | collective-permute-start | bytes 294920 | tf_op jit(solution)/shard_map/ppermute | solution.py:48
  20.0 1.5 %collective-permute-start.5 = (bf16[16,3072]{1,0:T(8,128)(2,1)S(1)}, bf16[16,3072]{1,0:T(8,128)(2,1)S(1)}, u32[]{:S(2)}, u32[]{:S(2)}) collective-permute-start(bf16[16,3072]{1,0:T(8,128)(2,1)S(1)} %collective-permute-done.4.refs_5_), channel_id=1, source_target_pairs={{0,16},{16,0},{1,17},{17,1},{2,18},{18,2},{3,19},{19,3},{4,20},{20... | collective-permute-start | bytes 294920 | tf_op jit(solution)/shard_map/ppermute | solution.py:52
  22.3 3.6 %collective-permute-start.8 = (bf16[16,3072]{1,0:T(8,128)(2,1)S(1)}, bf16[16,3072]{1,0:T(8,128)(2,1)S(1)}, u32[]{:S(2)}, u32[]{:S(2)}) collective-permute-start(bf16[16,3072]{1,0:T(8,128)(2,1)S(1)} %collective-permute-done.6.refs_7_), channel_id=1, source_target_pairs={{0,14},{2,0},{4,2},{6,4},{8,6},{10,8},{12,10},{14,12},{1,15},{3,1}... | collective-permute-start | bytes 294920 | tf_op jit(solution)/shard_map/ppermute | solution.py:48
  25.9 1.5 %collective-permute-start.7 = (bf16[16,3072]{1,0:T(8,128)(2,1)S(1)}, bf16[16,3072]{1,0:T(8,128)(2,1)S(1)}, u32[]{:S(2)}, u32[]{:S(2)}) collective-permute-start(bf16[16,3072]{1,0:T(8,128)(2,1)S(1)} %collective-permute-done.6.refs_7_), channel_id=1, source_target_pairs={{0,16},{16,0},{1,17},{17,1},{2,18},{18,2},{3,19},{19,3},{4,20},{20... | collective-permute-start | bytes 294920 | tf_op jit(solution)/shard_map/ppermute | solution.py:52
  27.4 0.9 collective-permute-done.8.refs_9_
  28.3 3.7 %collective-permute-start.10 = (bf16[16,3072]{1,0:T(8,128)(2,1)S(1)}, bf16[16,3072]{1,0:T(8,128)(2,1)S(1)}, u32[]{:S(2)}, u32[]{:S(2)}) collective-permute-start(bf16[16,3072]{1,0:T(8,128)(2,1)S(1)} %collective-permute-done.8.refs_9_), channel_id=1, source_target_pairs={{0,14},{2,0},{4,2},{6,4},{8,6},{10,8},{12,10},{14,12},{1,15},{3,1}... | collective-permute-start | bytes 294920 | tf_op jit(solution)/shard_map/ppermute | solution.py:48
  32.0 1.6 %collective-permute-start.9 = (bf16[16,3072]{1,0:T(8,128)(2,1)S(1)}, bf16[16,3072]{1,0:T(8,128)(2,1)S(1)}, u32[]{:S(2)}, u32[]{:S(2)}) collective-permute-start(bf16[16,3072]{1,0:T(8,128)(2,1)S(1)} %collective-permute-done.8.refs_9_), channel_id=1, source_target_pairs={{0,16},{16,0},{1,17},{17,1},{2,18},{18,2},{3,19},{19,3},{4,20},{20... | collective-permute-start | bytes 294920 | tf_op jit(solution)/shard_map/ppermute | solution.py:52
  34.2 1.5 %collective-permute-start.11 = (bf16[16,3072]{1,0:T(8,128)(2,1)S(1)}, bf16[16,3072]{1,0:T(8,128)(2,1)S(1)}, u32[]{:S(2)}, u32[]{:S(2)}) collective-permute-start(bf16[16,3072]{1,0:T(8,128)(2,1)S(1)} %collective-permute-done.10.refs_11_), channel_id=1, source_target_pairs={{0,16},{16,0},{1,17},{17,1},{2,18},{18,2},{3,19},{19,3},{4,20},{20... | collective-permute-start | bytes 294920 | tf_op jit(solution)/shard_map/ppermute | solution.py:52
  35.7 1.0 collective-permute-done.9.refs_10_
  36.7 2.1 %collective-permute-done.11.refs_12_ = bf16[16,3072]{1,0:T(8,128)(2,1)S(1)} collective-permute-done((bf16[16,3072]{1,0:T(8,128)(2,1)S(1)}, bf16[16,3072]{1,0:T(8,128)(2,1)S(1)}, u32[]{:S(2)}, u32[]{:S(2)}) %collective-permute-start.11) | collective-permute-done | bytes 98336 | tf_op jit(solution)/shard_map/ppermute | solution.py:52
  38.9 5.8 %project.1 = (bf16[256,3072]{1,0:T(8,128)(2,1)}, bf16[256,3072]{1,0:T(8,128)(2,1)S(1)}) custom-call(bf16[16,3072]{1,0:T(8,128)(2,1)S(1)} %pack.1.refs_0_, bf16[16,3072]{1,0:T(8,128)(2,1)S(1)} %collective-permute-done.refs_1_, bf16[32,3072]{1,0:T(8,128)(2,1)S(1)} %collective-permute-done.1.refs_2_, bf16[32,3072]{1,0:T(8,128)(2,1)S(1)} %collective-permute-done.2.refs_3_, ...), custom_call_target="tpu_custom_call" | custom-call | flops 1 | bytes 1 | tf_op jit(solution)/shard_map/project/pallas_call | solution.py:117
  44.7 7.4 %all-to-all-start = ((bf16[8,32,3072]{2,1,0:T(8,128)(2,1)}), bf16[8,32,3072]{2,1,0:T(8,128)(2,1)S(1)}, u32[]{:S(2)}, u32[]{:S(2)}) async-start(bf16[8,32,3072]{2,1,0:T(8,128)(2,1)} %bitcast.14), calls=%async_computation | async-start | bytes 3145728 | tf_op jit(solution)/shard_map/all_to_all | solution.py:301
  52.1 1.1 collective-permute-done.14
  53.3 13.4 %all-to-all-done = bf16[8,32,3072]{2,1,0:T(8,128)(2,1)S(1)} async-done(((bf16[8,32,3072]{2,1,0:T(8,128)(2,1)}), bf16[8,32,3072]{2,1,0:T(8,128)(2,1)S(1)}, u32[]{:S(2)}, u32[]{:S(2)}) %all-to-all-start) | async-done | bytes 1572896 | tf_op jit(solution)/shard_map/all_to_all | solution.py:301
  66.7 1.5 %pointwise.1 = bf16[256,3072]{1,0:T(8,128)(2,1)} custom-call(bf16[256,3072]{1,0:T(8,128)(2,1)S(1)} %bitcast.12, bf16[1,768]{1,0:T(2,128)(2,1)S(1)} %reshape.18.bias, bf16[1,768]{1,0:T(2,128)(2,1)S(1)} %reshape.19.bias_two), custom_call_target="tpu_custom_call" | custom-call | flops 20000000000 | bytes 2000000 | tf_op jit(solution)/shard_map/pointwise/pallas_call | solution.py:162
  68.2 6.2 %all-to-all-start.1 = ((bf16[8,32,3072]{2,1,0:T(8,128)(2,1)}), bf16[8,32,3072]{2,1,0:T(8,128)(2,1)S(1)}, u32[]{:S(2)}, u32[]{:S(2)}) async-start(bf16[8,32,3072]{2,1,0:T(8,128)(2,1)} %bitcast.15), calls=%async_computation.1 | async-start | bytes 3145728 | tf_op jit(solution)/shard_map/all_to_all | solution.py:303
  74.5 14.7 %all-to-all-done.1 = bf16[8,32,3072]{2,1,0:T(8,128)(2,1)S(1)} async-done(((bf16[8,32,3072]{2,1,0:T(8,128)(2,1)}), bf16[8,32,3072]{2,1,0:T(8,128)(2,1)S(1)}, u32[]{:S(2)}, u32[]{:S(2)}) %all-to-all-start.1) | async-done | bytes 1572896 | tf_op jit(solution)/shard_map/all_to_all | solution.py:303
  89.1 1.7 %copy-done.1 = bf16[1536,768]{1,0:T(8,128)(2,1)S(1)} copy-done((bf16[1536,768]{1,0:T(8,128)(2,1)S(1)}, bf16[1536,768]{1,0:T(8,128)(2,1)}, u32[]{:S(2)}) %copy-start.1) | copy-done | bytes 2359320
  90.8 1.7 %copy-done.3 = bf16[1536,768]{1,0:T(8,128)(2,1)S(1)} copy-done((bf16[1536,768]{1,0:T(8,128)(2,1)S(1)}, bf16[1536,768]{1,0:T(8,128)(2,1)}, u32[]{:S(2)}) %copy-start.3) | copy-done | bytes 2359320
  92.4 3.5 %back.1 = bf16[256,1536]{1,0:T(8,128)(2,1)} custom-call(s32[2]{0:T(128)S(1)} %pad_add_fusion.where, bf16[256,3072]{1,0:T(8,128)(2,1)S(1)} %bitcast.8, bf16[1536,768]{1,0:T(8,128)(2,1)S(1)} %copy-done.1, bf16[1536,768]{1,0:T(8,128)(2,1)S(1)} %copy-done.3), custom_call_target="tpu_custom_call" | custom-call | flops 1 | bytes 1 | tf_op jit(solution)/shard_map/back/pallas_call | solution.py:206
  95.9 7.0 %all-to-all-start.2 = ((bf16[16,16,1536]{2,1,0:T(8,128)(2,1)}), bf16[16,16,1536]{2,1,0:T(8,128)(2,1)}, u32[]{:S(2)}, u32[]{:S(2)}) async-start(bf16[16,16,1536]{2,1,0:T(8,128)(2,1)} %bitcast.13), calls=%async_computation.2 | async-start | bytes 1572864 | tf_op jit(solution)/shard_map/all_to_all | solution.py:306
  103.1 2.3 %collective-permute-done.16.right_two.left_two = bf16[256,1536]{1,0:T(8,128)(2,1)S(1)} collective-permute-done((bf16[256,1536]{1,0:T(8,128)(2,1)S(1)}, bf16[256,1536]{1,0:T(8,128)(2,1)S(1)}, u32[]{:S(2)}, u32[]{:S(2)}) %collective-permute-start.16) | collective-permute-done | bytes 786464 | tf_op jit(solution)/shard_map/ppermute | solution.py:52
  105.4 4.2 %outer.3 = bf16[768,1536]{1,0:T(8,128)(2,1)} custom-call(bf16[256,3072]{1,0:T(8,128)(2,1)S(1)} %bitcast.10, bf16[256,1536]{1,0:T(8,128)(2,1)S(1)} %collective-permute-done.16.right_two.left_two, bf16[256,3072]{1,0:T(8,128)(2,1)S(1)} %get-tuple-element.6.left.right, bf16[256,3072]{1,0:T(8,128)(2,1)} %collective-permute-done.15.left_two.right_two), custom_call_target="tpu_custom_call" | custom-call | flops 1 | bytes 1 | tf_op jit(solution)/shard_map/outer/pallas_call | solution.py:268
  109.6 4.2 %outer.2 = bf16[1536,768]{1,0:T(8,128)(2,1)} custom-call(bf16[256,3072]{1,0:T(8,128)(2,1)S(1)} %get-tuple-element.6.left.right, bf16[256,3072]{1,0:T(8,128)(2,1)} %collective-permute-done.15.left_two.right_two, bf16[256,3072]{1,0:T(8,128)(2,1)S(1)} %bitcast.11, bf16[256,1536]{1,0:T(8,128)(2,1)S(1)} %collective-permute-done.16.right_two.left_two), custom_call_target="tpu_custom_call" | custom-call | flops 1 | bytes 1 | tf_op jit(solution)/shard_map/outer/pallas_call | solution.py:268
  113.8 4.8 %all-to-all-done.2 = bf16[16,16,1536]{2,1,0:T(8,128)(2,1)} async-done(((bf16[16,16,1536]{2,1,0:T(8,128)(2,1)}), bf16[16,16,1536]{2,1,0:T(8,128)(2,1)}, u32[]{:S(2)}, u32[]{:S(2)}) %all-to-all-start.2) | async-done | bytes 786464 | tf_op jit(solution)/shard_map/all_to_all | solution.py:306
  118.6 1.9 %collect.1 = bf16[16,1536]{1,0:T(8,128)(2,1)} custom-call(bf16[256,1536]{1,0:T(8,128)(2,1)} %bitcast.7.parts), custom_call_target="tpu_custom_call" | custom-call | flops 1 | bytes 1 | tf_op jit(solution)/shard_map/collect/pallas_call | solution.py:239
  (36 shorter events, 3.1 us)
Async XLA Ops:
  0.6 38.2 %copy-start.4 = (bf16[768,1536]{1,0:T(8,128)(2,1)S(1)}, bf16[768,1536]{1,0:T(8,128)(2,1)}, u32[]{:S(2)}) copy-start(bf16[768,1536]{1,0:T(8,128)(2,1)} %refs_15_.1) | copy-start | bytes 7077892
  0.6 38.2 %copy-start = (bf16[1536,768]{1,0:T(8,128)(2,1)S(1)}, bf16[1536,768]{1,0:T(8,128)(2,1)}, u32[]{:S(2)}) copy-start(bf16[1536,768]{1,0:T(8,128)(2,1)} %up.1) | copy-start | bytes 7077892
  0.7 38.2 %collective-permute-start.13 = (bf16[768,1536]{1,0:T(8,128)(2,1)}, bf16[768,1536]{1,0:T(8,128)(2,1)S(1)}, u32[]{:S(2)}, u32[]{:S(2)}) collective-permute-start(bf16[768,1536]{1,0:T(8,128)(2,1)} %refs_15_.1), channel_id=1, source_target_pairs={{0,1},{1,0},{2,3},{3,2},{4,5},{5,4},{6,7},{7,6},{8,9},{9,8},{10,11... | collective-permute-start | bytes 7077896 | tf_op jit(solution)/shard_map/ppermute | solution.py:52
  0.8 38.1 %collective-permute-start.12 = (bf16[1536,768]{1,0:T(8,128)(2,1)}, bf16[1536,768]{1,0:T(8,128)(2,1)S(1)}, u32[]{:S(2)}, u32[]{:S(2)}) collective-permute-start(bf16[1536,768]{1,0:T(8,128)(2,1)} %up.1), channel_id=1, source_target_pairs={{0,1},{1,0},{2,3},{3,2},{4,5},{5,4},{6,7},{7,6},{8,9},{9,8},{10,11... | collective-permute-start | bytes 7077896 | tf_op jit(solution)/shard_map/ppermute | solution.py:52
  1.2 1.1 copy-start.5
  2.3 0.8 copy-start.6
  3.2 5.0 %collective-permute-start = (bf16[16,3072]{1,0:T(8,128)(2,1)S(1)}, bf16[16,3072]{1,0:T(8,128)(2,1)S(1)}, u32[]{:S(2)}, u32[]{:S(2)}) collective-permute-start(bf16[16,3072]{1,0:T(8,128)(2,1)S(1)} %pack.1.refs_0_), channel_id=1, source_target_pairs={{0,16},{16,0},{1,17},{17,1},{2,18},{18,2},{3,19},{19,3},{4,20},{20... | collective-permute-start | bytes 294920 | tf_op jit(solution)/shard_map/ppermute | solution.py:52
  8.2 11.9 %collective-permute-start.1 = (bf16[32,3072]{1,0:T(8,128)(2,1)S(1)}, bf16[32,3072]{1,0:T(8,128)(2,1)S(1)}, u32[]{:S(2)}, u32[]{:S(2)}) collective-permute-start(bf16[32,3072]{1,0:T(8,128)(2,1)S(1)} %pad_maximum_fusion), channel_id=1, source_target_pairs={{0,2},{2,4},{4,6},{6,8},{8,10},{10,12},{12,14},{14,0},{1,3},{3,5},... | collective-permute-start | bytes 589832 | tf_op jit(solution)/shard_map/ppermute | solution.py:48
  10.2 6.2 %collective-permute-start.4 = (bf16[16,3072]{1,0:T(8,128)(2,1)S(1)}, bf16[16,3072]{1,0:T(8,128)(2,1)S(1)}, u32[]{:S(2)}, u32[]{:S(2)}) collective-permute-start(bf16[16,3072]{1,0:T(8,128)(2,1)S(1)} %pack.1.refs_0_), channel_id=1, source_target_pairs={{0,14},{2,0},{4,2},{6,4},{8,6},{10,8},{12,10},{14,12},{1,15},{3,1}... | collective-permute-start | bytes 294920 | tf_op jit(solution)/shard_map/ppermute | solution.py:48
  16.4 5.8 %collective-permute-start.6 = (bf16[16,3072]{1,0:T(8,128)(2,1)S(1)}, bf16[16,3072]{1,0:T(8,128)(2,1)S(1)}, u32[]{:S(2)}, u32[]{:S(2)}) collective-permute-start(bf16[16,3072]{1,0:T(8,128)(2,1)S(1)} %collective-permute-done.4.refs_5_), channel_id=1, source_target_pairs={{0,14},{2,0},{4,2},{6,4},{8,6},{10,8},{12,10},{14,12},{1,15},{3,1}... | collective-permute-start | bytes 294920 | tf_op jit(solution)/shard_map/ppermute | solution.py:48
  20.0 11.9 %collective-permute-start.2 = (bf16[32,3072]{1,0:T(8,128)(2,1)S(1)}, bf16[32,3072]{1,0:T(8,128)(2,1)S(1)}, u32[]{:S(2)}, u32[]{:S(2)}) collective-permute-start(bf16[32,3072]{1,0:T(8,128)(2,1)S(1)} %collective-permute-done.1.refs_2_), channel_id=1, source_target_pairs={{0,2},{2,4},{4,6},{6,8},{8,10},{10,12},{12,14},{14,0},{1,3},{3,5},... | collective-permute-start | bytes 589832 | tf_op jit(solution)/shard_map/ppermute | solution.py:48
  20.0 5.8 %collective-permute-start.5 = (bf16[16,3072]{1,0:T(8,128)(2,1)S(1)}, bf16[16,3072]{1,0:T(8,128)(2,1)S(1)}, u32[]{:S(2)}, u32[]{:S(2)}) collective-permute-start(bf16[16,3072]{1,0:T(8,128)(2,1)S(1)} %collective-permute-done.4.refs_5_), channel_id=1, source_target_pairs={{0,16},{16,0},{1,17},{17,1},{2,18},{18,2},{3,19},{19,3},{4,20},{20... | collective-permute-start | bytes 294920 | tf_op jit(solution)/shard_map/ppermute | solution.py:52
  22.3 6.0 %collective-permute-start.8 = (bf16[16,3072]{1,0:T(8,128)(2,1)S(1)}, bf16[16,3072]{1,0:T(8,128)(2,1)S(1)}, u32[]{:S(2)}, u32[]{:S(2)}) collective-permute-start(bf16[16,3072]{1,0:T(8,128)(2,1)S(1)} %collective-permute-done.6.refs_7_), channel_id=1, source_target_pairs={{0,14},{2,0},{4,2},{6,4},{8,6},{10,8},{12,10},{14,12},{1,15},{3,1}... | collective-permute-start | bytes 294920 | tf_op jit(solution)/shard_map/ppermute | solution.py:48
  25.9 6.1 %collective-permute-start.7 = (bf16[16,3072]{1,0:T(8,128)(2,1)S(1)}, bf16[16,3072]{1,0:T(8,128)(2,1)S(1)}, u32[]{:S(2)}, u32[]{:S(2)}) collective-permute-start(bf16[16,3072]{1,0:T(8,128)(2,1)S(1)} %collective-permute-done.6.refs_7_), channel_id=1, source_target_pairs={{0,16},{16,0},{1,17},{17,1},{2,18},{18,2},{3,19},{19,3},{4,20},{20... | collective-permute-start | bytes 294920 | tf_op jit(solution)/shard_map/ppermute | solution.py:52
  28.3 5.9 %collective-permute-start.10 = (bf16[16,3072]{1,0:T(8,128)(2,1)S(1)}, bf16[16,3072]{1,0:T(8,128)(2,1)S(1)}, u32[]{:S(2)}, u32[]{:S(2)}) collective-permute-start(bf16[16,3072]{1,0:T(8,128)(2,1)S(1)} %collective-permute-done.8.refs_9_), channel_id=1, source_target_pairs={{0,14},{2,0},{4,2},{6,4},{8,6},{10,8},{12,10},{14,12},{1,15},{3,1}... | collective-permute-start | bytes 294920 | tf_op jit(solution)/shard_map/ppermute | solution.py:48
  32.0 6.9 %collective-permute-start.3 = (bf16[32,3072]{1,0:T(8,128)(2,1)S(1)}, bf16[32,3072]{1,0:T(8,128)(2,1)S(1)}, u32[]{:S(2)}, u32[]{:S(2)}) collective-permute-start(bf16[32,3072]{1,0:T(8,128)(2,1)S(1)} %collective-permute-done.2.refs_3_), channel_id=1, source_target_pairs={{0,2},{2,4},{4,6},{6,8},{8,10},{10,12},{12,14},{14,0},{1,3},{3,5},... | collective-permute-start | bytes 589832 | tf_op jit(solution)/shard_map/ppermute | solution.py:48
  32.0 4.7 %collective-permute-start.9 = (bf16[16,3072]{1,0:T(8,128)(2,1)S(1)}, bf16[16,3072]{1,0:T(8,128)(2,1)S(1)}, u32[]{:S(2)}, u32[]{:S(2)}) collective-permute-start(bf16[16,3072]{1,0:T(8,128)(2,1)S(1)} %collective-permute-done.8.refs_9_), channel_id=1, source_target_pairs={{0,16},{16,0},{1,17},{17,1},{2,18},{18,2},{3,19},{19,3},{4,20},{20... | collective-permute-start | bytes 294920 | tf_op jit(solution)/shard_map/ppermute | solution.py:52
  34.2 4.6 %collective-permute-start.11 = (bf16[16,3072]{1,0:T(8,128)(2,1)S(1)}, bf16[16,3072]{1,0:T(8,128)(2,1)S(1)}, u32[]{:S(2)}, u32[]{:S(2)}) collective-permute-start(bf16[16,3072]{1,0:T(8,128)(2,1)S(1)} %collective-permute-done.10.refs_11_), channel_id=1, source_target_pairs={{0,16},{16,0},{1,17},{17,1},{2,18},{18,2},{3,19},{19,3},{4,20},{20... | collective-permute-start | bytes 294920 | tf_op jit(solution)/shard_map/ppermute | solution.py:52
  38.9 5.8 %copy-start.2 = (bf16[1536,768]{1,0:T(8,128)(2,1)}, bf16[1536,768]{1,0:T(8,128)(2,1)S(1)}, u32[]{:S(2)}) copy-start(bf16[1536,768]{1,0:T(8,128)(2,1)S(1)} %collective-permute-done.12.refs_14_.up_two) | copy-start | bytes 7077892
  44.7 7.4 %copy-start.7 = (bf16[768]{0:T(1024)(128)(2,1)S(1)}, bf16[768]{0:T(1024)(128)(2,1)}, u32[]{:S(2)}) copy-start(bf16[768]{0:T(1024)(128)(2,1)} %param.7) | copy-start | bytes 4612
  44.7 22.0 %all-to-all-start = ((bf16[8,32,3072]{2,1,0:T(8,128)(2,1)}), bf16[8,32,3072]{2,1,0:T(8,128)(2,1)S(1)}, u32[]{:S(2)}, u32[]{:S(2)}) async-start(bf16[8,32,3072]{2,1,0:T(8,128)(2,1)} %bitcast.14), calls=%async_computation | async-start | bytes 3145728 | tf_op jit(solution)/shard_map/all_to_all | solution.py:301
  52.1 1.2 collective-permute-start.14
  68.2 20.9 %all-to-all-start.1 = ((bf16[8,32,3072]{2,1,0:T(8,128)(2,1)}), bf16[8,32,3072]{2,1,0:T(8,128)(2,1)S(1)}, u32[]{:S(2)}, u32[]{:S(2)}) async-start(bf16[8,32,3072]{2,1,0:T(8,128)(2,1)} %bitcast.15), calls=%async_computation.1 | async-start | bytes 3145728 | tf_op jit(solution)/shard_map/all_to_all | solution.py:303
  74.4 28.7 %collective-permute-start.15 = (bf16[256,3072]{1,0:T(8,128)(2,1)S(1)}, bf16[256,3072]{1,0:T(8,128)(2,1)}, u32[]{:S(2)}, u32[]{:S(2)}) collective-permute-start(bf16[256,3072]{1,0:T(8,128)(2,1)S(1)} %get-tuple-element.6.left.right), channel_id=1, source_target_pairs={{0,1},{1,0},{2,3},{3,2},{4,5},{5,4},{6,7},{7,6},{8,9},{9,8},{10,11... | collective-permute-start | bytes 4718600 | tf_op jit(solution)/shard_map/ppermute | solution.py:52
  89.1 1.7 %copy-start.1 = (bf16[1536,768]{1,0:T(8,128)(2,1)S(1)}, bf16[1536,768]{1,0:T(8,128)(2,1)}, u32[]{:S(2)}) copy-start(bf16[1536,768]{1,0:T(8,128)(2,1)} %up.1) | copy-start | bytes 7077892
  90.8 1.7 %copy-start.3 = (bf16[1536,768]{1,0:T(8,128)(2,1)S(1)}, bf16[1536,768]{1,0:T(8,128)(2,1)}, u32[]{:S(2)}) copy-start(bf16[1536,768]{1,0:T(8,128)(2,1)} %copy-done.2) | copy-start | bytes 7077892
  95.9 22.7 %all-to-all-start.2 = ((bf16[16,16,1536]{2,1,0:T(8,128)(2,1)}), bf16[16,16,1536]{2,1,0:T(8,128)(2,1)}, u32[]{:S(2)}, u32[]{:S(2)}) async-start(bf16[16,16,1536]{2,1,0:T(8,128)(2,1)} %bitcast.13), calls=%async_computation.2 | async-start | bytes 1572864 | tf_op jit(solution)/shard_map/all_to_all | solution.py:306
  103.0 2.4 %collective-permute-start.16 = (bf16[256,1536]{1,0:T(8,128)(2,1)S(1)}, bf16[256,1536]{1,0:T(8,128)(2,1)S(1)}, u32[]{:S(2)}, u32[]{:S(2)}) collective-permute-start(bf16[256,1536]{1,0:T(8,128)(2,1)S(1)} %slice.4), channel_id=1, source_target_pairs={{0,1},{1,0},{2,3},{3,2},{4,5},{5,4},{6,7},{7,6},{8,9},{9,8},{10,11... | collective-permute-start | bytes 2359304 | tf_op jit(solution)/shard_map/ppermute | solution.py:52

commit v5 on v4

--- a/solution.py
+++ b/solution.py
@@ -20,6 +20,14 @@
 FAR = pl.BlockSpec(memory_space=pltpu.HBM)
 
 
+def in_hbm(x):
+    return pltpu.with_memory_space_constraint(x, pltpu.HBM)
+
+
+def in_vmem(x):
+    return pltpu.with_memory_space_constraint(x, pltpu.VMEM)
+
+
 def light():
     return pl.CostEstimate(flops=1, bytes_accessed=1, transcendentals=0)
 
@@ -64,22 +72,29 @@
     return lax.dot_general(a, b, (((0,), (0,)), ((), ())), preferred_element_type=F32)
 
 
-def pack_kernel(tokens, cotangent, out):
+def pack_kernel(tokens, cotangent, out, sems):
     width = tokens.shape[1]
-    out[:, :width] = tokens[...]
-    out[:, width:] = cotangent[...]
+    copies = [
+        pltpu.make_async_copy(tokens, out.at[:, :width], sems.at[0]),
+        pltpu.make_async_copy(cotangent, out.at[:, width:], sems.at[1]),
+    ]
+    for copy in copies:
+        copy.start()
+    for copy in copies:
+        copy.wait()
 
 
 def pack(tokens, cotangent):
     return pl.pallas_call(
         pack_kernel,
         out_shape=jax.ShapeDtypeStruct((tokens.shape[0], 2 * tokens.shape[1]), BF16),
-        in_specs=[WHOLE] * 2,
-        out_specs=WHOLE,
+        in_specs=[FAR] * 2,
+        out_specs=REMAIN,
+        scratch_shapes=[pltpu.SemaphoreType.DMA((2,))],
         compiler_params=params(0),
         cost_estimate=heavy(),
         name="pack",
-    )(tokens, cotangent)
+    )(in_hbm(tokens), in_hbm(cotangent))
 
 
 def project_kernel(pieces, width, units, *refs):
@@ -94,8 +109,11 @@
         copy.start()
     for copy in loads:
         copy.wait()
-    sends = [pltpu.make_async_copy(rows, kept, sems.at[pieces])]
-    sends[0].start()
+    sends = [
+        pltpu.make_async_copy(rows, kept, sems.at[pieces]),
+    ]
+    for copy in sends:
+        copy.start()
     for k, weight in enumerate(weights):
         at = slice(k * units, (k + 1) * units)
         if k < 2:
@@ -174,26 +192,33 @@
     )(parts, bias.reshape(1, -1), bias_two.reshape(1, -1))
 
 
-def back_kernel(share, where, grads, up, up_two, out, rows, made, sems):
+def back_kernel(share, where, grads, up, up_two, out, rows, held, total, made, sems):
     width, units = up.shape
     tile = width // 3
+    parts = [slice(t * tile, (t + 1) * tile) for t in range(3)]
     z, x = where[0], where[1]
-    loads, sends = [], []
+    first = len(BLOCKS)
+    loads, fetches, sends = [], [], []
     for i, (side, k) in enumerate(BLOCKS):
         owner = lax.rem(z + k + ZN, ZN) + ZN * (1 - x if side else x)
         at = pl.multiple_of(owner * share, share)
         source = grads.at[i * share : (i + 1) * share, : 2 * units]
         loads.append(pltpu.make_async_copy(source, rows.at[pl.ds(at, share), :], sems.at[i]))
+    for t, part in enumerate(parts):
+        fetches.append(
+            pltpu.make_async_copy(up_two.at[part, :], held.at[part, :], sems.at[first + t])
+        )
+    for copy in loads + fetches:
+        copy.start()
     for copy in loads:
-        copy.start()
-    for copy in loads:
-        copy.wait()
-    for t in range(3):
-        part = slice(t * tile, (t + 1) * tile)
-        product = dot_t(rows[:, :units], up[part, :]) + dot_t(rows[:, units:], up_two[part, :])
-        made[:, part] = product.astype(BF16)
+        copy.wait()
+    for part in parts:
+        total[:, part] = dot_t(rows[:, :units], up[part, :])
+    for t, part in enumerate(parts):
+        fetches[t].wait()
+        made[:, part] = (total[:, part] + dot_t(rows[:, units:], held[part, :])).astype(BF16)
         sends.append(
-            pltpu.make_async_copy(made.at[:, part], out.at[:, part], sems.at[len(BLOCKS) + t])
+            pltpu.make_async_copy(made.at[:, part], out.at[:, part], sems.at[first + 3 + t])
         )
         sends[-1].start()
     for copy in sends:
@@ -206,17 +231,19 @@
     return pl.pallas_call(
         functools.partial(back_kernel, share),
         out_shape=pltpu.HBM((count, width), BF16),
-        in_specs=[pl.BlockSpec(memory_space=pltpu.SMEM), REMAIN, WHOLE, WHOLE],
+        in_specs=[pl.BlockSpec(memory_space=pltpu.SMEM), REMAIN, WHOLE, FAR],
         out_specs=FAR,
         scratch_shapes=[
             pltpu.VMEM((count, 2 * units), BF16),
+            pltpu.VMEM(up.shape, BF16),
+            pltpu.VMEM((count, width), F32),
             pltpu.VMEM((count, width), BF16),
-            pltpu.SemaphoreType.DMA((len(BLOCKS) + 3,)),
+            pltpu.SemaphoreType.DMA((len(BLOCKS) + 6,)),
         ],
         compiler_params=params(0),
         cost_estimate=light(),
         name="back",
-    )(where, both, up, up_two)
+    )(where, both, up, in_hbm(up_two))
 
 
 def collect_kernel(parts, out, held, sems):
@@ -284,7 +311,6 @@
 
     held = pack(tokens, cotangent)
     across = swap(held, "x_lo")
-    pieces = [held, across]
     forward = jnp.concatenate([held, across], axis=0)
     backward = held
     fore, aft = [], []
@@ -294,7 +320,7 @@
             forward = shift_z(forward, 1)
             fore.append(forward)
         aft += [backward, swap(backward, "x_lo")]
-    pieces += fore + aft
+    pieces = [held, across] + fore + aft
 
     up_two, down_two, bias_two = (swap(w, "core") for w in (up_weight, down_weight, up_bias))
     parts, rows = project(pieces, up_weight, up_two, down_weight, down_two)

time: 121 us -> 120 us (level)
  local copies, waits for them, and re-layouts: 5.31 us -> 1.75 us
  Pallas kernels: 21.1 us -> 23.2 us
    unnamed x16 -> x10, local copies, waits for them, and re-layouts: 5.25 us -> 1.69 us
  transfers between devices with their start and end apart: 20 -> 20, of which waited for: 13 -> 13; matrix products, arithmetic and copies ran while one was open for 0% -> 0% of each run, Pallas kernels for 10% -> 12%
where the time goes in v5:
time: 120 us; the launch traced here: 119 us
  waiting for transfers between devices  47.4 us (40%)
  starting transfers between devices  45.9 us (38%)
  Pallas kernels  23.2 us (19%)
  local copies, waits for them, and re-layouts  1.75 us (1%)
    ppermute x7, starting transfers between devices, shift_z(): return lax.ppermute(x, 'z', [(i, (i + k) % ZN) for i in range(ZN)])  16.9 us
    all_to_all x1, waiting for transfers between devices, on_device(): both = lax.all_to_all(both, ROW, 0, 0, tiled=True)  14.7 us
    all_to_all x1, waiting for transfers between devices, on_device(): parts = lax.all_to_all(parts, ROW, 0, 0, tiled=True)  13.4 us
    ppermute x10, waiting for transfers between devices, swap(): return lax.ppermute(x, axis, [(0, 1), (1, 0)])  9.98 us
    pallas_call x2, Pallas kernels, outer(): pl.pallas_call(functools.partial(outer_kernel, factor), grid=(tiles,), ou...  8.42 us
    ppermute x10, starting transfers between devices, swap(): return lax.ppermute(x, axis, [(0, 1), (1, 0)])  8.32 us
    all_to_all x1, starting transfers between devices, on_device(): parts = lax.all_to_all(parts, ROW, 0, 0, tiled=True)  7.39 us
    all_to_all x1, starting transfers between devices, on_device(): near = lax.all_to_all(near, ('x_lo', 'z'), 0, 0, tiled=True)  7.03 us
  transfers between devices with their start and end apart: 20, of which 13 were waited for; matrix products, arithmetic and copies ran while one was open for 0% of the time, Pallas kernels for 12%

profile of v5, /device:TPU:8, one launch (start us, length us, event | category | flops | bytes accessed | tf_op | source)
XLA Modules:
  0.0 119.2 jit_solution(9883586042464962238)
XLA Ops:
  1.2 1.1 pack.1.refs_0_
  2.4 1.6 %collective-permute-start = (bf16[16,3072]{1,0:T(8,128)(2,1)S(1)}, bf16[16,3072]{1,0:T(8,128)(2,1)S(1)}, u32[]{:S(2)}, u32[]{:S(2)}) collective-permute-start(bf16[16,3072]{1,0:T(8,128)(2,1)S(1)} %pack.1.refs_0_), channel_id=1, source_target_pairs={{0,16},{16,0},{1,17},{17,1},{2,18},{18,2},{3,19},{19,3},{4,20},{20... | collective-permute-start | bytes 294920 | tf_op jit(solution)/shard_map/ppermute | solution.py:60
  4.0 3.4 %collective-permute-done.refs_1_ = bf16[16,3072]{1,0:T(8,128)(2,1)S(1)} collective-permute-done((bf16[16,3072]{1,0:T(8,128)(2,1)S(1)}, bf16[16,3072]{1,0:T(8,128)(2,1)S(1)}, u32[]{:S(2)}, u32[]{:S(2)}) %collective-permute-start) | collective-permute-done | bytes 98336 | tf_op jit(solution)/shard_map/ppermute | solution.py:60
  7.4 2.0 %collective-permute-start.1 = (bf16[32,3072]{1,0:T(8,128)(2,1)S(1)}, bf16[32,3072]{1,0:T(8,128)(2,1)S(1)}, u32[]{:S(2)}, u32[]{:S(2)}) collective-permute-start(bf16[32,3072]{1,0:T(8,128)(2,1)S(1)} %pad_maximum_fusion), channel_id=1, source_target_pairs={{0,2},{2,4},{4,6},{6,8},{8,10},{10,12},{12,14},{14,0},{1,3},{3,5},... | collective-permute-start | bytes 589832 | tf_op jit(solution)/shard_map/ppermute | solution.py:56
  9.4 4.0 %collective-permute-start.4 = (bf16[16,3072]{1,0:T(8,128)(2,1)S(1)}, bf16[16,3072]{1,0:T(8,128)(2,1)S(1)}, u32[]{:S(2)}, u32[]{:S(2)}) collective-permute-start(bf16[16,3072]{1,0:T(8,128)(2,1)S(1)} %pack.1.refs_0_), channel_id=1, source_target_pairs={{0,14},{2,0},{4,2},{6,4},{8,6},{10,8},{12,10},{14,12},{1,15},{3,1}... | collective-permute-start | bytes 294920 | tf_op jit(solution)/shard_map/ppermute | solution.py:56
  13.5 2.2 %collective-permute-done.4.refs_5_ = bf16[16,3072]{1,0:T(8,128)(2,1)S(1)} collective-permute-done((bf16[16,3072]{1,0:T(8,128)(2,1)S(1)}, bf16[16,3072]{1,0:T(8,128)(2,1)S(1)}, u32[]{:S(2)}, u32[]{:S(2)}) %collective-permute-start.4) | collective-permute-done | bytes 98336 | tf_op jit(solution)/shard_map/ppermute | solution.py:56
  15.7 3.6 %collective-permute-start.6 = (bf16[16,3072]{1,0:T(8,128)(2,1)S(1)}, bf16[16,3072]{1,0:T(8,128)(2,1)S(1)}, u32[]{:S(2)}, u32[]{:S(2)}) collective-permute-start(bf16[16,3072]{1,0:T(8,128)(2,1)S(1)} %collective-permute-done.4.refs_5_), channel_id=1, source_target_pairs={{0,14},{2,0},{4,2},{6,4},{8,6},{10,8},{12,10},{14,12},{1,15},{3,1}... | collective-permute-start | bytes 294920 | tf_op jit(solution)/shard_map/ppermute | solution.py:56
  19.3 1.5 %collective-permute-start.5 = (bf16[16,3072]{1,0:T(8,128)(2,1)S(1)}, bf16[16,3072]{1,0:T(8,128)(2,1)S(1)}, u32[]{:S(2)}, u32[]{:S(2)}) collective-permute-start(bf16[16,3072]{1,0:T(8,128)(2,1)S(1)} %collective-permute-done.4.refs_5_), channel_id=1, source_target_pairs={{0,16},{16,0},{1,17},{17,1},{2,18},{18,2},{3,19},{19,3},{4,20},{20... | collective-permute-start | bytes 294920 | tf_op jit(solution)/shard_map/ppermute | solution.py:60
  20.8 0.7 collective-permute-done.6.refs_7_
  21.5 3.6 %collective-permute-start.8 = (bf16[16,3072]{1,0:T(8,128)(2,1)S(1)}, bf16[16,3072]{1,0:T(8,128)(2,1)S(1)}, u32[]{:S(2)}, u32[]{:S(2)}) collective-permute-start(bf16[16,3072]{1,0:T(8,128)(2,1)S(1)} %collective-permute-done.6.refs_7_), channel_id=1, source_target_pairs={{0,14},{2,0},{4,2},{6,4},{8,6},{10,8},{12,10},{14,12},{1,15},{3,1}... | collective-permute-start | bytes 294920 | tf_op jit(solution)/shard_map/ppermute | solution.py:56
  25.1 1.5 %collective-permute-start.7 = (bf16[16,3072]{1,0:T(8,128)(2,1)S(1)}, bf16[16,3072]{1,0:T(8,128)(2,1)S(1)}, u32[]{:S(2)}, u32[]{:S(2)}) collective-permute-start(bf16[16,3072]{1,0:T(8,128)(2,1)S(1)} %collective-permute-done.6.refs_7_), channel_id=1, source_target_pairs={{0,16},{16,0},{1,17},{17,1},{2,18},{18,2},{3,19},{19,3},{4,20},{20... | collective-permute-start | bytes 294920 | tf_op jit(solution)/shard_map/ppermute | solution.py:60
  26.6 0.9 collective-permute-done.8.refs_9_
  27.5 3.7 %collective-permute-start.10 = (bf16[16,3072]{1,0:T(8,128)(2,1)S(1)}, bf16[16,3072]{1,0:T(8,128)(2,1)S(1)}, u32[]{:S(2)}, u32[]{:S(2)}) collective-permute-start(bf16[16,3072]{1,0:T(8,128)(2,1)S(1)} %collective-permute-done.8.refs_9_), channel_id=1, source_target_pairs={{0,14},{2,0},{4,2},{6,4},{8,6},{10,8},{12,10},{14,12},{1,15},{3,1}... | collective-permute-start | bytes 294920 | tf_op jit(solution)/shard_map/ppermute | solution.py:56
  31.2 1.6 %collective-permute-start.9 = (bf16[16,3072]{1,0:T(8,128)(2,1)S(1)}, bf16[16,3072]{1,0:T(8,128)(2,1)S(1)}, u32[]{:S(2)}, u32[]{:S(2)}) collective-permute-start(bf16[16,3072]{1,0:T(8,128)(2,1)S(1)} %collective-permute-done.8.refs_9_), channel_id=1, source_target_pairs={{0,16},{16,0},{1,17},{17,1},{2,18},{18,2},{3,19},{19,3},{4,20},{20... | collective-permute-start | bytes 294920 | tf_op jit(solution)/shard_map/ppermute | solution.py:60
  33.4 1.5 %collective-permute-start.11 = (bf16[16,3072]{1,0:T(8,128)(2,1)S(1)}, bf16[16,3072]{1,0:T(8,128)(2,1)S(1)}, u32[]{:S(2)}, u32[]{:S(2)}) collective-permute-start(bf16[16,3072]{1,0:T(8,128)(2,1)S(1)} %collective-permute-done.10.refs_11_), channel_id=1, source_target_pairs={{0,16},{16,0},{1,17},{17,1},{2,18},{18,2},{3,19},{19,3},{4,20},{20... | collective-permute-start | bytes 294920 | tf_op jit(solution)/shard_map/ppermute | solution.py:60
  34.9 1.0 collective-permute-done.9.refs_10_
  35.9 2.1 %collective-permute-done.11.refs_12_ = bf16[16,3072]{1,0:T(8,128)(2,1)S(1)} collective-permute-done((bf16[16,3072]{1,0:T(8,128)(2,1)S(1)}, bf16[16,3072]{1,0:T(8,128)(2,1)S(1)}, u32[]{:S(2)}, u32[]{:S(2)}) %collective-permute-start.11) | collective-permute-done | bytes 98336 | tf_op jit(solution)/shard_map/ppermute | solution.py:60
  38.1 5.8 %project.1 = (bf16[256,3072]{1,0:T(8,128)(2,1)}, bf16[256,3072]{1,0:T(8,128)(2,1)S(1)}) custom-call(bf16[16,3072]{1,0:T(8,128)(2,1)S(1)} %pack.1.refs_0_, bf16[16,3072]{1,0:T(8,128)(2,1)S(1)} %collective-permute-done.refs_1_, bf16[32,3072]{1,0:T(8,128)(2,1)S(1)} %collective-permute-done.1.refs_2_, bf16[32,3072]{1,0:T(8,128)(2,1)S(1)} %collective-permute-done.2.refs_3_, ...), custom_call_target="tpu_custom_call" | custom-call | flops 1 | bytes 1 | tf_op jit(solution)/shard_map/project/pallas_call | solution.py:135
  44.0 7.4 %all-to-all-start = ((bf16[8,32,3072]{2,1,0:T(8,128)(2,1)}), bf16[8,32,3072]{2,1,0:T(8,128)(2,1)S(1)}, u32[]{:S(2)}, u32[]{:S(2)}) async-start(bf16[8,32,3072]{2,1,0:T(8,128)(2,1)} %bitcast.14), calls=%async_computation | async-start | bytes 3145728 | tf_op jit(solution)/shard_map/all_to_all | solution.py:327
  51.4 1.1 collective-permute-done.14
  52.5 13.4 %all-to-all-done = bf16[8,32,3072]{2,1,0:T(8,128)(2,1)S(1)} async-done(((bf16[8,32,3072]{2,1,0:T(8,128)(2,1)}), bf16[8,32,3072]{2,1,0:T(8,128)(2,1)S(1)}, u32[]{:S(2)}, u32[]{:S(2)}) %all-to-all-start) | async-done | bytes 1572896 | tf_op jit(solution)/shard_map/all_to_all | solution.py:327
  65.9 1.5 %pointwise.1 = bf16[256,3072]{1,0:T(8,128)(2,1)} custom-call(bf16[256,3072]{1,0:T(8,128)(2,1)S(1)} %bitcast.12, bf16[1,768]{1,0:T(2,128)(2,1)S(1)} %reshape.18.bias, bf16[1,768]{1,0:T(2,128)(2,1)S(1)} %reshape.19.bias_two), custom_call_target="tpu_custom_call" | custom-call | flops 20000000000 | bytes 2000000 | tf_op jit(solution)/shard_map/pointwise/pallas_call | solution.py:180
  67.5 6.2 %all-to-all-start.1 = ((bf16[8,32,3072]{2,1,0:T(8,128)(2,1)}), bf16[8,32,3072]{2,1,0:T(8,128)(2,1)S(1)}, u32[]{:S(2)}, u32[]{:S(2)}) async-start(bf16[8,32,3072]{2,1,0:T(8,128)(2,1)} %bitcast.15), calls=%async_computation.1 | async-start | bytes 3145728 | tf_op jit(solution)/shard_map/all_to_all | solution.py:329
  73.7 14.7 %all-to-all-done.1 = bf16[8,32,3072]{2,1,0:T(8,128)(2,1)S(1)} async-done(((bf16[8,32,3072]{2,1,0:T(8,128)(2,1)}), bf16[8,32,3072]{2,1,0:T(8,128)(2,1)S(1)}, u32[]{:S(2)}, u32[]{:S(2)}) %all-to-all-start.1) | async-done | bytes 1572896 | tf_op jit(solution)/shard_map/all_to_all | solution.py:329
  88.4 1.7 %copy-done.1 = bf16[1536,768]{1,0:T(8,128)(2,1)S(1)} copy-done((bf16[1536,768]{1,0:T(8,128)(2,1)S(1)}, bf16[1536,768]{1,0:T(8,128)(2,1)}, u32[]{:S(2)}) %copy-start.1) | copy-done | bytes 2359320
  90.0 4.4 %back.1 = bf16[256,1536]{1,0:T(8,128)(2,1)} custom-call(s32[2]{0:T(128)S(1)} %pad_add_fusion.where, bf16[256,3072]{1,0:T(8,128)(2,1)S(1)} %bitcast.8, bf16[1536,768]{1,0:T(8,128)(2,1)S(1)} %copy-done.1, bf16[1536,768]{1,0:T(8,128)(2,1)} %copy-done.2), custom_call_target="tpu_custom_call" | custom-call | flops 1 | bytes 1 | tf_op jit(solution)/shard_map/back/pallas_call | solution.py:231
  94.4 7.0 %all-to-all-start.2 = ((bf16[16,16,1536]{2,1,0:T(8,128)(2,1)}), bf16[16,16,1536]{2,1,0:T(8,128)(2,1)}, u32[]{:S(2)}, u32[]{:S(2)}) async-start(bf16[16,16,1536]{2,1,0:T(8,128)(2,1)} %bitcast.13), calls=%async_computation.2 | async-start | bytes 1572864 | tf_op jit(solution)/shard_map/all_to_all | solution.py:332
  101.6 2.3 %collective-permute-done.16.right_two.left_two = bf16[256,1536]{1,0:T(8,128)(2,1)S(1)} collective-permute-done((bf16[256,1536]{1,0:T(8,128)(2,1)S(1)}, bf16[256,1536]{1,0:T(8,128)(2,1)S(1)}, u32[]{:S(2)}, u32[]{:S(2)}) %collective-permute-start.16) | collective-permute-done | bytes 786464 | tf_op jit(solution)/shard_map/ppermute | solution.py:60
  103.9 4.2 %outer.3 = bf16[768,1536]{1,0:T(8,128)(2,1)} custom-call(bf16[256,3072]{1,0:T(8,128)(2,1)S(1)} %bitcast.10, bf16[256,1536]{1,0:T(8,128)(2,1)S(1)} %collective-permute-done.16.right_two.left_two, bf16[256,3072]{1,0:T(8,128)(2,1)S(1)} %get-tuple-element.6.left.right, bf16[256,3072]{1,0:T(8,128)(2,1)} %collective-permute-done.15.left_two.right_two), custom_call_target="tpu_custom_call" | custom-call | flops 1 | bytes 1 | tf_op jit(solution)/shard_map/outer/pallas_call | solution.py:295
  108.1 4.2 %outer.2 = bf16[1536,768]{1,0:T(8,128)(2,1)} custom-call(bf16[256,3072]{1,0:T(8,128)(2,1)S(1)} %get-tuple-element.6.left.right, bf16[256,3072]{1,0:T(8,128)(2,1)} %collective-permute-done.15.left_two.right_two, bf16[256,3072]{1,0:T(8,128)(2,1)S(1)} %bitcast.11, bf16[256,1536]{1,0:T(8,128)(2,1)S(1)} %collective-permute-done.16.right_two.left_two), custom_call_target="tpu_custom_call" | custom-call | flops 1 | bytes 1 | tf_op jit(solution)/shard_map/outer/pallas_call | solution.py:295
  112.3 4.8 %all-to-all-done.2 = bf16[16,16,1536]{2,1,0:T(8,128)(2,1)} async-done(((bf16[16,16,1536]{2,1,0:T(8,128)(2,1)}), bf16[16,16,1536]{2,1,0:T(8,128)(2,1)}, u32[]{:S(2)}, u32[]{:S(2)}) %all-to-all-start.2) | async-done | bytes 786464 | tf_op jit(solution)/shard_map/all_to_all | solution.py:332
  117.2 1.9 %collect.1 = bf16[16,1536]{1,0:T(8,128)(2,1)} custom-call(bf16[256,1536]{1,0:T(8,128)(2,1)} %bitcast.7.parts), custom_call_target="tpu_custom_call" | custom-call | flops 1 | bytes 1 | tf_op jit(solution)/shard_map/collect/pallas_call | solution.py:266
  (30 shorter events, 1.6 us)
Async XLA Ops:
  0.6 37.5 %copy-start.3 = (bf16[768,1536]{1,0:T(8,128)(2,1)S(1)}, bf16[768,1536]{1,0:T(8,128)(2,1)}, u32[]{:S(2)}) copy-start(bf16[768,1536]{1,0:T(8,128)(2,1)} %refs_15_.1) | copy-start | bytes 7077892
  0.6 37.5 %copy-start = (bf16[1536,768]{1,0:T(8,128)(2,1)S(1)}, bf16[1536,768]{1,0:T(8,128)(2,1)}, u32[]{:S(2)}) copy-start(bf16[1536,768]{1,0:T(8,128)(2,1)} %up.1) | copy-start | bytes 7077892
  0.7 37.4 %collective-permute-start.13 = (bf16[768,1536]{1,0:T(8,128)(2,1)}, bf16[768,1536]{1,0:T(8,128)(2,1)S(1)}, u32[]{:S(2)}, u32[]{:S(2)}) collective-permute-start(bf16[768,1536]{1,0:T(8,128)(2,1)} %refs_15_.1), channel_id=1, source_target_pairs={{0,1},{1,0},{2,3},{3,2},{4,5},{5,4},{6,7},{7,6},{8,9},{9,8},{10,11... | collective-permute-start | bytes 7077896 | tf_op jit(solution)/shard_map/ppermute | solution.py:60
  0.8 37.3 %collective-permute-start.12 = (bf16[1536,768]{1,0:T(8,128)(2,1)}, bf16[1536,768]{1,0:T(8,128)(2,1)S(1)}, u32[]{:S(2)}, u32[]{:S(2)}) collective-permute-start(bf16[1536,768]{1,0:T(8,128)(2,1)} %up.1), channel_id=1, source_target_pairs={{0,1},{1,0},{2,3},{3,2},{4,5},{5,4},{6,7},{7,6},{8,9},{9,8},{10,11... | collective-permute-start | bytes 7077896 | tf_op jit(solution)/shard_map/ppermute | solution.py:60
  2.4 5.0 %collective-permute-start = (bf16[16,3072]{1,0:T(8,128)(2,1)S(1)}, bf16[16,3072]{1,0:T(8,128)(2,1)S(1)}, u32[]{:S(2)}, u32[]{:S(2)}) collective-permute-start(bf16[16,3072]{1,0:T(8,128)(2,1)S(1)} %pack.1.refs_0_), channel_id=1, source_target_pairs={{0,16},{16,0},{1,17},{17,1},{2,18},{18,2},{3,19},{19,3},{4,20},{20... | collective-permute-start | bytes 294920 | tf_op jit(solution)/shard_map/ppermute | solution.py:60
  7.4 11.9 %collective-permute-start.1 = (bf16[32,3072]{1,0:T(8,128)(2,1)S(1)}, bf16[32,3072]{1,0:T(8,128)(2,1)S(1)}, u32[]{:S(2)}, u32[]{:S(2)}) collective-permute-start(bf16[32,3072]{1,0:T(8,128)(2,1)S(1)} %pad_maximum_fusion), channel_id=1, source_target_pairs={{0,2},{2,4},{4,6},{6,8},{8,10},{10,12},{12,14},{14,0},{1,3},{3,5},... | collective-permute-start | bytes 589832 | tf_op jit(solution)/shard_map/ppermute | solution.py:56
  9.4 6.2 %collective-permute-start.4 = (bf16[16,3072]{1,0:T(8,128)(2,1)S(1)}, bf16[16,3072]{1,0:T(8,128)(2,1)S(1)}, u32[]{:S(2)}, u32[]{:S(2)}) collective-permute-start(bf16[16,3072]{1,0:T(8,128)(2,1)S(1)} %pack.1.refs_0_), channel_id=1, source_target_pairs={{0,14},{2,0},{4,2},{6,4},{8,6},{10,8},{12,10},{14,12},{1,15},{3,1}... | collective-permute-start | bytes 294920 | tf_op jit(solution)/shard_map/ppermute | solution.py:56
  15.7 5.8 %collective-permute-start.6 = (bf16[16,3072]{1,0:T(8,128)(2,1)S(1)}, bf16[16,3072]{1,0:T(8,128)(2,1)S(1)}, u32[]{:S(2)}, u32[]{:S(2)}) collective-permute-start(bf16[16,3072]{1,0:T(8,128)(2,1)S(1)} %collective-permute-done.4.refs_5_), channel_id=1, source_target_pairs={{0,14},{2,0},{4,2},{6,4},{8,6},{10,8},{12,10},{14,12},{1,15},{3,1}... | collective-permute-start | bytes 294920 | tf_op jit(solution)/shard_map/ppermute | solution.py:56
  19.3 11.9 %collective-permute-start.2 = (bf16[32,3072]{1,0:T(8,128)(2,1)S(1)}, bf16[32,3072]{1,0:T(8,128)(2,1)S(1)}, u32[]{:S(2)}, u32[]{:S(2)}) collective-permute-start(bf16[32,3072]{1,0:T(8,128)(2,1)S(1)} %collective-permute-done.1.refs_2_), channel_id=1, source_target_pairs={{0,2},{2,4},{4,6},{6,8},{8,10},{10,12},{12,14},{14,0},{1,3},{3,5},... | collective-permute-start | bytes 589832 | tf_op jit(solution)/shard_map/ppermute | solution.py:56
  19.3 5.8 %collective-permute-start.5 = (bf16[16,3072]{1,0:T(8,128)(2,1)S(1)}, bf16[16,3072]{1,0:T(8,128)(2,1)S(1)}, u32[]{:S(2)}, u32[]{:S(2)}) collective-permute-start(bf16[16,3072]{1,0:T(8,128)(2,1)S(1)} %collective-permute-done.4.refs_5_), channel_id=1, source_target_pairs={{0,16},{16,0},{1,17},{17,1},{2,18},{18,2},{3,19},{19,3},{4,20},{20... | collective-permute-start | bytes 294920 | tf_op jit(solution)/shard_map/ppermute | solution.py:60
  21.5 6.0 %collective-permute-start.8 = (bf16[16,3072]{1,0:T(8,128)(2,1)S(1)}, bf16[16,3072]{1,0:T(8,128)(2,1)S(1)}, u32[]{:S(2)}, u32[]{:S(2)}) collective-permute-start(bf16[16,3072]{1,0:T(8,128)(2,1)S(1)} %collective-permute-done.6.refs_7_), channel_id=1, source_target_pairs={{0,14},{2,0},{4,2},{6,4},{8,6},{10,8},{12,10},{14,12},{1,15},{3,1}... | collective-permute-start | bytes 294920 | tf_op jit(solution)/shard_map/ppermute | solution.py:56
  25.1 6.1 %collective-permute-start.7 = (bf16[16,3072]{1,0:T(8,128)(2,1)S(1)}, bf16[16,3072]{1,0:T(8,128)(2,1)S(1)}, u32[]{:S(2)}, u32[]{:S(2)}) collective-permute-start(bf16[16,3072]{1,0:T(8,128)(2,1)S(1)} %collective-permute-done.6.refs_7_), channel_id=1, source_target_pairs={{0,16},{16,0},{1,17},{17,1},{2,18},{18,2},{3,19},{19,3},{4,20},{20... | collective-permute-start | bytes 294920 | tf_op jit(solution)/shard_map/ppermute | solution.py:60
  27.5 5.9 %collective-permute-start.10 = (bf16[16,3072]{1,0:T(8,128)(2,1)S(1)}, bf16[16,3072]{1,0:T(8,128)(2,1)S(1)}, u32[]{:S(2)}, u32[]{:S(2)}) collective-permute-start(bf16[16,3072]{1,0:T(8,128)(2,1)S(1)} %collective-permute-done.8.refs_9_), channel_id=1, source_target_pairs={{0,14},{2,0},{4,2},{6,4},{8,6},{10,8},{12,10},{14,12},{1,15},{3,1}... | collective-permute-start | bytes 294920 | tf_op jit(solution)/shard_map/ppermute | solution.py:56
  31.2 6.9 %collective-permute-start.3 = (bf16[32,3072]{1,0:T(8,128)(2,1)S(1)}, bf16[32,3072]{1,0:T(8,128)(2,1)S(1)}, u32[]{:S(2)}, u32[]{:S(2)}) collective-permute-start(bf16[32,3072]{1,0:T(8,128)(2,1)S(1)} %collective-permute-done.2.refs_3_), channel_id=1, source_target_pairs={{0,2},{2,4},{4,6},{6,8},{8,10},{10,12},{12,14},{14,0},{1,3},{3,5},... | collective-permute-start | bytes 589832 | tf_op jit(solution)/shard_map/ppermute | solution.py:56
  31.2 4.7 %collective-permute-start.9 = (bf16[16,3072]{1,0:T(8,128)(2,1)S(1)}, bf16[16,3072]{1,0:T(8,128)(2,1)S(1)}, u32[]{:S(2)}, u32[]{:S(2)}) collective-permute-start(bf16[16,3072]{1,0:T(8,128)(2,1)S(1)} %collective-permute-done.8.refs_9_), channel_id=1, source_target_pairs={{0,16},{16,0},{1,17},{17,1},{2,18},{18,2},{3,19},{19,3},{4,20},{20... | collective-permute-start | bytes 294920 | tf_op jit(solution)/shard_map/ppermute | solution.py:60
  33.4 4.6 %collective-permute-start.11 = (bf16[16,3072]{1,0:T(8,128)(2,1)S(1)}, bf16[16,3072]{1,0:T(8,128)(2,1)S(1)}, u32[]{:S(2)}, u32[]{:S(2)}) collective-permute-start(bf16[16,3072]{1,0:T(8,128)(2,1)S(1)} %collective-permute-done.10.refs_11_), channel_id=1, source_target_pairs={{0,16},{16,0},{1,17},{17,1},{2,18},{18,2},{3,19},{19,3},{4,20},{20... | collective-permute-start | bytes 294920 | tf_op jit(solution)/shard_map/ppermute | solution.py:60
  38.1 5.8 %copy-start.2 = (bf16[1536,768]{1,0:T(8,128)(2,1)}, bf16[1536,768]{1,0:T(8,128)(2,1)S(1)}, u32[]{:S(2)}) copy-start(bf16[1536,768]{1,0:T(8,128)(2,1)S(1)} %collective-permute-done.12.refs_14_.up_two) | copy-start | bytes 7077892
  44.0 7.4 %copy-start.4 = (bf16[768]{0:T(1024)(128)(2,1)S(1)}, bf16[768]{0:T(1024)(128)(2,1)}, u32[]{:S(2)}) copy-start(bf16[768]{0:T(1024)(128)(2,1)} %param.7) | copy-start | bytes 4612
  44.0 22.0 %all-to-all-start = ((bf16[8,32,3072]{2,1,0:T(8,128)(2,1)}), bf16[8,32,3072]{2,1,0:T(8,128)(2,1)S(1)}, u32[]{:S(2)}, u32[]{:S(2)}) async-start(bf16[8,32,3072]{2,1,0:T(8,128)(2,1)} %bitcast.14), calls=%async_computation | async-start | bytes 3145728 | tf_op jit(solution)/shard_map/all_to_all | solution.py:327
  51.4 1.2 collective-permute-start.14
  67.5 20.9 %all-to-all-start.1 = ((bf16[8,32,3072]{2,1,0:T(8,128)(2,1)}), bf16[8,32,3072]{2,1,0:T(8,128)(2,1)S(1)}, u32[]{:S(2)}, u32[]{:S(2)}) async-start(bf16[8,32,3072]{2,1,0:T(8,128)(2,1)} %bitcast.15), calls=%async_computation.1 | async-start | bytes 3145728 | tf_op jit(solution)/shard_map/all_to_all | solution.py:329
  73.6 28.0 %collective-permute-start.15 = (bf16[256,3072]{1,0:T(8,128)(2,1)S(1)}, bf16[256,3072]{1,0:T(8,128)(2,1)}, u32[]{:S(2)}, u32[]{:S(2)}) collective-permute-start(bf16[256,3072]{1,0:T(8,128)(2,1)S(1)} %get-tuple-element.6.left.right), channel_id=1, source_target_pairs={{0,1},{1,0},{2,3},{3,2},{4,5},{5,4},{6,7},{7,6},{8,9},{9,8},{10,11... | collective-permute-start | bytes 4718600 | tf_op jit(solution)/shard_map/ppermute | solution.py:60
  88.4 1.7 %copy-start.1 = (bf16[1536,768]{1,0:T(8,128)(2,1)S(1)}, bf16[1536,768]{1,0:T(8,128)(2,1)}, u32[]{:S(2)}) copy-start(bf16[1536,768]{1,0:T(8,128)(2,1)} %up.1) | copy-start | bytes 7077892
  94.4 22.7 %all-to-all-start.2 = ((bf16[16,16,1536]{2,1,0:T(8,128)(2,1)}), bf16[16,16,1536]{2,1,0:T(8,128)(2,1)}, u32[]{:S(2)}, u32[]{:S(2)}) async-start(bf16[16,16,1536]{2,1,0:T(8,128)(2,1)} %bitcast.13), calls=%async_computation.2 | async-start | bytes 1572864 | tf_op jit(solution)/shard_map/all_to_all | solution.py:332
  101.5 2.4 %collective-permute-start.16 = (bf16[256,1536]{1,0:T(8,128)(2,1)S(1)}, bf16[256,1536]{1,0:T(8,128)(2,1)S(1)}, u32[]{:S(2)}, u32[]{:S(2)}) collective-permute-start(bf16[256,1536]{1,0:T(8,128)(2,1)S(1)} %slice.4), channel_id=1, source_target_pairs={{0,1},{1,0},{2,3},{3,2},{4,5},{5,4},{6,7},{7,6},{8,9},{9,8},{10,11... | collective-permute-start | bytes 2359304 | tf_op jit(solution)/shard_map/ppermute | solution.py:60

commit v6 on v5

--- a/solution.py
+++ b/solution.py
@@ -192,7 +192,7 @@
     )(parts, bias.reshape(1, -1), bias_two.reshape(1, -1))
 
 
-def back_kernel(share, where, grads, up, up_two, out, rows, held, total, made, sems):
+def back_kernel(share, where, grads, up, up_two, out, rows, held, held_two, total, made, sems):
     width, units = up.shape
     tile = width // 3
     parts = [slice(t * tile, (t + 1) * tile) for t in range(3)]
@@ -204,23 +204,27 @@
         at = pl.multiple_of(owner * share, share)
         source = grads.at[i * share : (i + 1) * share, : 2 * units]
         loads.append(pltpu.make_async_copy(source, rows.at[pl.ds(at, share), :], sems.at[i]))
-    for t, part in enumerate(parts):
-        fetches.append(
-            pltpu.make_async_copy(up_two.at[part, :], held.at[part, :], sems.at[first + t])
-        )
-    for copy in loads + fetches:
+    for weight, place in ((up, held), (up_two, held_two)):
+        for part in parts:
+            sem = sems.at[first + len(fetches)]
+            fetches.append(pltpu.make_async_copy(weight.at[part, :], place.at[part, :], sem))
+    for copy in loads + fetches[:4]:
         copy.start()
     for copy in loads:
         copy.wait()
-    for part in parts:
-        total[:, part] = dot_t(rows[:, :units], up[part, :])
-    for t, part in enumerate(parts):
-        fetches[t].wait()
-        made[:, part] = (total[:, part] + dot_t(rows[:, units:], held[part, :])).astype(BF16)
-        sends.append(
-            pltpu.make_async_copy(made.at[:, part], out.at[:, part], sems.at[first + 3 + t])
-        )
-        sends[-1].start()
+    for t, fetch in enumerate(fetches):
+        part = parts[t % 3]
+        fetch.wait()
+        if t + 4 < len(fetches):
+            fetches[t + 4].start()
+        if t < 3:
+            total[:, part] = dot_t(rows[:, :units], held[part, :])
+        else:
+            sums = total[:, part] + dot_t(rows[:, units:], held_two[part, :])
+            made[:, part] = sums.astype(BF16)
+            sem = sems.at[first + 3 + t]
+            sends.append(pltpu.make_async_copy(made.at[:, part], out.at[:, part], sem))
+            sends[-1].start()
     for copy in sends:
         copy.wait()
 
@@ -231,19 +235,20 @@
     return pl.pallas_call(
         functools.partial(back_kernel, share),
         out_shape=pltpu.HBM((count, width), BF16),
-        in_specs=[pl.BlockSpec(memory_space=pltpu.SMEM), REMAIN, WHOLE, FAR],
+        in_specs=[pl.BlockSpec(memory_space=pltpu.SMEM), REMAIN, FAR, FAR],
         out_specs=FAR,
         scratch_shapes=[
             pltpu.VMEM((count, 2 * units), BF16),
             pltpu.VMEM(up.shape, BF16),
+            pltpu.VMEM(up.shape, BF16),
             pltpu.VMEM((count, width), F32),
             pltpu.VMEM((count, width), BF16),
-            pltpu.SemaphoreType.DMA((len(BLOCKS) + 6,)),
+            pltpu.SemaphoreType.DMA((len(BLOCKS) + 9,)),
         ],
         compiler_params=params(0),
         cost_estimate=light(),
         name="back",
-    )(where, both, up, in_hbm(up_two))
+    )(where, both, in_hbm(up), in_hbm(up_two))
 
 
 def collect_kernel(parts, out, held, sems):

time: 120 us -> 119 us (level)
  local copies, waits for them, and re-layouts: 1.75 us -> 0.09 us
    unnamed x10 -> x8, local copies, waits for them, and re-layouts: 1.69 us -> 0.02 us
  transfers between devices with their start and end apart: 20 -> 20, of which waited for: 13 -> 13; matrix products, arithmetic and copies ran while one was open for 0% -> 0% of each run, Pallas kernels for 12% -> 13%
where the time goes in v6:
time: 119 us; the launch traced here: 118 us
  waiting for transfers between devices  47.4 us (40%)
  starting transfers between devices  45.9 us (39%)
  Pallas kernels  24.1 us (20%)
    ppermute x7, starting transfers between devices, shift_z(): return lax.ppermute(x, 'z', [(i, (i + k) % ZN) for i in range(ZN)])  16.9 us
    all_to_all x1, waiting for transfers between devices, on_device(): both = lax.all_to_all(both, ROW, 0, 0, tiled=True)  14.7 us
    all_to_all x1, waiting for transfers between devices, on_device(): parts = lax.all_to_all(parts, ROW, 0, 0, tiled=True)  13.4 us
    ppermute x10, waiting for transfers between devices, swap(): return lax.ppermute(x, axis, [(0, 1), (1, 0)])  9.98 us
    pallas_call x2, Pallas kernels, outer(): pl.pallas_call(functools.partial(outer_kernel, factor), grid=(tiles,), ou...  8.42 us
    ppermute x10, starting transfers between devices, swap(): return lax.ppermute(x, axis, [(0, 1), (1, 0)])  8.32 us
    all_to_all x1, starting transfers between devices, on_device(): parts = lax.all_to_all(parts, ROW, 0, 0, tiled=True)  7.39 us
    all_to_all x1, starting transfers between devices, on_device(): near = lax.all_to_all(near, ('x_lo', 'z'), 0, 0, tiled=True)  7.02 us
  transfers between devices with their start and end apart: 20, of which 13 were waited for; matrix products, arithmetic and copies ran while one was open for 0% of the time, Pallas kernels for 13%

profile of v6, /device:TPU:8, one launch (start us, length us, event | category | flops | bytes accessed | tf_op | source)
XLA Modules:
  0.0 118.4 jit_solution(11071177990316072000)
XLA Ops:
  1.2 1.1 pack.1.refs_0_
  2.4 1.6 %collective-permute-start = (bf16[16,3072]{1,0:T(8,128)(2,1)S(1)}, bf16[16,3072]{1,0:T(8,128)(2,1)S(1)}, u32[]{:S(2)}, u32[]{:S(2)}) collective-permute-start(bf16[16,3072]{1,0:T(8,128)(2,1)S(1)} %pack.1.refs_0_), channel_id=1, source_target_pairs={{0,16},{16,0},{1,17},{17,1},{2,18},{18,2},{3,19},{19,3},{4,20},{20... | collective-permute-start | bytes 294920 | tf_op jit(solution)/shard_map/ppermute | solution.py:60
  4.0 3.4 %collective-permute-done.refs_1_ = bf16[16,3072]{1,0:T(8,128)(2,1)S(1)} collective-permute-done((bf16[16,3072]{1,0:T(8,128)(2,1)S(1)}, bf16[16,3072]{1,0:T(8,128)(2,1)S(1)}, u32[]{:S(2)}, u32[]{:S(2)}) %collective-permute-start) | collective-permute-done | bytes 98336 | tf_op jit(solution)/shard_map/ppermute | solution.py:60
  7.4 2.0 %collective-permute-start.1 = (bf16[32,3072]{1,0:T(8,128)(2,1)S(1)}, bf16[32,3072]{1,0:T(8,128)(2,1)S(1)}, u32[]{:S(2)}, u32[]{:S(2)}) collective-permute-start(bf16[32,3072]{1,0:T(8,128)(2,1)S(1)} %pad_maximum_fusion), channel_id=1, source_target_pairs={{0,2},{2,4},{4,6},{6,8},{8,10},{10,12},{12,14},{14,0},{1,3},{3,5},... | collective-permute-start | bytes 589832 | tf_op jit(solution)/shard_map/ppermute | solution.py:56
  9.4 4.0 %collective-permute-start.4 = (bf16[16,3072]{1,0:T(8,128)(2,1)S(1)}, bf16[16,3072]{1,0:T(8,128)(2,1)S(1)}, u32[]{:S(2)}, u32[]{:S(2)}) collective-permute-start(bf16[16,3072]{1,0:T(8,128)(2,1)S(1)} %pack.1.refs_0_), channel_id=1, source_target_pairs={{0,14},{2,0},{4,2},{6,4},{8,6},{10,8},{12,10},{14,12},{1,15},{3,1}... | collective-permute-start | bytes 294920 | tf_op jit(solution)/shard_map/ppermute | solution.py:56
  13.5 2.2 %collective-permute-done.4.refs_5_ = bf16[16,3072]{1,0:T(8,128)(2,1)S(1)} collective-permute-done((bf16[16,3072]{1,0:T(8,128)(2,1)S(1)}, bf16[16,3072]{1,0:T(8,128)(2,1)S(1)}, u32[]{:S(2)}, u32[]{:S(2)}) %collective-permute-start.4) | collective-permute-done | bytes 98336 | tf_op jit(solution)/shard_map/ppermute | solution.py:56
  15.7 3.6 %collective-permute-start.6 = (bf16[16,3072]{1,0:T(8,128)(2,1)S(1)}, bf16[16,3072]{1,0:T(8,128)(2,1)S(1)}, u32[]{:S(2)}, u32[]{:S(2)}) collective-permute-start(bf16[16,3072]{1,0:T(8,128)(2,1)S(1)} %collective-permute-done.4.refs_5_), channel_id=1, source_target_pairs={{0,14},{2,0},{4,2},{6,4},{8,6},{10,8},{12,10},{14,12},{1,15},{3,1}... | collective-permute-start | bytes 294920 | tf_op jit(solution)/shard_map/ppermute | solution.py:56
  19.3 1.5 %collective-permute-start.5 = (bf16[16,3072]{1,0:T(8,128)(2,1)S(1)}, bf16[16,3072]{1,0:T(8,128)(2,1)S(1)}, u32[]{:S(2)}, u32[]{:S(2)}) collective-permute-start(bf16[16,3072]{1,0:T(8,128)(2,1)S(1)} %collective-permute-done.4.refs_5_), channel_id=1, source_target_pairs={{0,16},{16,0},{1,17},{17,1},{2,18},{18,2},{3,19},{19,3},{4,20},{20... | collective-permute-start | bytes 294920 | tf_op jit(solution)/shard_map/ppermute | solution.py:60
  20.8 0.7 collective-permute-done.6.refs_7_
  21.5 3.6 %collective-permute-start.8 = (bf16[16,3072]{1,0:T(8,128)(2,1)S(1)}, bf16[16,3072]{1,0:T(8,128)(2,1)S(1)}, u32[]{:S(2)}, u32[]{:S(2)}) collective-permute-start(bf16[16,3072]{1,0:T(8,128)(2,1)S(1)} %collective-permute-done.6.refs_7_), channel_id=1, source_target_pairs={{0,14},{2,0},{4,2},{6,4},{8,6},{10,8},{12,10},{14,12},{1,15},{3,1}... | collective-permute-start | bytes 294920 | tf_op jit(solution)/shard_map/ppermute | solution.py:56
  25.1 1.5 %collective-permute-start.7 = (bf16[16,3072]{1,0:T(8,128)(2,1)S(1)}, bf16[16,3072]{1,0:T(8,128)(2,1)S(1)}, u32[]{:S(2)}, u32[]{:S(2)}) collective-permute-start(bf16[16,3072]{1,0:T(8,128)(2,1)S(1)} %collective-permute-done.6.refs_7_), channel_id=1, source_target_pairs={{0,16},{16,0},{1,17},{17,1},{2,18},{18,2},{3,19},{19,3},{4,20},{20... | collective-permute-start | bytes 294920 | tf_op jit(solution)/shard_map/ppermute | solution.py:60
  26.6 0.9 collective-permute-done.8.refs_9_
  27.5 3.7 %collective-permute-start.10 = (bf16[16,3072]{1,0:T(8,128)(2,1)S(1)}, bf16[16,3072]{1,0:T(8,128)(2,1)S(1)}, u32[]{:S(2)}, u32[]{:S(2)}) collective-permute-start(bf16[16,3072]{1,0:T(8,128)(2,1)S(1)} %collective-permute-done.8.refs_9_), channel_id=1, source_target_pairs={{0,14},{2,0},{4,2},{6,4},{8,6},{10,8},{12,10},{14,12},{1,15},{3,1}... | collective-permute-start | bytes 294920 | tf_op jit(solution)/shard_map/ppermute | solution.py:56
  31.2 1.6 %collective-permute-start.9 = (bf16[16,3072]{1,0:T(8,128)(2,1)S(1)}, bf16[16,3072]{1,0:T(8,128)(2,1)S(1)}, u32[]{:S(2)}, u32[]{:S(2)}) collective-permute-start(bf16[16,3072]{1,0:T(8,128)(2,1)S(1)} %collective-permute-done.8.refs_9_), channel_id=1, source_target_pairs={{0,16},{16,0},{1,17},{17,1},{2,18},{18,2},{3,19},{19,3},{4,20},{20... | collective-permute-start | bytes 294920 | tf_op jit(solution)/shard_map/ppermute | solution.py:60
  32.8 0.6 collective-permute-done.10.refs_11_
  33.4 1.5 %collective-permute-start.11 = (bf16[16,3072]{1,0:T(8,128)(2,1)S(1)}, bf16[16,3072]{1,0:T(8,128)(2,1)S(1)}, u32[]{:S(2)}, u32[]{:S(2)}) collective-permute-start(bf16[16,3072]{1,0:T(8,128)(2,1)S(1)} %collective-permute-done.10.refs_11_), channel_id=1, source_target_pairs={{0,16},{16,0},{1,17},{17,1},{2,18},{18,2},{3,19},{19,3},{4,20},{20... | collective-permute-start | bytes 294920 | tf_op jit(solution)/shard_map/ppermute | solution.py:60
  34.9 1.0 collective-permute-done.9.refs_10_
  35.9 2.1 %collective-permute-done.11.refs_12_ = bf16[16,3072]{1,0:T(8,128)(2,1)S(1)} collective-permute-done((bf16[16,3072]{1,0:T(8,128)(2,1)S(1)}, bf16[16,3072]{1,0:T(8,128)(2,1)S(1)}, u32[]{:S(2)}, u32[]{:S(2)}) %collective-permute-start.11) | collective-permute-done | bytes 98336 | tf_op jit(solution)/shard_map/ppermute | solution.py:60
  38.1 5.8 %project.1 = (bf16[256,3072]{1,0:T(8,128)(2,1)}, bf16[256,3072]{1,0:T(8,128)(2,1)S(1)}) custom-call(bf16[16,3072]{1,0:T(8,128)(2,1)S(1)} %pack.1.refs_0_, bf16[16,3072]{1,0:T(8,128)(2,1)S(1)} %collective-permute-done.refs_1_, bf16[32,3072]{1,0:T(8,128)(2,1)S(1)} %collective-permute-done.1.refs_2_, bf16[32,3072]{1,0:T(8,128)(2,1)S(1)} %collective-permute-done.2.refs_3_, ...), custom_call_target="tpu_custom_call" | custom-call | flops 1 | bytes 1 | tf_op jit(solution)/shard_map/project/pallas_call | solution.py:135
  44.0 7.4 %all-to-all-start = ((bf16[8,32,3072]{2,1,0:T(8,128)(2,1)}), bf16[8,32,3072]{2,1,0:T(8,128)(2,1)S(1)}, u32[]{:S(2)}, u32[]{:S(2)}) async-start(bf16[8,32,3072]{2,1,0:T(8,128)(2,1)} %bitcast.14), calls=%async_computation | async-start | bytes 3145728 | tf_op jit(solution)/shard_map/all_to_all | solution.py:332
  51.4 1.1 collective-permute-done.14
  52.5 13.4 %all-to-all-done = bf16[8,32,3072]{2,1,0:T(8,128)(2,1)S(1)} async-done(((bf16[8,32,3072]{2,1,0:T(8,128)(2,1)}), bf16[8,32,3072]{2,1,0:T(8,128)(2,1)S(1)}, u32[]{:S(2)}, u32[]{:S(2)}) %all-to-all-start) | async-done | bytes 1572896 | tf_op jit(solution)/shard_map/all_to_all | solution.py:332
  65.9 1.5 %pointwise.1 = bf16[256,3072]{1,0:T(8,128)(2,1)} custom-call(bf16[256,3072]{1,0:T(8,128)(2,1)S(1)} %bitcast.12, bf16[1,768]{1,0:T(2,128)(2,1)S(1)} %reshape.18.bias, bf16[1,768]{1,0:T(2,128)(2,1)S(1)} %reshape.19.bias_two), custom_call_target="tpu_custom_call" | custom-call | flops 20000000000 | bytes 2000000 | tf_op jit(solution)/shard_map/pointwise/pallas_call | solution.py:180
  67.5 6.2 %all-to-all-start.1 = ((bf16[8,32,3072]{2,1,0:T(8,128)(2,1)}), bf16[8,32,3072]{2,1,0:T(8,128)(2,1)S(1)}, u32[]{:S(2)}, u32[]{:S(2)}) async-start(bf16[8,32,3072]{2,1,0:T(8,128)(2,1)} %bitcast.15), calls=%async_computation.1 | async-start | bytes 3145728 | tf_op jit(solution)/shard_map/all_to_all | solution.py:334
  73.7 14.7 %all-to-all-done.1 = bf16[8,32,3072]{2,1,0:T(8,128)(2,1)S(1)} async-done(((bf16[8,32,3072]{2,1,0:T(8,128)(2,1)}), bf16[8,32,3072]{2,1,0:T(8,128)(2,1)S(1)}, u32[]{:S(2)}, u32[]{:S(2)}) %all-to-all-start.1) | async-done | bytes 1572896 | tf_op jit(solution)/shard_map/all_to_all | solution.py:334
  88.4 5.3 %back.1 = bf16[256,1536]{1,0:T(8,128)(2,1)} custom-call(s32[2]{0:T(128)S(1)} %pad_add_fusion.where, bf16[256,3072]{1,0:T(8,128)(2,1)S(1)} %bitcast.8, bf16[1536,768]{1,0:T(8,128)(2,1)} %up.1, bf16[1536,768]{1,0:T(8,128)(2,1)} %copy-done.1), custom_call_target="tpu_custom_call" | custom-call | flops 1 | bytes 1 | tf_op jit(solution)/shard_map/back/pallas_call | solution.py:235
  93.7 7.0 %all-to-all-start.2 = ((bf16[16,16,1536]{2,1,0:T(8,128)(2,1)}), bf16[16,16,1536]{2,1,0:T(8,128)(2,1)}, u32[]{:S(2)}, u32[]{:S(2)}) async-start(bf16[16,16,1536]{2,1,0:T(8,128)(2,1)} %bitcast.13), calls=%async_computation.2 | async-start | bytes 1572864 | tf_op jit(solution)/shard_map/all_to_all | solution.py:337
  100.9 2.3 %collective-permute-done.16.right_two.left_two = bf16[256,1536]{1,0:T(8,128)(2,1)S(1)} collective-permute-done((bf16[256,1536]{1,0:T(8,128)(2,1)S(1)}, bf16[256,1536]{1,0:T(8,128)(2,1)S(1)}, u32[]{:S(2)}, u32[]{:S(2)}) %collective-permute-start.16) | collective-permute-done | bytes 786464 | tf_op jit(solution)/shard_map/ppermute | solution.py:60
  103.2 4.2 %outer.3 = bf16[768,1536]{1,0:T(8,128)(2,1)} custom-call(bf16[256,3072]{1,0:T(8,128)(2,1)S(1)} %bitcast.10, bf16[256,1536]{1,0:T(8,128)(2,1)S(1)} %collective-permute-done.16.right_two.left_two, bf16[256,3072]{1,0:T(8,128)(2,1)S(1)} %get-tuple-element.6.left.right, bf16[256,3072]{1,0:T(8,128)(2,1)} %collective-permute-done.15.left_two.right_two), custom_call_target="tpu_custom_call" | custom-call | flops 1 | bytes 1 | tf_op jit(solution)/shard_map/outer/pallas_call | solution.py:300
  107.3 4.2 %outer.2 = bf16[1536,768]{1,0:T(8,128)(2,1)} custom-call(bf16[256,3072]{1,0:T(8,128)(2,1)S(1)} %get-tuple-element.6.left.right, bf16[256,3072]{1,0:T(8,128)(2,1)} %collective-permute-done.15.left_two.right_two, bf16[256,3072]{1,0:T(8,128)(2,1)S(1)} %bitcast.11, bf16[256,1536]{1,0:T(8,128)(2,1)S(1)} %collective-permute-done.16.right_two.left_two), custom_call_target="tpu_custom_call" | custom-call | flops 1 | bytes 1 | tf_op jit(solution)/shard_map/outer/pallas_call | solution.py:300
  111.6 4.8 %all-to-all-done.2 = bf16[16,16,1536]{2,1,0:T(8,128)(2,1)} async-done(((bf16[16,16,1536]{2,1,0:T(8,128)(2,1)}), bf16[16,16,1536]{2,1,0:T(8,128)(2,1)}, u32[]{:S(2)}, u32[]{:S(2)}) %all-to-all-start.2) | async-done | bytes 786464 | tf_op jit(solution)/shard_map/all_to_all | solution.py:337
  116.4 1.9 %collect.1 = bf16[16,1536]{1,0:T(8,128)(2,1)} custom-call(bf16[256,1536]{1,0:T(8,128)(2,1)} %bitcast.7.parts), custom_call_target="tpu_custom_call" | custom-call | flops 1 | bytes 1 | tf_op jit(solution)/shard_map/collect/pallas_call | solution.py:271
  (28 shorter events, 0.9 us)
Async XLA Ops:
  0.6 37.5 %copy-start.2 = (bf16[768,1536]{1,0:T(8,128)(2,1)S(1)}, bf16[768,1536]{1,0:T(8,128)(2,1)}, u32[]{:S(2)}) copy-start(bf16[768,1536]{1,0:T(8,128)(2,1)} %refs_15_.1) | copy-start | bytes 7077892
  0.6 37.5 %copy-start = (bf16[1536,768]{1,0:T(8,128)(2,1)S(1)}, bf16[1536,768]{1,0:T(8,128)(2,1)}, u32[]{:S(2)}) copy-start(bf16[1536,768]{1,0:T(8,128)(2,1)} %up.1) | copy-start | bytes 7077892
  0.7 37.4 %collective-permute-start.13 = (bf16[768,1536]{1,0:T(8,128)(2,1)}, bf16[768,1536]{1,0:T(8,128)(2,1)S(1)}, u32[]{:S(2)}, u32[]{:S(2)}) collective-permute-start(bf16[768,1536]{1,0:T(8,128)(2,1)} %refs_15_.1), channel_id=1, source_target_pairs={{0,1},{1,0},{2,3},{3,2},{4,5},{5,4},{6,7},{7,6},{8,9},{9,8},{10,11... | collective-permute-start | bytes 7077896 | tf_op jit(solution)/shard_map/ppermute | solution.py:60
  0.8 37.3 %collective-permute-start.12 = (bf16[1536,768]{1,0:T(8,128)(2,1)}, bf16[1536,768]{1,0:T(8,128)(2,1)S(1)}, u32[]{:S(2)}, u32[]{:S(2)}) collective-permute-start(bf16[1536,768]{1,0:T(8,128)(2,1)} %up.1), channel_id=1, source_target_pairs={{0,1},{1,0},{2,3},{3,2},{4,5},{5,4},{6,7},{7,6},{8,9},{9,8},{10,11... | collective-permute-start | bytes 7077896 | tf_op jit(solution)/shard_map/ppermute | solution.py:60
  2.4 5.0 %collective-permute-start = (bf16[16,3072]{1,0:T(8,128)(2,1)S(1)}, bf16[16,3072]{1,0:T(8,128)(2,1)S(1)}, u32[]{:S(2)}, u32[]{:S(2)}) collective-permute-start(bf16[16,3072]{1,0:T(8,128)(2,1)S(1)} %pack.1.refs_0_), channel_id=1, source_target_pairs={{0,16},{16,0},{1,17},{17,1},{2,18},{18,2},{3,19},{19,3},{4,20},{20... | collective-permute-start | bytes 294920 | tf_op jit(solution)/shard_map/ppermute | solution.py:60
  7.4 11.9 %collective-permute-start.1 = (bf16[32,3072]{1,0:T(8,128)(2,1)S(1)}, bf16[32,3072]{1,0:T(8,128)(2,1)S(1)}, u32[]{:S(2)}, u32[]{:S(2)}) collective-permute-start(bf16[32,3072]{1,0:T(8,128)(2,1)S(1)} %pad_maximum_fusion), channel_id=1, source_target_pairs={{0,2},{2,4},{4,6},{6,8},{8,10},{10,12},{12,14},{14,0},{1,3},{3,5},... | collective-permute-start | bytes 589832 | tf_op jit(solution)/shard_map/ppermute | solution.py:56
  9.4 6.2 %collective-permute-start.4 = (bf16[16,3072]{1,0:T(8,128)(2,1)S(1)}, bf16[16,3072]{1,0:T(8,128)(2,1)S(1)}, u32[]{:S(2)}, u32[]{:S(2)}) collective-permute-start(bf16[16,3072]{1,0:T(8,128)(2,1)S(1)} %pack.1.refs_0_), channel_id=1, source_target_pairs={{0,14},{2,0},{4,2},{6,4},{8,6},{10,8},{12,10},{14,12},{1,15},{3,1}... | collective-permute-start | bytes 294920 | tf_op jit(solution)/shard_map/ppermute | solution.py:56
  15.7 5.8 %collective-permute-start.6 = (bf16[16,3072]{1,0:T(8,128)(2,1)S(1)}, bf16[16,3072]{1,0:T(8,128)(2,1)S(1)}, u32[]{:S(2)}, u32[]{:S(2)}) collective-permute-start(bf16[16,3072]{1,0:T(8,128)(2,1)S(1)} %collective-permute-done.4.refs_5_), channel_id=1, source_target_pairs={{0,14},{2,0},{4,2},{6,4},{8,6},{10,8},{12,10},{14,12},{1,15},{3,1}... | collective-permute-start | bytes 294920 | tf_op jit(solution)/shard_map/ppermute | solution.py:56
  19.3 11.9 %collective-permute-start.2 = (bf16[32,3072]{1,0:T(8,128)(2,1)S(1)}, bf16[32,3072]{1,0:T(8,128)(2,1)S(1)}, u32[]{:S(2)}, u32[]{:S(2)}) collective-permute-start(bf16[32,3072]{1,0:T(8,128)(2,1)S(1)} %collective-permute-done.1.refs_2_), channel_id=1, source_target_pairs={{0,2},{2,4},{4,6},{6,8},{8,10},{10,12},{12,14},{14,0},{1,3},{3,5},... | collective-permute-start | bytes 589832 | tf_op jit(solution)/shard_map/ppermute | solution.py:56
  19.3 5.8 %collective-permute-start.5 = (bf16[16,3072]{1,0:T(8,128)(2,1)S(1)}, bf16[16,3072]{1,0:T(8,128)(2,1)S(1)}, u32[]{:S(2)}, u32[]{:S(2)}) collective-permute-start(bf16[16,3072]{1,0:T(8,128)(2,1)S(1)} %collective-permute-done.4.refs_5_), channel_id=1, source_target_pairs={{0,16},{16,0},{1,17},{17,1},{2,18},{18,2},{3,19},{19,3},{4,20},{20... | collective-permute-start | bytes 294920 | tf_op jit(solution)/shard_map/ppermute | solution.py:60
  21.5 6.0 %collective-permute-start.8 = (bf16[16,3072]{1,0:T(8,128)(2,1)S(1)}, bf16[16,3072]{1,0:T(8,128)(2,1)S(1)}, u32[]{:S(2)}, u32[]{:S(2)}) collective-permute-start(bf16[16,3072]{1,0:T(8,128)(2,1)S(1)} %collective-permute-done.6.refs_7_), channel_id=1, source_target_pairs={{0,14},{2,0},{4,2},{6,4},{8,6},{10,8},{12,10},{14,12},{1,15},{3,1}... | collective-permute-start | bytes 294920 | tf_op jit(solution)/shard_map/ppermute | solution.py:56
  25.1 6.1 %collective-permute-start.7 = (bf16[16,3072]{1,0:T(8,128)(2,1)S(1)}, bf16[16,3072]{1,0:T(8,128)(2,1)S(1)}, u32[]{:S(2)}, u32[]{:S(2)}) collective-permute-start(bf16[16,3072]{1,0:T(8,128)(2,1)S(1)} %collective-permute-done.6.refs_7_), channel_id=1, source_target_pairs={{0,16},{16,0},{1,17},{17,1},{2,18},{18,2},{3,19},{19,3},{4,20},{20... | collective-permute-start | bytes 294920 | tf_op jit(solution)/shard_map/ppermute | solution.py:60
  27.5 5.9 %collective-permute-start.10 = (bf16[16,3072]{1,0:T(8,128)(2,1)S(1)}, bf16[16,3072]{1,0:T(8,128)(2,1)S(1)}, u32[]{:S(2)}, u32[]{:S(2)}) collective-permute-start(bf16[16,3072]{1,0:T(8,128)(2,1)S(1)} %collective-permute-done.8.refs_9_), channel_id=1, source_target_pairs={{0,14},{2,0},{4,2},{6,4},{8,6},{10,8},{12,10},{14,12},{1,15},{3,1}... | collective-permute-start | bytes 294920 | tf_op jit(solution)/shard_map/ppermute | solution.py:56
  31.2 6.9 %collective-permute-start.3 = (bf16[32,3072]{1,0:T(8,128)(2,1)S(1)}, bf16[32,3072]{1,0:T(8,128)(2,1)S(1)}, u32[]{:S(2)}, u32[]{:S(2)}) collective-permute-start(bf16[32,3072]{1,0:T(8,128)(2,1)S(1)} %collective-permute-done.2.refs_3_), channel_id=1, source_target_pairs={{0,2},{2,4},{4,6},{6,8},{8,10},{10,12},{12,14},{14,0},{1,3},{3,5},... | collective-permute-start | bytes 589832 | tf_op jit(solution)/shard_map/ppermute | solution.py:56
  31.2 4.7 %collective-permute-start.9 = (bf16[16,3072]{1,0:T(8,128)(2,1)S(1)}, bf16[16,3072]{1,0:T(8,128)(2,1)S(1)}, u32[]{:S(2)}, u32[]{:S(2)}) collective-permute-start(bf16[16,3072]{1,0:T(8,128)(2,1)S(1)} %collective-permute-done.8.refs_9_), channel_id=1, source_target_pairs={{0,16},{16,0},{1,17},{17,1},{2,18},{18,2},{3,19},{19,3},{4,20},{20... | collective-permute-start | bytes 294920 | tf_op jit(solution)/shard_map/ppermute | solution.py:60
  33.4 4.6 %collective-permute-start.11 = (bf16[16,3072]{1,0:T(8,128)(2,1)S(1)}, bf16[16,3072]{1,0:T(8,128)(2,1)S(1)}, u32[]{:S(2)}, u32[]{:S(2)}) collective-permute-start(bf16[16,3072]{1,0:T(8,128)(2,1)S(1)} %collective-permute-done.10.refs_11_), channel_id=1, source_target_pairs={{0,16},{16,0},{1,17},{17,1},{2,18},{18,2},{3,19},{19,3},{4,20},{20... | collective-permute-start | bytes 294920 | tf_op jit(solution)/shard_map/ppermute | solution.py:60
  38.1 5.8 %copy-start.1 = (bf16[1536,768]{1,0:T(8,128)(2,1)}, bf16[1536,768]{1,0:T(8,128)(2,1)S(1)}, u32[]{:S(2)}) copy-start(bf16[1536,768]{1,0:T(8,128)(2,1)S(1)} %collective-permute-done.12.refs_14_.up_two) | copy-start | bytes 7077892
  44.0 7.4 %copy-start.3 = (bf16[768]{0:T(1024)(128)(2,1)S(1)}, bf16[768]{0:T(1024)(128)(2,1)}, u32[]{:S(2)}) copy-start(bf16[768]{0:T(1024)(128)(2,1)} %param.7) | copy-start | bytes 4612
  44.0 22.0 %all-to-all-start = ((bf16[8,32,3072]{2,1,0:T(8,128)(2,1)}), bf16[8,32,3072]{2,1,0:T(8,128)(2,1)S(1)}, u32[]{:S(2)}, u32[]{:S(2)}) async-start(bf16[8,32,3072]{2,1,0:T(8,128)(2,1)} %bitcast.14), calls=%async_computation | async-start | bytes 3145728 | tf_op jit(solution)/shard_map/all_to_all | solution.py:332
  51.4 1.2 collective-permute-start.14
  67.5 20.9 %all-to-all-start.1 = ((bf16[8,32,3072]{2,1,0:T(8,128)(2,1)}), bf16[8,32,3072]{2,1,0:T(8,128)(2,1)S(1)}, u32[]{:S(2)}, u32[]{:S(2)}) async-start(bf16[8,32,3072]{2,1,0:T(8,128)(2,1)} %bitcast.15), calls=%async_computation.1 | async-start | bytes 3145728 | tf_op jit(solution)/shard_map/all_to_all | solution.py:334
  73.6 27.3 %collective-permute-start.15 = (bf16[256,3072]{1,0:T(8,128)(2,1)S(1)}, bf16[256,3072]{1,0:T(8,128)(2,1)}, u32[]{:S(2)}, u32[]{:S(2)}) collective-permute-start(bf16[256,3072]{1,0:T(8,128)(2,1)S(1)} %get-tuple-element.6.left.right), channel_id=1, source_target_pairs={{0,1},{1,0},{2,3},{3,2},{4,5},{5,4},{6,7},{7,6},{8,9},{9,8},{10,11... | collective-permute-start | bytes 4718600 | tf_op jit(solution)/shard_map/ppermute | solution.py:60
  93.7 22.7 %all-to-all-start.2 = ((bf16[16,16,1536]{2,1,0:T(8,128)(2,1)}), bf16[16,16,1536]{2,1,0:T(8,128)(2,1)}, u32[]{:S(2)}, u32[]{:S(2)}) async-start(bf16[16,16,1536]{2,1,0:T(8,128)(2,1)} %bitcast.13), calls=%async_computation.2 | async-start | bytes 1572864 | tf_op jit(solution)/shard_map/all_to_all | solution.py:337
  100.8 2.4 %collective-permute-start.16 = (bf16[256,1536]{1,0:T(8,128)(2,1)S(1)}, bf16[256,1536]{1,0:T(8,128)(2,1)S(1)}, u32[]{:S(2)}, u32[]{:S(2)}) collective-permute-start(bf16[256,1536]{1,0:T(8,128)(2,1)S(1)} %slice.4), channel_id=1, source_target_pairs={{0,1},{1,0},{2,3},{3,2},{4,5},{5,4},{6,7},{7,6},{8,9},{9,8},{10,11... | collective-permute-start | bytes 2359304 | tf_op jit(solution)/shard_map/ppermute | solution.py:60

commit v7 on v6

--- a/solution.py
+++ b/solution.py
@@ -208,15 +208,13 @@
         for part in parts:
             sem = sems.at[first + len(fetches)]
             fetches.append(pltpu.make_async_copy(weight.at[part, :], place.at[part, :], sem))
-    for copy in loads + fetches[:4]:
+    for copy in loads + fetches:
         copy.start()
     for copy in loads:
         copy.wait()
     for t, fetch in enumerate(fetches):
         part = parts[t % 3]
         fetch.wait()
-        if t + 4 < len(fetches):
-            fetches[t + 4].start()
         if t < 3:
             total[:, part] = dot_t(rows[:, :units], held[part, :])
         else:

time: 119 us -> 119 us (level)
  no operation moved by 1% of the time
where the time goes in v7:
time: 119 us; the launch traced here: 118 us
  waiting for transfers between devices  47.4 us (40%)
  starting transfers between devices  45.9 us (39%)
  Pallas kernels  24 us (20%)
    ppermute x7, starting transfers between devices, shift_z(): return lax.ppermute(x, 'z', [(i, (i + k) % ZN) for i in range(ZN)])  16.9 us
    all_to_all x1, waiting for transfers between devices, on_device(): both = lax.all_to_all(both, ROW, 0, 0, tiled=True)  14.7 us
    all_to_all x1, waiting for transfers between devices, on_device(): parts = lax.all_to_all(parts, ROW, 0, 0, tiled=True)  13.4 us
    ppermute x10, waiting for transfers between devices, swap(): return lax.ppermute(x, axis, [(0, 1), (1, 0)])  9.98 us
    pallas_call x2, Pallas kernels, outer(): pl.pallas_call(functools.partial(outer_kernel, factor), grid=(tiles,), ou...  8.42 us
    ppermute x10, starting transfers between devices, swap(): return lax.ppermute(x, axis, [(0, 1), (1, 0)])  8.32 us
    all_to_all x1, starting transfers between devices, on_device(): parts = lax.all_to_all(parts, ROW, 0, 0, tiled=True)  7.39 us
    all_to_all x1, starting transfers between devices, on_device(): near = lax.all_to_all(near, ('x_lo', 'z'), 0, 0, tiled=True)  7.02 us
  transfers between devices with their start and end apart: 20, of which 13 were waited for; matrix products, arithmetic and copies ran while one was open for 0% of the time, Pallas kernels for 13%

profile of v7, /device:TPU:8, one launch (start us, length us, event | category | flops | bytes accessed | tf_op | source)
XLA Modules:
  0.0 118.4 jit_solution(13691085894134088971)
XLA Ops:
  1.2 1.1 pack.1.refs_0_
  2.4 1.6 %collective-permute-start = (bf16[16,3072]{1,0:T(8,128)(2,1)S(1)}, bf16[16,3072]{1,0:T(8,128)(2,1)S(1)}, u32[]{:S(2)}, u32[]{:S(2)}) collective-permute-start(bf16[16,3072]{1,0:T(8,128)(2,1)S(1)} %pack.1.refs_0_), channel_id=1, source_target_pairs={{0,16},{16,0},{1,17},{17,1},{2,18},{18,2},{3,19},{19,3},{4,20},{20... | collective-permute-start | bytes 294920 | tf_op jit(solution)/shard_map/ppermute | solution.py:60
  4.0 3.4 %collective-permute-done.refs_1_ = bf16[16,3072]{1,0:T(8,128)(2,1)S(1)} collective-permute-done((bf16[16,3072]{1,0:T(8,128)(2,1)S(1)}, bf16[16,3072]{1,0:T(8,128)(2,1)S(1)}, u32[]{:S(2)}, u32[]{:S(2)}) %collective-permute-start) | collective-permute-done | bytes 98336 | tf_op jit(solution)/shard_map/ppermute | solution.py:60
  7.4 2.0 %collective-permute-start.1 = (bf16[32,3072]{1,0:T(8,128)(2,1)S(1)}, bf16[32,3072]{1,0:T(8,128)(2,1)S(1)}, u32[]{:S(2)}, u32[]{:S(2)}) collective-permute-start(bf16[32,3072]{1,0:T(8,128)(2,1)S(1)} %pad_maximum_fusion), channel_id=1, source_target_pairs={{0,2},{2,4},{4,6},{6,8},{8,10},{10,12},{12,14},{14,0},{1,3},{3,5},... | collective-permute-start | bytes 589832 | tf_op jit(solution)/shard_map/ppermute | solution.py:56
  9.4 4.0 %collective-permute-start.4 = (bf16[16,3072]{1,0:T(8,128)(2,1)S(1)}, bf16[16,3072]{1,0:T(8,128)(2,1)S(1)}, u32[]{:S(2)}, u32[]{:S(2)}) collective-permute-start(bf16[16,3072]{1,0:T(8,128)(2,1)S(1)} %pack.1.refs_0_), channel_id=1, source_target_pairs={{0,14},{2,0},{4,2},{6,4},{8,6},{10,8},{12,10},{14,12},{1,15},{3,1}... | collective-permute-start | bytes 294920 | tf_op jit(solution)/shard_map/ppermute | solution.py:56
  13.5 2.2 %collective-permute-done.4.refs_5_ = bf16[16,3072]{1,0:T(8,128)(2,1)S(1)} collective-permute-done((bf16[16,3072]{1,0:T(8,128)(2,1)S(1)}, bf16[16,3072]{1,0:T(8,128)(2,1)S(1)}, u32[]{:S(2)}, u32[]{:S(2)}) %collective-permute-start.4) | collective-permute-done | bytes 98336 | tf_op jit(solution)/shard_map/ppermute | solution.py:56
  15.7 3.6 %collective-permute-start.6 = (bf16[16,3072]{1,0:T(8,128)(2,1)S(1)}, bf16[16,3072]{1,0:T(8,128)(2,1)S(1)}, u32[]{:S(2)}, u32[]{:S(2)}) collective-permute-start(bf16[16,3072]{1,0:T(8,128)(2,1)S(1)} %collective-permute-done.4.refs_5_), channel_id=1, source_target_pairs={{0,14},{2,0},{4,2},{6,4},{8,6},{10,8},{12,10},{14,12},{1,15},{3,1}... | collective-permute-start | bytes 294920 | tf_op jit(solution)/shard_map/ppermute | solution.py:56
  19.3 1.5 %collective-permute-start.5 = (bf16[16,3072]{1,0:T(8,128)(2,1)S(1)}, bf16[16,3072]{1,0:T(8,128)(2,1)S(1)}, u32[]{:S(2)}, u32[]{:S(2)}) collective-permute-start(bf16[16,3072]{1,0:T(8,128)(2,1)S(1)} %collective-permute-done.4.refs_5_), channel_id=1, source_target_pairs={{0,16},{16,0},{1,17},{17,1},{2,18},{18,2},{3,19},{19,3},{4,20},{20... | collective-permute-start | bytes 294920 | tf_op jit(solution)/shard_map/ppermute | solution.py:60
  20.8 0.7 collective-permute-done.6.refs_7_
  21.5 3.6 %collective-permute-start.8 = (bf16[16,3072]{1,0:T(8,128)(2,1)S(1)}, bf16[16,3072]{1,0:T(8,128)(2,1)S(1)}, u32[]{:S(2)}, u32[]{:S(2)}) collective-permute-start(bf16[16,3072]{1,0:T(8,128)(2,1)S(1)} %collective-permute-done.6.refs_7_), channel_id=1, source_target_pairs={{0,14},{2,0},{4,2},{6,4},{8,6},{10,8},{12,10},{14,12},{1,15},{3,1}... | collective-permute-start | bytes 294920 | tf_op jit(solution)/shard_map/ppermute | solution.py:56
  25.1 1.5 %collective-permute-start.7 = (bf16[16,3072]{1,0:T(8,128)(2,1)S(1)}, bf16[16,3072]{1,0:T(8,128)(2,1)S(1)}, u32[]{:S(2)}, u32[]{:S(2)}) collective-permute-start(bf16[16,3072]{1,0:T(8,128)(2,1)S(1)} %collective-permute-done.6.refs_7_), channel_id=1, source_target_pairs={{0,16},{16,0},{1,17},{17,1},{2,18},{18,2},{3,19},{19,3},{4,20},{20... | collective-permute-start | bytes 294920 | tf_op jit(solution)/shard_map/ppermute | solution.py:60
  26.6 0.9 collective-permute-done.8.refs_9_
  27.5 3.7 %collective-permute-start.10 = (bf16[16,3072]{1,0:T(8,128)(2,1)S(1)}, bf16[16,3072]{1,0:T(8,128)(2,1)S(1)}, u32[]{:S(2)}, u32[]{:S(2)}) collective-permute-start(bf16[16,3072]{1,0:T(8,128)(2,1)S(1)} %collective-permute-done.8.refs_9_), channel_id=1, source_target_pairs={{0,14},{2,0},{4,2},{6,4},{8,6},{10,8},{12,10},{14,12},{1,15},{3,1}... | collective-permute-start | bytes 294920 | tf_op jit(solution)/shard_map/ppermute | solution.py:56
  31.2 1.6 %collective-permute-start.9 = (bf16[16,3072]{1,0:T(8,128)(2,1)S(1)}, bf16[16,3072]{1,0:T(8,128)(2,1)S(1)}, u32[]{:S(2)}, u32[]{:S(2)}) collective-permute-start(bf16[16,3072]{1,0:T(8,128)(2,1)S(1)} %collective-permute-done.8.refs_9_), channel_id=1, source_target_pairs={{0,16},{16,0},{1,17},{17,1},{2,18},{18,2},{3,19},{19,3},{4,20},{20... | collective-permute-start | bytes 294920 | tf_op jit(solution)/shard_map/ppermute | solution.py:60
  32.8 0.6 collective-permute-done.10.refs_11_
  33.4 1.5 %collective-permute-start.11 = (bf16[16,3072]{1,0:T(8,128)(2,1)S(1)}, bf16[16,3072]{1,0:T(8,128)(2,1)S(1)}, u32[]{:S(2)}, u32[]{:S(2)}) collective-permute-start(bf16[16,3072]{1,0:T(8,128)(2,1)S(1)} %collective-permute-done.10.refs_11_), channel_id=1, source_target_pairs={{0,16},{16,0},{1,17},{17,1},{2,18},{18,2},{3,19},{19,3},{4,20},{20... | collective-permute-start | bytes 294920 | tf_op jit(solution)/shard_map/ppermute | solution.py:60
  34.9 1.0 collective-permute-done.9.refs_10_
  35.9 2.1 %collective-permute-done.11.refs_12_ = bf16[16,3072]{1,0:T(8,128)(2,1)S(1)} collective-permute-done((bf16[16,3072]{1,0:T(8,128)(2,1)S(1)}, bf16[16,3072]{1,0:T(8,128)(2,1)S(1)}, u32[]{:S(2)}, u32[]{:S(2)}) %collective-permute-start.11) | collective-permute-done | bytes 98336 | tf_op jit(solution)/shard_map/ppermute | solution.py:60
  38.1 5.8 %project.1 = (bf16[256,3072]{1,0:T(8,128)(2,1)}, bf16[256,3072]{1,0:T(8,128)(2,1)S(1)}) custom-call(bf16[16,3072]{1,0:T(8,128)(2,1)S(1)} %pack.1.refs_0_, bf16[16,3072]{1,0:T(8,128)(2,1)S(1)} %collective-permute-done.refs_1_, bf16[32,3072]{1,0:T(8,128)(2,1)S(1)} %collective-permute-done.1.refs_2_, bf16[32,3072]{1,0:T(8,128)(2,1)S(1)} %collective-permute-done.2.refs_3_, ...), custom_call_target="tpu_custom_call" | custom-call | flops 1 | bytes 1 | tf_op jit(solution)/shard_map/project/pallas_call | solution.py:135
  44.0 7.4 %all-to-all-start = ((bf16[8,32,3072]{2,1,0:T(8,128)(2,1)}), bf16[8,32,3072]{2,1,0:T(8,128)(2,1)S(1)}, u32[]{:S(2)}, u32[]{:S(2)}) async-start(bf16[8,32,3072]{2,1,0:T(8,128)(2,1)} %bitcast.14), calls=%async_computation | async-start | bytes 3145728 | tf_op jit(solution)/shard_map/all_to_all | solution.py:330
  51.4 1.1 collective-permute-done.14
  52.5 13.4 %all-to-all-done = bf16[8,32,3072]{2,1,0:T(8,128)(2,1)S(1)} async-done(((bf16[8,32,3072]{2,1,0:T(8,128)(2,1)}), bf16[8,32,3072]{2,1,0:T(8,128)(2,1)S(1)}, u32[]{:S(2)}, u32[]{:S(2)}) %all-to-all-start) | async-done | bytes 1572896 | tf_op jit(solution)/shard_map/all_to_all | solution.py:330
  65.9 1.5 %pointwise.1 = bf16[256,3072]{1,0:T(8,128)(2,1)} custom-call(bf16[256,3072]{1,0:T(8,128)(2,1)S(1)} %bitcast.12, bf16[1,768]{1,0:T(2,128)(2,1)S(1)} %reshape.18.bias, bf16[1,768]{1,0:T(2,128)(2,1)S(1)} %reshape.19.bias_two), custom_call_target="tpu_custom_call" | custom-call | flops 20000000000 | bytes 2000000 | tf_op jit(solution)/shard_map/pointwise/pallas_call | solution.py:180
  67.5 6.2 %all-to-all-start.1 = ((bf16[8,32,3072]{2,1,0:T(8,128)(2,1)}), bf16[8,32,3072]{2,1,0:T(8,128)(2,1)S(1)}, u32[]{:S(2)}, u32[]{:S(2)}) async-start(bf16[8,32,3072]{2,1,0:T(8,128)(2,1)} %bitcast.15), calls=%async_computation.1 | async-start | bytes 3145728 | tf_op jit(solution)/shard_map/all_to_all | solution.py:332
  73.7 14.7 %all-to-all-done.1 = bf16[8,32,3072]{2,1,0:T(8,128)(2,1)S(1)} async-done(((bf16[8,32,3072]{2,1,0:T(8,128)(2,1)}), bf16[8,32,3072]{2,1,0:T(8,128)(2,1)S(1)}, u32[]{:S(2)}, u32[]{:S(2)}) %all-to-all-start.1) | async-done | bytes 1572896 | tf_op jit(solution)/shard_map/all_to_all | solution.py:332
  88.4 5.3 %back.1 = bf16[256,1536]{1,0:T(8,128)(2,1)} custom-call(s32[2]{0:T(128)S(1)} %pad_add_fusion.where, bf16[256,3072]{1,0:T(8,128)(2,1)S(1)} %bitcast.8, bf16[1536,768]{1,0:T(8,128)(2,1)} %up.1, bf16[1536,768]{1,0:T(8,128)(2,1)} %copy-done.1), custom_call_target="tpu_custom_call" | custom-call | flops 1 | bytes 1 | tf_op jit(solution)/shard_map/back/pallas_call | solution.py:233
  93.6 7.0 %all-to-all-start.2 = ((bf16[16,16,1536]{2,1,0:T(8,128)(2,1)}), bf16[16,16,1536]{2,1,0:T(8,128)(2,1)}, u32[]{:S(2)}, u32[]{:S(2)}) async-start(bf16[16,16,1536]{2,1,0:T(8,128)(2,1)} %bitcast.13), calls=%async_computation.2 | async-start | bytes 1572864 | tf_op jit(solution)/shard_map/all_to_all | solution.py:335
  100.8 2.3 %collective-permute-done.16.right_two.left_two = bf16[256,1536]{1,0:T(8,128)(2,1)S(1)} collective-permute-done((bf16[256,1536]{1,0:T(8,128)(2,1)S(1)}, bf16[256,1536]{1,0:T(8,128)(2,1)S(1)}, u32[]{:S(2)}, u32[]{:S(2)}) %collective-permute-start.16) | collective-permute-done | bytes 786464 | tf_op jit(solution)/shard_map/ppermute | solution.py:60
  103.1 4.2 %outer.3 = bf16[768,1536]{1,0:T(8,128)(2,1)} custom-call(bf16[256,3072]{1,0:T(8,128)(2,1)S(1)} %bitcast.10, bf16[256,1536]{1,0:T(8,128)(2,1)S(1)} %collective-permute-done.16.right_two.left_two, bf16[256,3072]{1,0:T(8,128)(2,1)S(1)} %get-tuple-element.6.left.right, bf16[256,3072]{1,0:T(8,128)(2,1)} %collective-permute-done.15.left_two.right_two), custom_call_target="tpu_custom_call" | custom-call | flops 1 | bytes 1 | tf_op jit(solution)/shard_map/outer/pallas_call | solution.py:298
  107.3 4.2 %outer.2 = bf16[1536,768]{1,0:T(8,128)(2,1)} custom-call(bf16[256,3072]{1,0:T(8,128)(2,1)S(1)} %get-tuple-element.6.left.right, bf16[256,3072]{1,0:T(8,128)(2,1)} %collective-permute-done.15.left_two.right_two, bf16[256,3072]{1,0:T(8,128)(2,1)S(1)} %bitcast.11, bf16[256,1536]{1,0:T(8,128)(2,1)S(1)} %collective-permute-done.16.right_two.left_two), custom_call_target="tpu_custom_call" | custom-call | flops 1 | bytes 1 | tf_op jit(solution)/shard_map/outer/pallas_call | solution.py:298
  111.5 4.8 %all-to-all-done.2 = bf16[16,16,1536]{2,1,0:T(8,128)(2,1)} async-done(((bf16[16,16,1536]{2,1,0:T(8,128)(2,1)}), bf16[16,16,1536]{2,1,0:T(8,128)(2,1)}, u32[]{:S(2)}, u32[]{:S(2)}) %all-to-all-start.2) | async-done | bytes 786464 | tf_op jit(solution)/shard_map/all_to_all | solution.py:335
  116.3 1.9 %collect.1 = bf16[16,1536]{1,0:T(8,128)(2,1)} custom-call(bf16[256,1536]{1,0:T(8,128)(2,1)} %bitcast.7.parts), custom_call_target="tpu_custom_call" | custom-call | flops 1 | bytes 1 | tf_op jit(solution)/shard_map/collect/pallas_call | solution.py:269
  (28 shorter events, 0.9 us)
Async XLA Ops:
  0.6 37.5 %copy-start.2 = (bf16[768,1536]{1,0:T(8,128)(2,1)S(1)}, bf16[768,1536]{1,0:T(8,128)(2,1)}, u32[]{:S(2)}) copy-start(bf16[768,1536]{1,0:T(8,128)(2,1)} %refs_15_.1) | copy-start | bytes 7077892
  0.6 37.5 %copy-start = (bf16[1536,768]{1,0:T(8,128)(2,1)S(1)}, bf16[1536,768]{1,0:T(8,128)(2,1)}, u32[]{:S(2)}) copy-start(bf16[1536,768]{1,0:T(8,128)(2,1)} %up.1) | copy-start | bytes 7077892
  0.7 37.4 %collective-permute-start.13 = (bf16[768,1536]{1,0:T(8,128)(2,1)}, bf16[768,1536]{1,0:T(8,128)(2,1)S(1)}, u32[]{:S(2)}, u32[]{:S(2)}) collective-permute-start(bf16[768,1536]{1,0:T(8,128)(2,1)} %refs_15_.1), channel_id=1, source_target_pairs={{0,1},{1,0},{2,3},{3,2},{4,5},{5,4},{6,7},{7,6},{8,9},{9,8},{10,11... | collective-permute-start | bytes 7077896 | tf_op jit(solution)/shard_map/ppermute | solution.py:60
  0.8 37.3 %collective-permute-start.12 = (bf16[1536,768]{1,0:T(8,128)(2,1)}, bf16[1536,768]{1,0:T(8,128)(2,1)S(1)}, u32[]{:S(2)}, u32[]{:S(2)}) collective-permute-start(bf16[1536,768]{1,0:T(8,128)(2,1)} %up.1), channel_id=1, source_target_pairs={{0,1},{1,0},{2,3},{3,2},{4,5},{5,4},{6,7},{7,6},{8,9},{9,8},{10,11... | collective-permute-start | bytes 7077896 | tf_op jit(solution)/shard_map/ppermute | solution.py:60
  2.4 5.0 %collective-permute-start = (bf16[16,3072]{1,0:T(8,128)(2,1)S(1)}, bf16[16,3072]{1,0:T(8,128)(2,1)S(1)}, u32[]{:S(2)}, u32[]{:S(2)}) collective-permute-start(bf16[16,3072]{1,0:T(8,128)(2,1)S(1)} %pack.1.refs_0_), channel_id=1, source_target_pairs={{0,16},{16,0},{1,17},{17,1},{2,18},{18,2},{3,19},{19,3},{4,20},{20... | collective-permute-start | bytes 294920 | tf_op jit(solution)/shard_map/ppermute | solution.py:60
  7.4 11.9 %collective-permute-start.1 = (bf16[32,3072]{1,0:T(8,128)(2,1)S(1)}, bf16[32,3072]{1,0:T(8,128)(2,1)S(1)}, u32[]{:S(2)}, u32[]{:S(2)}) collective-permute-start(bf16[32,3072]{1,0:T(8,128)(2,1)S(1)} %pad_maximum_fusion), channel_id=1, source_target_pairs={{0,2},{2,4},{4,6},{6,8},{8,10},{10,12},{12,14},{14,0},{1,3},{3,5},... | collective-permute-start | bytes 589832 | tf_op jit(solution)/shard_map/ppermute | solution.py:56
  9.4 6.2 %collective-permute-start.4 = (bf16[16,3072]{1,0:T(8,128)(2,1)S(1)}, bf16[16,3072]{1,0:T(8,128)(2,1)S(1)}, u32[]{:S(2)}, u32[]{:S(2)}) collective-permute-start(bf16[16,3072]{1,0:T(8,128)(2,1)S(1)} %pack.1.refs_0_), channel_id=1, source_target_pairs={{0,14},{2,0},{4,2},{6,4},{8,6},{10,8},{12,10},{14,12},{1,15},{3,1}... | collective-permute-start | bytes 294920 | tf_op jit(solution)/shard_map/ppermute | solution.py:56
  15.7 5.8 %collective-permute-start.6 = (bf16[16,3072]{1,0:T(8,128)(2,1)S(1)}, bf16[16,3072]{1,0:T(8,128)(2,1)S(1)}, u32[]{:S(2)}, u32[]{:S(2)}) collective-permute-start(bf16[16,3072]{1,0:T(8,128)(2,1)S(1)} %collective-permute-done.4.refs_5_), channel_id=1, source_target_pairs={{0,14},{2,0},{4,2},{6,4},{8,6},{10,8},{12,10},{14,12},{1,15},{3,1}... | collective-permute-start | bytes 294920 | tf_op jit(solution)/shard_map/ppermute | solution.py:56
  19.3 11.9 %collective-permute-start.2 = (bf16[32,3072]{1,0:T(8,128)(2,1)S(1)}, bf16[32,3072]{1,0:T(8,128)(2,1)S(1)}, u32[]{:S(2)}, u32[]{:S(2)}) collective-permute-start(bf16[32,3072]{1,0:T(8,128)(2,1)S(1)} %collective-permute-done.1.refs_2_), channel_id=1, source_target_pairs={{0,2},{2,4},{4,6},{6,8},{8,10},{10,12},{12,14},{14,0},{1,3},{3,5},... | collective-permute-start | bytes 589832 | tf_op jit(solution)/shard_map/ppermute | solution.py:56
  19.3 5.8 %collective-permute-start.5 = (bf16[16,3072]{1,0:T(8,128)(2,1)S(1)}, bf16[16,3072]{1,0:T(8,128)(2,1)S(1)}, u32[]{:S(2)}, u32[]{:S(2)}) collective-permute-start(bf16[16,3072]{1,0:T(8,128)(2,1)S(1)} %collective-permute-done.4.refs_5_), channel_id=1, source_target_pairs={{0,16},{16,0},{1,17},{17,1},{2,18},{18,2},{3,19},{19,3},{4,20},{20... | collective-permute-start | bytes 294920 | tf_op jit(solution)/shard_map/ppermute | solution.py:60
  21.5 6.0 %collective-permute-start.8 = (bf16[16,3072]{1,0:T(8,128)(2,1)S(1)}, bf16[16,3072]{1,0:T(8,128)(2,1)S(1)}, u32[]{:S(2)}, u32[]{:S(2)}) collective-permute-start(bf16[16,3072]{1,0:T(8,128)(2,1)S(1)} %collective-permute-done.6.refs_7_), channel_id=1, source_target_pairs={{0,14},{2,0},{4,2},{6,4},{8,6},{10,8},{12,10},{14,12},{1,15},{3,1}... | collective-permute-start | bytes 294920 | tf_op jit(solution)/shard_map/ppermute | solution.py:56
  25.1 6.1 %collective-permute-start.7 = (bf16[16,3072]{1,0:T(8,128)(2,1)S(1)}, bf16[16,3072]{1,0:T(8,128)(2,1)S(1)}, u32[]{:S(2)}, u32[]{:S(2)}) collective-permute-start(bf16[16,3072]{1,0:T(8,128)(2,1)S(1)} %collective-permute-done.6.refs_7_), channel_id=1, source_target_pairs={{0,16},{16,0},{1,17},{17,1},{2,18},{18,2},{3,19},{19,3},{4,20},{20... | collective-permute-start | bytes 294920 | tf_op jit(solution)/shard_map/ppermute | solution.py:60
  27.5 5.9 %collective-permute-start.10 = (bf16[16,3072]{1,0:T(8,128)(2,1)S(1)}, bf16[16,3072]{1,0:T(8,128)(2,1)S(1)}, u32[]{:S(2)}, u32[]{:S(2)}) collective-permute-start(bf16[16,3072]{1,0:T(8,128)(2,1)S(1)} %collective-permute-done.8.refs_9_), channel_id=1, source_target_pairs={{0,14},{2,0},{4,2},{6,4},{8,6},{10,8},{12,10},{14,12},{1,15},{3,1}... | collective-permute-start | bytes 294920 | tf_op jit(solution)/shard_map/ppermute | solution.py:56
  31.2 6.9 %collective-permute-start.3 = (bf16[32,3072]{1,0:T(8,128)(2,1)S(1)}, bf16[32,3072]{1,0:T(8,128)(2,1)S(1)}, u32[]{:S(2)}, u32[]{:S(2)}) collective-permute-start(bf16[32,3072]{1,0:T(8,128)(2,1)S(1)} %collective-permute-done.2.refs_3_), channel_id=1, source_target_pairs={{0,2},{2,4},{4,6},{6,8},{8,10},{10,12},{12,14},{14,0},{1,3},{3,5},... | collective-permute-start | bytes 589832 | tf_op jit(solution)/shard_map/ppermute | solution.py:56
  31.2 4.7 %collective-permute-start.9 = (bf16[16,3072]{1,0:T(8,128)(2,1)S(1)}, bf16[16,3072]{1,0:T(8,128)(2,1)S(1)}, u32[]{:S(2)}, u32[]{:S(2)}) collective-permute-start(bf16[16,3072]{1,0:T(8,128)(2,1)S(1)} %collective-permute-done.8.refs_9_), channel_id=1, source_target_pairs={{0,16},{16,0},{1,17},{17,1},{2,18},{18,2},{3,19},{19,3},{4,20},{20... | collective-permute-start | bytes 294920 | tf_op jit(solution)/shard_map/ppermute | solution.py:60
  33.4 4.6 %collective-permute-start.11 = (bf16[16,3072]{1,0:T(8,128)(2,1)S(1)}, bf16[16,3072]{1,0:T(8,128)(2,1)S(1)}, u32[]{:S(2)}, u32[]{:S(2)}) collective-permute-start(bf16[16,3072]{1,0:T(8,128)(2,1)S(1)} %collective-permute-done.10.refs_11_), channel_id=1, source_target_pairs={{0,16},{16,0},{1,17},{17,1},{2,18},{18,2},{3,19},{19,3},{4,20},{20... | collective-permute-start | bytes 294920 | tf_op jit(solution)/shard_map/ppermute | solution.py:60
  38.1 5.8 %copy-start.1 = (bf16[1536,768]{1,0:T(8,128)(2,1)}, bf16[1536,768]{1,0:T(8,128)(2,1)S(1)}, u32[]{:S(2)}) copy-start(bf16[1536,768]{1,0:T(8,128)(2,1)S(1)} %collective-permute-done.12.refs_14_.up_two) | copy-start | bytes 7077892
  44.0 7.4 %copy-start.3 = (bf16[768]{0:T(1024)(128)(2,1)S(1)}, bf16[768]{0:T(1024)(128)(2,1)}, u32[]{:S(2)}) copy-start(bf16[768]{0:T(1024)(128)(2,1)} %param.7) | copy-start | bytes 4612
  44.0 22.0 %all-to-all-start = ((bf16[8,32,3072]{2,1,0:T(8,128)(2,1)}), bf16[8,32,3072]{2,1,0:T(8,128)(2,1)S(1)}, u32[]{:S(2)}, u32[]{:S(2)}) async-start(bf16[8,32,3072]{2,1,0:T(8,128)(2,1)} %bitcast.14), calls=%async_computation | async-start | bytes 3145728 | tf_op jit(solution)/shard_map/all_to_all | solution.py:330
  51.4 1.2 collective-permute-start.14
  67.5 20.9 %all-to-all-start.1 = ((bf16[8,32,3072]{2,1,0:T(8,128)(2,1)}), bf16[8,32,3072]{2,1,0:T(8,128)(2,1)S(1)}, u32[]{:S(2)}, u32[]{:S(2)}) async-start(bf16[8,32,3072]{2,1,0:T(8,128)(2,1)} %bitcast.15), calls=%async_computation.1 | async-start | bytes 3145728 | tf_op jit(solution)/shard_map/all_to_all | solution.py:332
  73.6 27.2 %collective-permute-start.15 = (bf16[256,3072]{1,0:T(8,128)(2,1)S(1)}, bf16[256,3072]{1,0:T(8,128)(2,1)}, u32[]{:S(2)}, u32[]{:S(2)}) collective-permute-start(bf16[256,3072]{1,0:T(8,128)(2,1)S(1)} %get-tuple-element.6.left.right), channel_id=1, source_target_pairs={{0,1},{1,0},{2,3},{3,2},{4,5},{5,4},{6,7},{7,6},{8,9},{9,8},{10,11... | collective-permute-start | bytes 4718600 | tf_op jit(solution)/shard_map/ppermute | solution.py:60
  93.6 22.7 %all-to-all-start.2 = ((bf16[16,16,1536]{2,1,0:T(8,128)(2,1)}), bf16[16,16,1536]{2,1,0:T(8,128)(2,1)}, u32[]{:S(2)}, u32[]{:S(2)}) async-start(bf16[16,16,1536]{2,1,0:T(8,128)(2,1)} %bitcast.13), calls=%async_computation.2 | async-start | bytes 1572864 | tf_op jit(solution)/shard_map/all_to_all | solution.py:335
  100.7 2.4 %collective-permute-start.16 = (bf16[256,1536]{1,0:T(8,128)(2,1)S(1)}, bf16[256,1536]{1,0:T(8,128)(2,1)S(1)}, u32[]{:S(2)}, u32[]{:S(2)}) collective-permute-start(bf16[256,1536]{1,0:T(8,128)(2,1)S(1)} %slice.4), channel_id=1, source_target_pairs={{0,1},{1,0},{2,3},{3,2},{4,5},{5,4},{6,7},{7,6},{8,9},{9,8},{10,11... | collective-permute-start | bytes 2359304 | tf_op jit(solution)/shard_map/ppermute | solution.py:60
